TPU v7x, 512 devices: a whole 4x4x16 slice. The times are simulated.
512 devices in a mesh: ctx: 64 (over y_lo, z, core), mp: 8 (over y_hi, x).
Axes of the slice: x: 4, y: 4 (y_hi: 2, y_lo: 2; y = y_hi * 2 + y_lo), z: 16, core: 2. Of those that a mesh axis runs over, the one named last changes fastest.
Arguments:
- sublayer_input: bfloat16 [8192, 4096], P('ctx'), may hold values from -16 to 16
- rotated_queries: bfloat16 [8192, 8192], P('ctx', 'mp'), may hold values from -5 to 5
- rotated_keys: bfloat16 [8192, 1024], P('ctx', 'mp'), may hold values from -5 to 5
- output_grad: bfloat16 [8192, 8192], P('ctx', 'mp'), may hold values from -6 to 6
- value_weight: bfloat16 [4096, 1024], P(None, 'mp'), may hold values from -0.09375 to 0.09375
- segment_ids: int32 [8192], replicated, may hold values from 0 to 3, never falling along the last dimension, each value on 1 to 6144 neighbouring positions
- label_positions: int32 [128], replicated, may hold values from 0 to 8191
Outputs:
- query_grad: bfloat16 [8192, 8192], P('ctx', 'mp')
- key_grad: bfloat16 [8192, 1024], P('ctx', 'mp')
- input_grad: bfloat16 [8192, 4096], P('ctx', 'mp')
- value_weight_grad: bfloat16 [4096, 1024], P('ctx', 'mp')
Inputs may be any that keep to these rules, and one draw needn't show every extreme that they name: `segment_ids`: ids never fall along the slab; one trace takes exactly 6144 positions. `label_positions`: a position may appear more than once.
All inputs are finite; a program needn't handle non-finite values.
Results may differ from a plain program's by a relative error of at most 0.017.
Values may be sent and summed in bfloat16 or wider, within the bound.
No kernel may reach another device: no remote copies, remote signals or barrier semaphores. Data moves between devices by JAX's collectives and lax.ppermute only.
A program may use at most 64 MiB of HBM per device.

v0:
```python
import jax
import jax.numpy as jnp
from jax import lax
from jax.sharding import PartitionSpec as P

HEADS = 64
KV_HEADS = 8
HD = 128


NEGATIVE = -1e30


def from_partner(value, axis, distance):
    mask = 2**distance
    pairs = [(source, source ^ mask) for source in range(lax.axis_size(axis))]
    return lax.ppermute(value, axis, pairs)


def halve_sum(blocks_view, context_index):
    bit_count = blocks_view.shape[0].bit_length() - 1
    target_index = context_index ^ 1
    current = blocks_view
    for bit_index in reversed(range(bit_count)):
        half_count = current.shape[0] // 2
        lower_half = current[:half_count]
        upper_half = current[half_count:]
        upper_mine = target_index >> bit_index & 1 == 1
        keep_part = jnp.where(upper_mine, upper_half, lower_half)
        send_part = jnp.where(upper_mine, lower_half, upper_half)
        current = keep_part + from_partner(send_part, "ctx", bit_index)
    return from_partner(current[0].astype(jnp.bfloat16), "ctx", 0).astype(jnp.float32)


def on_device(
    sublayer_input,
    rotated_queries,
    rotated_keys,
    output_grad,
    value_weight,
    segment_ids,
    label_positions,
):
    local_rows = sublayer_input.shape[0]
    context_count = lax.axis_size("ctx")
    context_index = lax.axis_index("ctx")
    total_rows = local_rows * context_count
    group_size = HEADS // KV_HEADS
    local_heads = rotated_keys.shape[1] // HD
    score_scale = HD ** (-0.5)
    key_width = 512
    first_row = context_index * local_rows
    own_positions = first_row + jnp.arange(local_rows, dtype=jnp.int32)
    labelled = jnp.any(own_positions[:, None] == label_positions[None, :], axis=1)
    loss_weight = jnp.where(labelled, 4.0, 1.0).astype(jnp.float32)
    weighted = (output_grad.astype(jnp.float32) * loss_weight[:, None]).astype(jnp.bfloat16)
    values = jnp.dot(sublayer_input, value_weight, preferred_element_type=jnp.float32).astype(
        jnp.bfloat16
    )
    all_keys, all_values = (
        lax.all_gather(rotated_keys, "ctx", axis=0, tiled=True),
        lax.all_gather(values, "ctx", axis=0, tiled=True),
    )
    query_four = rotated_queries.reshape(local_rows, local_heads, group_size, HD)
    grad_four = weighted.reshape(local_rows, local_heads, group_size, HD)
    own_segments = lax.dynamic_slice_in_dim(segment_ids, first_row, local_rows)
    every_position = jnp.arange(total_rows, dtype=jnp.int32)
    doc_begin = jnp.min(jnp.where(segment_ids == own_segments[0], every_position, total_rows))
    lower_block = doc_begin // key_width
    upper_block = (first_row + local_rows - 1) // key_width + 1

    def block_terms(block_index):
        block_start = block_index * key_width
        key_part = lax.dynamic_slice_in_dim(all_keys, block_start, key_width, 0).reshape(
            key_width, local_heads, HD
        )
        value_part = lax.dynamic_slice_in_dim(all_values, block_start, key_width, 0).reshape(
            key_width, local_heads, HD
        )
        key_positions = block_start + jnp.arange(key_width, dtype=jnp.int32)
        key_segments = lax.dynamic_slice_in_dim(segment_ids, block_start, key_width)
        allowed = (own_segments[:, None] == key_segments[None, :]) & (
            own_positions[:, None] >= key_positions[None, :]
        )
        allowed = allowed[None, None, :, :]
        scores = (
            jnp.einsum("tcgd,kcd->cgtk", query_four, key_part, preferred_element_type=jnp.float32)
            * score_scale
        )
        grad_probs = jnp.einsum(
            "tcgd,kcd->cgtk", grad_four, value_part, preferred_element_type=jnp.float32
        )
        masked = jnp.where(allowed, scores, NEGATIVE)
        return (block_start, key_part, allowed, masked, grad_probs)

    def first_pass(block_index, carry):
        running_max, running_sum, running_dot = carry
        block_start, key_part, allowed, masked, grad_probs = block_terms(block_index)
        new_max = jnp.maximum(running_max, jnp.max(masked, axis=-1))
        factor = jnp.exp(running_max - new_max)
        weights = jnp.where(allowed, jnp.exp(masked - new_max[..., None]), 0.0)
        new_sum = running_sum * factor + jnp.sum(weights, axis=-1)
        new_dot = running_dot * factor + jnp.sum(weights * grad_probs, axis=-1)
        return (new_max, new_sum, new_dot)

    stat_shape = (local_heads, group_size, local_rows)
    start_stats = (
        jnp.full(stat_shape, NEGATIVE, jnp.float32),
        jnp.zeros(stat_shape, jnp.float32),
        jnp.zeros(stat_shape, jnp.float32),
    )
    running_max, running_sum, running_dot = lax.fori_loop(
        lower_block, upper_block, first_pass, start_stats
    )
    log_total = running_max + jnp.log(running_sum)
    delta = running_dot / running_sum

    def second_pass(block_index, carry):
        query_sum, grad_buffer = carry
        block_start, key_part, allowed, masked, grad_probs = block_terms(block_index)
        probabilities = jnp.where(allowed, jnp.exp(masked - log_total[..., None]), 0.0)
        probs_low = probabilities.astype(jnp.bfloat16)
        grad_scores = (probabilities * (grad_probs - delta[..., None]) * score_scale).astype(
            jnp.bfloat16
        )
        query_sum = query_sum + jnp.einsum(
            "cgtk,kcd->tcgd", grad_scores, key_part, preferred_element_type=jnp.float32
        )
        key_term = jnp.einsum(
            "cgtk,tcgd->kcd", grad_scores, query_four, preferred_element_type=jnp.float32
        )
        value_term = jnp.einsum(
            "cgtk,tcgd->kcd", probs_low, grad_four, preferred_element_type=jnp.float32
        )
        joined = jnp.concatenate(
            [
                key_term.reshape(key_width, local_heads * HD),
                value_term.reshape(key_width, local_heads * HD),
            ],
            axis=1,
        )
        grad_buffer = lax.dynamic_update_slice_in_dim(grad_buffer, joined, block_start, 0)
        return (query_sum, grad_buffer)

    start_query = jnp.zeros((local_rows, local_heads, group_size, HD), jnp.float32)
    start_buffer = jnp.zeros((total_rows, 2 * local_heads * HD), jnp.float32)
    query_sum, grad_buffer = lax.fori_loop(
        lower_block, upper_block, second_pass, (start_query, start_buffer)
    )
    query_grad = query_sum.reshape(local_rows, local_heads * group_size * HD).astype(jnp.bfloat16)
    blocks_view = grad_buffer.reshape(context_count, local_rows, 2 * local_heads * HD)
    summed = halve_sum(blocks_view, context_index)
    key_grad = summed[:, : local_heads * HD].astype(jnp.bfloat16)
    value_grad = summed[:, local_heads * HD :].astype(jnp.bfloat16)
    input_term = lax.dot_general(
        value_grad, value_weight, (((1,), (1,)), ((), ())), preferred_element_type=jnp.float32
    )
    input_grad = lax.psum_scatter(
        input_term.astype(jnp.bfloat16), "mp", scatter_dimension=1, tiled=True
    )
    value_weight_grad = lax.psum_scatter(
        lax.dot_general(
            sublayer_input, value_grad, (((0,), (0,)), ((), ())), preferred_element_type=jnp.float32
        ),
        "ctx",
        scatter_dimension=0,
        tiled=True,
    ).astype(jnp.bfloat16)
    return (query_grad, key_grad, input_grad, value_weight_grad)


def solution(mesh):
    placed = (
        P("ctx", None),
        P("ctx", "mp"),
        P("ctx", "mp"),
        P("ctx", "mp"),
        P(None, "mp"),
        P(),
        P(),
    )
    return jax.shard_map(
        on_device,
        mesh=mesh,
        in_specs=placed,
        out_specs=(P("ctx", "mp"), P("ctx", "mp"), P("ctx", "mp"), P("ctx", "mp")),
        check_vma=False,
    )
```

profile of v0, /device:TPU:24, one launch (start us, length us, event | category | flops | bytes accessed | tf_op | source)
XLA Modules:
  0.0 1116.1 jit_solution(14265563072426648610)
XLA Ops:
  8.4 2.3 convolution_convert_fusion.1
  15.2 121.1 %all-gather.3.cloned.1.call-done = bf16[8192,128]{1,0:T(8,128)(2,1)} async-done(((bf16[128,128]{1,0:T(8,128)(2,1)}), bf16[8192,128]{1,0:T(8,128)(2,1)}) %all-gather.3.cloned.1.call-update) | async-done | bytes 2097168 | tf_op jit(solution)/shard_map/all_gather | solution.py:61
  136.3 121.2 %all-gather.5.cloned.1.call-done = bf16[8192,128]{1,0:T(8,128)(2,1)} async-done(((bf16[128,128]{1,0:T(8,128)(2,1)}), bf16[8192,128]{1,0:T(8,128)(2,1)}) %all-gather.5.cloned.1.call-update) | async-done | bytes 2097168 | tf_op jit(solution)/shard_map/all_gather | solution.py:62
  257.5 35.3 %while.28 = (s32[]{:T(128)}, f32[1,8,128]{2,1,0:T(8,128)S(1)}, f32[1,8,128]{2,1,0:T(8,128)S(1)}, f32[1,8,128]{2,1,0:T(8,128)S(1)}, s32[]{:T(128)}, /*index=5*/s3...) while((s32[]{:T(128)}, f32[1,8,128]{2,1,0:T(8,128)S(1)}, ...), condition=%wide.region_6.7_spmd.clone, body=%wide.region_2.6_spmd.clone.sunk | while | flops 275975808 | bytes 7425759 | solution.py:112
  292.8 4.2 broadcast_in_dim.71
  297.0 56.6 %while.29 = (s32[]{:T(128)}, f32[128,1,8,128]{0,3,2,1:T(8,128)S(1)}, f32[8192,256]{0,1:T(8,128)}, s32[]{:T(128)}, bf16[8192,128]{1,0:T(8,128)(2,1)}, /*index=5*/...) while((s32[]{:T(128)}, ...), condition=%wide.region_8.9_spmd.clone, body=%wide.region_7.8_spmd.clone.sunk | while | flops 676266624 | bytes 13651695 | solution.py:147
  353.5 7.8 slice_select_fusion
  361.4 5.6 copy.51
  368.9 5.6 copy.50
  374.5 87.4 %collective-permute-done = f32[32,128,256]{2,1,0:T(8,128)} collective-permute-done((f32[32,128,256]{2,1,0:T(8,128)}, f32[32,128,256]{2,1,0:T(8,128)}, u32[]{:S(2)}, u32[]{:S(2)}) %collective-permute-start) | collective-permute-done | bytes 4194336 | tf_op jit(solution)/shard_map/ppermute | solution.py:17
  461.9 4.1 add.98
  470.5 173.3 %collective-permute-done.1 = f32[16,128,256]{2,1,0:T(8,128)} collective-permute-done((f32[16,128,256]{2,1,0:T(8,128)}, f32[16,128,256]{2,1,0:T(8,128)}, u32[]{:S(2)}, u32[]{:S(2)}) %collective-permute-start.1) | collective-permute-done | bytes 2097184 | tf_op jit(solution)/shard_map/ppermute | solution.py:17
  643.9 3.3 select_add_fusion
  648.6 1.9 collective-permute-start.2
  650.6 102.1 %collective-permute-done.2 = f32[8,128,256]{2,1,0:T(8,128)} collective-permute-done((f32[8,128,256]{2,1,0:T(8,128)S(1)}, f32[8,128,256]{2,1,0:T(8,128)}, u32[]{:S(2)}, u32[]{:S(2)}) %collective-permute-start.2) | collective-permute-done | bytes 1048608 | tf_op jit(solution)/shard_map/ppermute | solution.py:17
  752.7 2.1 select_add_fusion.1
  754.9 1.9 collective-permute-start.3
  756.8 24.0 %collective-permute-done.3 = f32[4,128,256]{2,1,0:T(8,128)} collective-permute-done((f32[4,128,256]{2,1,0:T(8,128)S(1)}, f32[4,128,256]{2,1,0:T(8,128)}, u32[]{:S(2)}, u32[]{:S(2)}) %collective-permute-start.3) | collective-permute-done | bytes 524320 | tf_op jit(solution)/shard_map/ppermute | solution.py:17
  782.0 1.9 collective-permute-start.4
  783.9 8.2 collective-permute-done.4
  795.5 2.1 collective-permute-start.6
  800.4 2.9 copy.61
  807.5 218.3 %reduce-scatter.7.cloned.1.call-done = f32[64,128]{1,0:T(8,128)} async-done(((f32[4096,128]{1,0:T(8,128)}), f32[64,128]{1,0:T(8,128)}) %reduce-scatter.7.cloned.1.call-update) | async-done | bytes 32784
  1027.3 82.2 %reduce-scatter.5.cloned.1.call-done = bf16[128,512]{1,0:T(8,128)(2,1)} async-done(((bf16[128,4096]{1,0:T(8,128)(2,1)}), bf16[128,512]{1,0:T(8,128)(2,1)}) %reduce-scatter.5.cloned.1.call-update) | async-done | bytes 131088 | tf_op jit(solution)/shard_map/reduce_scatter | solution.py:158
  (239 shorter events, 114.6 us)
Async XLA Ops:
  7.2 1.2 copy-start
  7.2 3.6 copy-start.6
  7.2 6.9 copy-start.5
  7.2 7.3 copy-start.7
  7.2 7.5 copy-start.4
  7.2 129.1 %all-gather.3.cloned.1.call-start = ((), (), s32[]{:S(2)}) async-start(), calls=%async_computation.2 | async-start | bytes 2129920 | tf_op jit(solution)/shard_map/all_gather | solution.py:61
  8.0 249.5 %all-gather.5.cloned.1.call-start = ((), (), s32[]{:S(2)}) async-start(), calls=%async_computation.3 | async-start | bytes 2129920 | tf_op jit(solution)/shard_map/all_gather | solution.py:62
  10.7 1015.1 %reduce-scatter.7.cloned.1.call-start = ((), (), s32[]{:S(2)}) async-start(), calls=%async_computation.5 | async-start | bytes 2129920
  367.0 94.9 %collective-permute-start = (f32[32,128,256]{2,1,0:T(8,128)}, f32[32,128,256]{2,1,0:T(8,128)}, u32[]{:S(2)}, u32[]{:S(2)}) collective-permute-start(f32[32,128,256]{2,1,0:T(8,128)} %bitcast.180), channel_id=1, source_target_pairs={{0,256},{8,264},{16,272},{24,280},{32,288},{40,296},{48,304},{56,3... | collective-permute-start | bytes 12582920 | tf_op jit(solution)/shard_map/ppermute | solution.py:17
  466.0 2.6 copy-start.1
  468.6 175.2 %collective-permute-start.1 = (f32[16,128,256]{2,1,0:T(8,128)}, f32[16,128,256]{2,1,0:T(8,128)}, u32[]{:S(2)}, u32[]{:S(2)}) collective-permute-start(f32[16,128,256]{2,1,0:T(8,128)} %slice_select_fusion.2), channel_id=1, source_target_pairs={{0,128},{8,136},{16,144},{24,152},{32,160},{40,168},{48,176},{56,1... | collective-permute-start | bytes 6291464 | tf_op jit(solution)/shard_map/ppermute | solution.py:17
  647.2 1.3 copy-start.2
  648.6 104.0 %collective-permute-start.2 = (f32[8,128,256]{2,1,0:T(8,128)S(1)}, f32[8,128,256]{2,1,0:T(8,128)}, u32[]{:S(2)}, u32[]{:S(2)}) collective-permute-start(f32[8,128,256]{2,1,0:T(8,128)S(1)} %slice_select_fusion.3), channel_id=1, source_target_pairs={{0,64},{8,72},{16,80},{24,88},{32,96},{40,104},{48,112},{56,120},{... | collective-permute-start | bytes 3145736 | tf_op jit(solution)/shard_map/ppermute | solution.py:17
  754.9 25.9 %collective-permute-start.3 = (f32[4,128,256]{2,1,0:T(8,128)S(1)}, f32[4,128,256]{2,1,0:T(8,128)}, u32[]{:S(2)}, u32[]{:S(2)}) collective-permute-start(f32[4,128,256]{2,1,0:T(8,128)S(1)} %slice_select_fusion.4), channel_id=1, source_target_pairs={{0,32},{8,40},{16,48},{24,56},{32,0},{40,8},{48,16},{56,24},{64,96... | collective-permute-start | bytes 1572872 | tf_op jit(solution)/shard_map/ppermute | solution.py:17
  782.0 10.1 collective-permute-start.4
  792.2 3.2 collective-permute-start.5
  795.5 3.1 collective-permute-start.6
  803.3 1.2 copy-start.3
  803.3 306.2 %reduce-scatter.5.cloned.1.call-start = ((), (), s32[]{:S(2)}) async-start(), calls=%async_computation.4 | async-start | bytes 1179648 | tf_op jit(solution)/shard_map/reduce_scatter | solution.py:158
Sparse Core Ops, SparseCore 0:
  10.2 126.0 all-gather.2
  139.0 118.4 all-gather.4
  803.4 222.2 reduce-scatter.6
  1031.4 78.1 reduce-scatter.4
where the time goes:
time: 1120 us
  waiting for transfers between devices  941 us (84%)
  matrix products  78.4 us (7%)
  other arithmetic  38 us (3%)
  local copies, waits for them, and re-layouts  27.2 us (2%)
  between operations  16.7 us (1%)
  starting transfers between devices  13.7 us (1%)
    ppermute x7, waiting for transfers between devices, from_partner(): return lax.ppermute(value, axis, pairs)  397 us
    unnamed x5, waiting for transfers between devices  219 us
    all_gather x1, waiting for transfers between devices, on_device(): lax.all_gather(values, 'ctx', axis=0, tiled=True)  121 us
    all_gather x1, waiting for transfers between devices, on_device(): lax.all_gather(rotated_keys, 'ctx', axis=0, tiled=True)  121 us
    reduce_scatter x1, waiting for transfers between devices, on_device(): lax.psum_scatter(input_term.astype(jnp.bfloat16), 'mp', scatter_dimension...  82.2 us
    dot_general x18, matrix products, block_terms(): jnp.einsum('tcgd,kcd->cgtk', grad_four, value_part, preferred_element_typ...  26.9 us
    dot_general x18, matrix products, block_terms(): jnp.einsum('tcgd,kcd->cgtk', query_four, key_part, preferred_element_type...  26.2 us
  transfers between devices with their start and end apart: 11, of which 11 were waited for; matrix products, arithmetic and copies ran while one was open for 1% of the time, Pallas kernels for 0%

commit v1 on v0

v1 whole, which is shorter than its diff:
```python
import math

import jax
import jax.numpy as jnp
from jax import lax
from jax.experimental import pallas as pl
from jax.experimental.pallas import tpu as pltpu
from jax.sharding import PartitionSpec as P

HEADS = 64
KV_HEADS = 8
GROUP = HEADS // KV_HEADS
HD = 128
ROWS = 128
SCALE = HD ** (-0.5)
POWER = SCALE * math.log2(math.e)
FLOOR = -1e30
HIDDEN = -1e32
Y, Z, C = 2, 16, 2
TILE = 256
TILES = Z * ROWS // TILE
NT = (((1,), (1,)), ((), ()))
NN = (((1,), (0,)), ((), ()))


def at(y, z, c):
    return (y * Z + z) * C + c


Y_SWAP = [(i, i ^ (Z * C)) for i in range(Y * Z * C)]
C_SWAP = [(i, i ^ 1) for i in range(Y * Z * C)]
QUADS = [[at(y, z, c) for y in range(Y) for c in range(C)] for z in range(Z)]
LINES = [[at(y, z, c) for z in range(Z)] for y in range(Y) for c in range(C)]
CLASSES = [
    sorted(at((z + s) % 2, z, c) for z in range(Z)) for s in range(2) for c in range(C)
]


def dot(a, b, dims):
    return lax.dot_general(a, b, dims, preferred_element_type=jnp.float32)


def tile_first(place, tile):
    half = TILES // 2
    low = place[4] + 8 * tile
    high = place[5] + 8 * (tile - half)
    return jnp.where(tile < half, low, high) * ROWS


def doc_start(place, position):
    begin = jnp.zeros_like(position)
    for k in range(6, 9):
        begin = jnp.where(place[k] <= position, jnp.maximum(begin, place[k]), begin)
    return begin


def tile_state(place, j, tile):
    query_first = place[j] * ROWS
    key_first = tile_first(place, tile)
    key_last = key_first + 5 * ROWS - 1
    active = (key_first < query_first + ROWS) & (
        key_last >= doc_start(place, query_first)
    )
    return query_first, key_first, active


def tile_mask(place, query_first, key_first):
    row = lax.broadcasted_iota(jnp.int32, (TILE, ROWS), 0)
    key_position = key_first + row + jnp.where(row >= ROWS, 3 * ROWS, 0)
    query_position = query_first + lax.broadcasted_iota(jnp.int32, (TILE, ROWS), 1)
    begin = doc_start(place, query_position)
    return (key_position <= query_position) & (key_position >= begin)


def stats_kernel(place, qd, kv, out, top, total, inner):
    def query_block(j, _):
        top[...] = jnp.full(top.shape, FLOOR, jnp.float32)
        total[...] = jnp.zeros(total.shape, jnp.float32)
        inner[...] = jnp.zeros(inner.shape, jnp.float32)

        def key_tile(tile, _):
            query_first, key_first, active = tile_state(place, j, tile)

            @pl.when(active)
            def _():
                mask = tile_mask(place, query_first, key_first)
                rows = pl.ds(pl.multiple_of(tile * TILE, TILE), TILE)
                keys = kv[rows, :HD]
                values = kv[rows, HD:]
                for pair in range(GROUP // 2):
                    span = pl.ds(pair * 2 * ROWS, 2 * ROWS)
                    grad_span = pl.ds((GROUP + pair * 2) * ROWS, 2 * ROWS)
                    scores = dot(keys, qd[j, span, :], NT)
                    grad_probs = dot(values, qd[j, grad_span, :], NT)
                    for i in range(2):
                        head = 2 * pair + i
                        lanes = slice(i * ROWS, (i + 1) * ROWS)
                        s = jnp.where(mask, scores[:, lanes], HIDDEN)
                        s = s.reshape(TILE // 8, 8, ROWS)
                        g = grad_probs[:, lanes].reshape(TILE // 8, 8, ROWS)
                        old = top[head]
                        new = jnp.maximum(old, jnp.max(s, axis=0))
                        factor = jnp.exp2((old - new) * POWER)
                        p = jnp.exp2((s - new[None]) * POWER)
                        total[head] = total[head] * factor + jnp.sum(p, axis=0)
                        inner[head] = inner[head] * factor + jnp.sum(p * g, axis=0)
                        top[head] = new

            return 0

        lax.fori_loop(0, TILES, key_tile, 0)
        tops = top[...]
        best = jnp.max(tops, axis=1)
        weight = jnp.exp2((tops - best[:, None, :]) * POWER)
        out[0, j] = best
        out[1, j] = jnp.sum(total[...] * weight, axis=1)
        out[2, j] = jnp.sum(inner[...] * weight, axis=1)
        return 0

    lax.fori_loop(0, Y * C, query_block, 0)


def grads_kernel(
    place, stats, qd, kv, kt, dq, dkv, log_total, delta, probs, grad_scores, dqt, dkv_sum
):
    mine_y, mine_c = place[9], place[10]
    for j in range(Y * C):
        parts = []
        for r in range(Y * C):
            slot = 2 * (mine_y ^ (r & 1)) + (mine_c ^ (r >> 1))
            parts.append([stats[slot, k, j ^ r] for k in range(3)])
        best = parts[0][0]
        for part in parts[1:]:
            best = jnp.maximum(best, part[0])
        total = jnp.zeros_like(best)
        inner = jnp.zeros_like(best)
        for part in parts:
            weight = jnp.exp2((part[0] - best) * POWER)
            total += part[1] * weight
            inner += part[2] * weight
        log_total[j] = best * POWER + jnp.log(total) * math.log2(math.e)
        delta[j] = inner / total
    dkv_sum[...] = jnp.zeros(dkv_sum.shape, jnp.float32)

    def query_block(j, _):
        dqt[...] = jnp.zeros(dqt.shape, jnp.float32)

        def key_tile(tile, _):
            query_first, key_first, active = tile_state(place, j, tile)

            @pl.when(active)
            def _():
                mask = tile_mask(place, query_first, key_first)
                rows = pl.ds(pl.multiple_of(tile * TILE, TILE), TILE)
                keys = kv[rows, :HD]
                values = kv[rows, HD:]
                for pair in range(GROUP // 2):
                    span = pl.ds(pair * 2 * ROWS, 2 * ROWS)
                    grad_span = pl.ds((GROUP + pair * 2) * ROWS, 2 * ROWS)
                    scores = dot(keys, qd[j, span, :], NT)
                    grads = dot(values, qd[j, grad_span, :], NT)
                    for i in range(2):
                        head = 2 * pair + i
                        lanes = slice(i * ROWS, (i + 1) * ROWS)
                        whole = slice(head * ROWS, (head + 1) * ROWS)
                        x = scores[:, lanes] * POWER - log_total[j, pl.ds(head, 1), :]
                        p = jnp.exp2(jnp.where(mask, x, FLOOR))
                        probs[:, whole] = p.astype(jnp.bfloat16)
                        d = p * (grads[:, lanes] - delta[j, pl.ds(head, 1), :])
                        grad_scores[:, whole] = d.astype(jnp.bfloat16)
                weights = grad_scores[...]
                dqt[...] += dot(kt[:, rows], weights, NN)
                dkv_sum[rows, :HD] += dot(weights, qd[j, pl.ds(0, GROUP * ROWS), :], NN)
                dkv_sum[rows, HD:] += dot(
                    probs[...], qd[j, pl.ds(GROUP * ROWS, GROUP * ROWS), :], NN
                )

            return 0

        lax.fori_loop(0, TILES, key_tile, 0)
        for head in range(GROUP):
            lanes = slice(head * ROWS, (head + 1) * ROWS)
            dq[j, :, lanes] = (dqt[:, lanes].T * SCALE).astype(jnp.bfloat16)
        return 0

    lax.fori_loop(0, Y * C, query_block, 0)
    dkv[:, :HD] = (dkv_sum[:, :HD] * SCALE).astype(jnp.bfloat16)
    dkv[:, HD:] = dkv_sum[:, HD:].astype(jnp.bfloat16)


def on_device(
    sublayer_input,
    rotated_queries,
    rotated_keys,
    output_grad,
    value_weight,
    segment_ids,
    label_positions,
):
    bf16, f32 = jnp.bfloat16, jnp.float32
    context = lax.axis_index("ctx")
    mine_y, mine_z, mine_c = context // (Z * C), context // C % Z, context % C
    side = (mine_y + mine_z) % 2
    own_positions = context * ROWS + jnp.arange(ROWS, dtype=jnp.int32)
    labelled = jnp.any(own_positions[:, None] == label_positions[None, :], axis=1)
    loss_weight = jnp.where(labelled, 4.0, 1.0).astype(f32)
    weighted = (output_grad.astype(f32) * loss_weight[:, None]).astype(bf16)
    starts = [jnp.sum((segment_ids < k).astype(jnp.int32)) for k in range(1, 4)]
    place = jnp.stack(
        [
            at(mine_y ^ (j & 1), mine_z, mine_c ^ (j >> 1)).astype(jnp.int32)
            for j in range(Y * C)
        ]
        + [2 * side + mine_c, 2 * Z + 2 * (1 - side) + mine_c]
        + starts
        + [mine_y, mine_c]
    ).astype(jnp.int32)

    def by_head(x):
        return x.reshape(ROWS, GROUP, HD).transpose(1, 0, 2).reshape(GROUP * ROWS, HD)

    own = jnp.concatenate([by_head(rotated_queries), by_head(weighted)], axis=0)
    across = lax.ppermute(own, "ctx", Y_SWAP)
    values = jnp.dot(sublayer_input, value_weight, preferred_element_type=f32).astype(bf16)
    own_kv = jnp.concatenate([rotated_keys, values], axis=1)
    kv = lax.all_to_all(
        jnp.broadcast_to(own_kv[None], (Z,) + own_kv.shape),
        "ctx",
        0,
        0,
        axis_index_groups=CLASSES,
    ).reshape(Z * ROWS, 2 * HD)
    beside = lax.ppermute(jnp.stack([own, across]), "ctx", C_SWAP)
    qd = jnp.concatenate([own[None], across[None], beside], axis=0)

    smem = pl.BlockSpec(memory_space=pltpu.SMEM)
    vmem = pl.BlockSpec(memory_space=pltpu.VMEM)
    params = pltpu.CompilerParams(vmem_limit_bytes=48 * 1024 * 1024)
    stat = pltpu.VMEM((GROUP, 8, ROWS), f32)
    stats = pl.pallas_call(
        stats_kernel,
        out_shape=jax.ShapeDtypeStruct((3, Y * C, GROUP, ROWS), f32),
        in_specs=[smem, vmem, vmem],
        out_specs=vmem,
        scratch_shapes=[stat, stat, stat],
        compiler_params=params,
    )(place, qd, kv)
    all_stats = lax.all_gather(stats, "ctx", axis_index_groups=QUADS)
    kt = kv[:, :HD].T
    dq, dkv = pl.pallas_call(
        grads_kernel,
        out_shape=(
            jax.ShapeDtypeStruct((Y * C, ROWS, GROUP * HD), bf16),
            jax.ShapeDtypeStruct((Z * ROWS, 2 * HD), bf16),
        ),
        in_specs=[smem, vmem, vmem, vmem, vmem],
        out_specs=(vmem, vmem),
        scratch_shapes=[
            pltpu.VMEM((Y * C, GROUP, ROWS), f32),
            pltpu.VMEM((Y * C, GROUP, ROWS), f32),
            pltpu.VMEM((TILE, GROUP * ROWS), bf16),
            pltpu.VMEM((TILE, GROUP * ROWS), bf16),
            pltpu.VMEM((HD, GROUP * ROWS), f32),
            pltpu.VMEM((Z * ROWS, 2 * HD), f32),
        ],
        compiler_params=params,
    )(place, all_stats, qd, kv, kt)

    from_core = lax.ppermute(dq[2:], "ctx", C_SWAP).astype(f32)
    for_across = (dq[1].astype(f32) + from_core[1]).astype(bf16)
    from_across = lax.ppermute(for_across, "ctx", Y_SWAP).astype(f32)
    query_grad = (dq[0].astype(f32) + from_core[0] + from_across).astype(bf16)

    parts = lax.all_to_all(
        dkv.reshape(Z, ROWS, 2 * HD), "ctx", 0, 0, axis_index_groups=CLASSES
    )
    summed = jnp.sum(parts.astype(f32), axis=0).astype(bf16)
    key_grad = summed[:, :HD]
    value_grad = summed[:, HD:]

    mp_count = lax.axis_size("mp")
    width = value_weight.shape[0] // mp_count
    input_terms = jnp.einsum(
        "td,med->mte",
        value_grad,
        value_weight.reshape(mp_count, width, HD),
        preferred_element_type=f32,
    ).astype(bf16)
    input_parts = lax.all_to_all(input_terms, "mp", 0, 0)
    input_grad = jnp.sum(input_parts.astype(f32), axis=0).astype(bf16)

    term = lax.dot_general(
        sublayer_input, value_grad, (((0,), (0,)), ((), ())), preferred_element_type=f32
    ).astype(bf16)
    piece = term.shape[0] // (Y * Z * C)
    term = term.reshape(Y * Z, C, piece, HD)
    near = lax.ppermute(jnp.where(mine_c == 0, term[:, 1], term[:, 0]), "ctx", C_SWAP)
    term = jnp.where(mine_c == 0, term[:, 0], term[:, 1]).astype(f32) + near.astype(f32)
    term = term.astype(bf16).reshape(Y, Z, piece, HD)
    far = lax.ppermute(jnp.where(mine_y == 0, term[1], term[0]), "ctx", Y_SWAP)
    term = jnp.where(mine_y == 0, term[0], term[1]).astype(f32) + far.astype(f32)
    pieces = lax.all_to_all(term.astype(bf16), "ctx", 0, 0, axis_index_groups=LINES)
    value_weight_grad = jnp.sum(pieces.astype(f32), axis=0).astype(bf16)
    return (query_grad, key_grad, input_grad, value_weight_grad)


def solution(mesh):
    placed = (
        P("ctx", None),
        P("ctx", "mp"),
        P("ctx", "mp"),
        P("ctx", "mp"),
        P(None, "mp"),
        P(),
        P(),
    )
    return jax.shard_map(
        on_device,
        mesh=mesh,
        in_specs=placed,
        out_specs=(P("ctx", "mp"), P("ctx", "mp"), P("ctx", "mp"), P("ctx", "mp")),
        check_vma=False,
    )
```

time: 1120 us -> 238 us (0.21)
  waiting for transfers between devices: 941 us -> 107 us
  matrix products: 78.4 us -> 4.65 us
  starting transfers between devices: 13.7 us -> 73.2 us
  other arithmetic: 38 us -> 9.79 us
  Pallas kernels: 0 us -> 18.9 us
  between operations: 16.7 us -> 1.04 us
    ppermute x7 -> x6, waiting for transfers between devices: 397 us -> 35.8 us  [the longest x1 17.3 us: on_device(): across = lax.ppermute(own, 'ctx', Y_SWAP)]
    all_gather x2 -> x0, waiting for transfers between devices: 242 us -> none  [the longest x1 121 us: on_device(): lax.all_gather(values, 'ctx', axis=0, tiled=True)]
    unnamed x5 -> x0, waiting for transfers between devices: 219 us -> none
    reduce_scatter x1 -> x0, waiting for transfers between devices: 82.2 us -> none  [on_device(): lax.psum_scatter(input_term.astype(jnp.bfloat16), 'mp', scatter_dimension...]
    dot_general x65 -> x2, matrix products: 76.6 us -> 3.17 us  [the longest x1 1.74 us: on_device(): jnp.dot(sublayer_input, value_weight, preferred_element_type=f32)]
    all_to_all x0 -> x4, waiting for transfers between devices: none -> 71.1 us  [the longest x1 43.4 us: on_device(): lax.all_to_all(dkv.reshape(Z, ROWS, 2 * HD), 'ctx', 0, 0, axis_index_grou...]
    all_to_all x0 -> x4, starting transfers between devices: none -> 60.2 us  [the longest x1 24.6 us: on_device(): lax.all_to_all(dkv.reshape(Z, ROWS, 2 * HD), 'ctx', 0, 0, axis_index_grou...]
    pallas_call x0 -> x2, Pallas kernels: none -> 18.9 us  [the longest x1 12.3 us: on_device(): pl.pallas_call(grads_kernel, out_shape=(jax.ShapeDtypeStruct((Y * C, ROWS...]
  transfers between devices with their start and end apart: 11 -> 10, of which waited for: 11 -> 6; matrix products, arithmetic and copies ran while one was open for 1% -> 5% of each run, Pallas kernels for 0% -> 0%
where the time goes in v1:
time: 238 us; the launch traced here: 236 us
  waiting for transfers between devices  107 us (45%)
  starting transfers between devices  73.2 us (31%)
  Pallas kernels  18.9 us (8%)
  local copies, waits for them, and re-layouts  16.1 us (7%)
  other arithmetic  9.79 us (4%)
  blocking collectives  5.61 us (2%)
  matrix products  4.65 us (2%)
    all_to_all x1, waiting for transfers between devices, on_device(): lax.all_to_all(dkv.reshape(Z, ROWS, 2 * HD), 'ctx', 0, 0, axis_index_grou...  43.4 us
    all_to_all x1, starting transfers between devices, on_device(): lax.all_to_all(dkv.reshape(Z, ROWS, 2 * HD), 'ctx', 0, 0, axis_index_grou...  24.6 us
    all_to_all x1, waiting for transfers between devices, on_device(): lax.all_to_all(jnp.broadcast_to(own_kv[None], (Z,) + own_kv.shape), 'ctx'...  22.5 us
    ppermute x1, waiting for transfers between devices, on_device(): across = lax.ppermute(own, 'ctx', Y_SWAP)  17.3 us
    all_to_all x1, starting transfers between devices, on_device(): lax.all_to_all(jnp.broadcast_to(own_kv[None], (Z,) + own_kv.shape), 'ctx'...  16.6 us
    ppermute x1, waiting for transfers between devices, on_device(): far = lax.ppermute(jnp.where(mine_y == 0, term[1], term[0]), 'ctx', Y_SWAP)  12.4 us
    pallas_call x1, Pallas kernels, on_device(): pl.pallas_call(grads_kernel, out_shape=(jax.ShapeDtypeStruct((Y * C, ROWS...  12.3 us
    all_to_all x1, starting transfers between devices, on_device(): lax.all_to_all(term.astype(bf16), 'ctx', 0, 0, axis_index_groups=LINES)  11.6 us
  transfers between devices with their start and end apart: 10, of which 6 were waited for; matrix products, arithmetic and copies ran while one was open for 5% of the time, Pallas kernels for 0%

profile of v1, /device:TPU:24, one launch (start us, length us, event | category | flops | bytes accessed | tf_op | source)
XLA Modules:
  0.0 236.2 jit_solution(13762851908311530579)
XLA Ops:
  1.9 1.7 convolution_convert_fusion.2
  4.9 16.6 %all-to-all-start = ((bf16[16,128,256]{1,2,0:T(8,128)(2,1)}), bf16[16,128,256]{1,2,0:T(8,128)(2,1)}, u32[]{:S(2)}, u32[]{:S(2)}) async-start(bf16[16,128,256]{1,2,0:T(8,128)(2,1)} %broadcast_in_dim.27), calls=%async_computation | async-start | bytes 2097152 | tf_op jit(solution)/shard_map/all_to_all | solution.py:226
  22.0 1.9 collective-permute-start
  23.9 17.3 %collective-permute-done = bf16[2048,128]{1,0:T(8,128)(2,1)S(1)} collective-permute-done((bf16[2048,128]{1,0:T(8,128)(2,1)S(1)}, bf16[2048,128]{1,0:T(8,128)(2,1)S(1)}, u32[]{:S(2)}, u32[]{:S(2)}) %collective-permute-start) | collective-permute-done | bytes 524320 | tf_op jit(solution)/shard_map/ppermute | solution.py:223
  42.0 1.9 collective-permute-start.1
  44.8 1.9 stack.52.place
  46.7 1.7 pad_maximum_fusion.qd
  48.4 22.5 %all-to-all-done = bf16[16,128,256]{1,2,0:T(8,128)(2,1)} async-done(((bf16[16,128,256]{1,2,0:T(8,128)(2,1)}), bf16[16,128,256]{1,2,0:T(8,128)(2,1)}, u32[]{:S(2)}, u32[]{:S(2)}) %all-to-all-start) | async-done | bytes 1048608 | tf_op jit(solution)/shard_map/all_to_all | solution.py:226
  74.2 2.3 copy.37.kv
  77.7 6.6 %shard_map.102 = f32[3,4,8,128]{3,2,1,0:T(8,128)S(1)} custom-call(s32[11]{0:T(128)S(1)} %stack.52.place, bf16[4,2048,128]{2,1,0:T(8,128)(2,1)S(1)} %pad_maximum_fusion.qd, bf16[2048,256]{1,0:T(8,128)(2,1)S(1)} %copy-done.1), custom_call_target="tpu_custom_call" | custom-call | tf_op jit(solution)/shard_map/pallas_call | solution.py:240
  84.3 5.6 %all-gather = f32[12,4,8,128]{3,2,1,0:T(8,128)S(1)} all-gather(f32[3,4,8,128]{3,2,1,0:T(8,128)S(1)} %shard_map.102), channel_id=2, replica_groups={{0,8,256,264},{16,24,272,280},{32,40,288,296},{48,56,304,312},{64,72,32..., dimensions={0}, use_global_device_ids=true | all-gather | bytes 245760 | tf_op jit(solution)/shard_map/all_gather | solution.py:248
  89.9 12.3 %shard_map.103 = (bf16[4,128,1024]{2,1,0:T(8,128)(2,1)S(1)}, bf16[2048,256]{1,0:T(8,128)(2,1)S(1)}) custom-call(s32[11]{0:T(128)S(1)} %stack.52.place, f32[4,3,4,8,128]{4,3,2,1,0:T(8,128)S(1)} %bitcast.67, bf16[4,2048,128]{2,1,0:T(8,128)(2,1)S(1)} %pad_maximum_fusion.qd, bf16[2048,256]{1,0:T(8,128)(2,1)S(1)} %copy-done.1, bf16[128,2048]{1,0:T(8,128)(2,1)S(1)} %copy-done.2), custom_call_target="tpu_custom_call" | custom-call | tf_op jit(solution)/shard_map/pallas_call | solution.py:250
  104.2 24.6 %all-to-all-start.1 = ((bf16[16,128,256]{2,1,0:T(8,128)(2,1)}), bf16[16,128,256]{2,1,0:T(8,128)(2,1)S(1)}, u32[]{:S(2)}, u32[]{:S(2)}) async-start(bf16[16,128,256]{2,1,0:T(8,128)(2,1)} %bitcast.66), calls=%async_computation.1 | async-start | bytes 2097152 | tf_op jit(solution)/shard_map/all_to_all | solution.py:274
  128.8 43.4 %all-to-all-done.1 = bf16[16,128,256]{2,1,0:T(8,128)(2,1)S(1)} async-done(((bf16[16,128,256]{2,1,0:T(8,128)(2,1)}), bf16[16,128,256]{2,1,0:T(8,128)(2,1)S(1)}, u32[]{:S(2)}, u32[]{:S(2)}) %all-to-all-start.1) | async-done | bytes 1048608 | tf_op jit(solution)/shard_map/all_to_all | solution.py:274
  176.4 1.9 collective-permute-start.4
  179.8 7.4 %all-to-all-start.2 = ((bf16[8,128,512]{2,1,0:T(8,128)(2,1)}), bf16[8,128,512]{2,1,0:T(8,128)(2,1)}, u32[]{:S(2)}, u32[]{:S(2)}) async-start(bf16[8,128,512]{2,1,0:T(8,128)(2,1)} %fusion.1), calls=%async_computation.2 | async-start | bytes 2097152 | tf_op jit(solution)/shard_map/all_to_all | solution.py:289
  188.5 1.9 collective-permute-start.5
  190.5 1.9 collective-permute-start.2
  192.4 12.4 %collective-permute-done.5 = bf16[16,64,128]{2,1,0:T(8,128)(2,1)S(1)} collective-permute-done((bf16[16,64,128]{2,1,0:T(8,128)(2,1)S(1)}, bf16[16,64,128]{2,1,0:T(8,128)(2,1)S(1)}, u32[]{:S(2)}, u32[]{:S(2)}) %collective-permute-start.5) | collective-permute-done | bytes 262176 | tf_op jit(solution)/shard_map/ppermute | solution.py:300
  205.6 11.6 %all-to-all-start.3 = ((bf16[16,64,128]{2,1,0:T(8,128)(2,1)}), bf16[16,64,128]{2,1,0:T(8,128)(2,1)S(1)}, u32[]{:S(2)}, u32[]{:S(2)}) async-start(bf16[16,64,128]{2,1,0:T(8,128)(2,1)} %add_convert_fusion), calls=%async_computation.3 | async-start | bytes 524288 | tf_op jit(solution)/shard_map/all_to_all | solution.py:302
  217.3 3.5 %collective-permute-start.3 = (bf16[128,1024]{1,0:T(8,128)(2,1)S(1)}, bf16[128,1024]{1,0:T(8,128)(2,1)S(1)}, u32[]{:S(2)}, u32[]{:S(2)}) collective-permute-start(bf16[128,1024]{1,0:T(8,128)(2,1)S(1)} %fusion.8), channel_id=1, source_target_pairs={{0,256},{8,264},{16,272},{24,280},{32,288},{40,296},{48,304},{56,3... | collective-permute-start | bytes 786440 | tf_op jit(solution)/shard_map/ppermute | solution.py:271
  220.8 6.1 %collective-permute-done.3 = bf16[128,1024]{1,0:T(8,128)(2,1)S(1)} collective-permute-done((bf16[128,1024]{1,0:T(8,128)(2,1)S(1)}, bf16[128,1024]{1,0:T(8,128)(2,1)S(1)}, u32[]{:S(2)}, u32[]{:S(2)}) %collective-permute-start.3) | collective-permute-done | bytes 262176 | tf_op jit(solution)/shard_map/ppermute | solution.py:271
  228.4 2.1 reduce_sum.67
  230.4 5.1 %all-to-all-done.3 = bf16[16,64,128]{2,1,0:T(8,128)(2,1)S(1)} async-done(((bf16[16,64,128]{2,1,0:T(8,128)(2,1)}), bf16[16,64,128]{2,1,0:T(8,128)(2,1)S(1)}, u32[]{:S(2)}, u32[]{:S(2)}) %all-to-all-start.3) | async-done | bytes 262176 | tf_op jit(solution)/shard_map/all_to_all | solution.py:302
  (59 shorter events, 20.9 us)
Async XLA Ops:
  0.6 1.2 copy-start
  3.6 17.9 %copy-start.13 = (s32[128]{0:T(128)S(1)}, s32[128]{0:T(128)}, u32[]{:S(2)}) copy-start(s32[128]{0:T(128)} %param.13) | copy-start | bytes 1540
  3.6 18.0 %copy-start.11 = (bf16[128,1024]{1,0:T(8,128)(2,1)S(1)}, bf16[128,1024]{1,0:T(8,128)(2,1)}, u32[]{:S(2)}) copy-start(bf16[128,1024]{1,0:T(8,128)(2,1)} %param.8) | copy-start | bytes 786436
  3.7 18.1 %copy-start.10 = (bf16[128,1024]{1,0:T(8,128)(2,1)S(1)}, bf16[128,1024]{1,0:T(8,128)(2,1)}, u32[]{:S(2)}) copy-start(bf16[128,1024]{1,0:T(8,128)(2,1)} %param.10) | copy-start | bytes 786436
  4.9 66.1 %all-to-all-start = ((bf16[16,128,256]{1,2,0:T(8,128)(2,1)}), bf16[16,128,256]{1,2,0:T(8,128)(2,1)}, u32[]{:S(2)}, u32[]{:S(2)}) async-start(bf16[16,128,256]{1,2,0:T(8,128)(2,1)} %broadcast_in_dim.27), calls=%async_computation | async-start | bytes 2097152 | tf_op jit(solution)/shard_map/all_to_all | solution.py:226
  21.8 22.3 %copy-start.12 = (s32[8192]{0:T(1024)S(1)}, s32[8192]{0:T(1024)}, u32[]{:S(2)}) copy-start(s32[8192]{0:T(1024)} %param.12) | copy-start | bytes 98308
  22.0 19.3 %copy-start.7 = (bf16[1,2048,128]{2,1,0:T(8,128)(2,1)}, bf16[1,2048,128]{2,1,0:T(8,128)(2,1)S(1)}, u32[]{:S(2)}) copy-start(bf16[1,2048,128]{2,1,0:T(8,128)(2,1)S(1)} %get-tuple-element.11) | copy-start | bytes 1572868
  22.0 19.2 %collective-permute-start = (bf16[2048,128]{1,0:T(8,128)(2,1)S(1)}, bf16[2048,128]{1,0:T(8,128)(2,1)S(1)}, u32[]{:S(2)}, u32[]{:S(2)}) collective-permute-start(bf16[2048,128]{1,0:T(8,128)(2,1)S(1)} %get-tuple-element.12), channel_id=1, source_target_pairs={{0,256},{8,264},{16,272},{24,280},{32,288},{40,296},{48,304},{56,3... | collective-permute-start | bytes 1572872 | tf_op jit(solution)/shard_map/ppermute | solution.py:223
  41.2 0.8 copy-start.9
  42.0 4.7 %collective-permute-start.1 = (bf16[2,2048,128]{2,1,0:T(8,128)(2,1)S(1)}, bf16[2,2048,128]{2,1,0:T(8,128)(2,1)}, u32[]{:S(2)}, u32[]{:S(2)}) collective-permute-start(bf16[2,2048,128]{2,1,0:T(8,128)(2,1)S(1)} %pad_maximum_fusion.1), channel_id=1, source_target_pairs={{0,8},{8,0},{16,24},{24,16},{32,40},{40,32},{48,56},{56,48},{64,72... | collective-permute-start | bytes 3145736 | tf_op jit(solution)/shard_map/ppermute | solution.py:233
  72.4 1.0 copy-start.6
  76.4 1.2 copy-start.1
  77.7 12.2 %copy-start.2 = (bf16[128,2048]{1,0:T(8,128)(2,1)S(1)}, bf16[128,2048]{1,0:T(8,128)(2,1)}, u32[]{:S(2)}) copy-start(bf16[128,2048]{1,0:T(8,128)(2,1)} %slice_bitcast_fusion.kt) | copy-start | bytes 1572868
  102.2 1.0 copy-start.3
  103.2 1.0 copy-start.5
  104.2 68.2 %copy-start.8 = (bf16[128,4096]{1,0:T(8,128)(2,1)S(1)}, bf16[128,4096]{1,0:T(8,128)(2,1)}, u32[]{:S(2)}) copy-start(bf16[128,4096]{1,0:T(8,128)(2,1)} %param.7) | copy-start | bytes 3145732
  104.2 68.1 %all-to-all-start.1 = ((bf16[16,128,256]{2,1,0:T(8,128)(2,1)}), bf16[16,128,256]{2,1,0:T(8,128)(2,1)S(1)}, u32[]{:S(2)}, u32[]{:S(2)}) async-start(bf16[16,128,256]{2,1,0:T(8,128)(2,1)} %bitcast.66), calls=%async_computation.1 | async-start | bytes 2097152 | tf_op jit(solution)/shard_map/all_to_all | solution.py:274
  176.4 10.7 %collective-permute-start.4 = (bf16[32,64,128]{2,1,0:T(8,128)(2,1)}, bf16[32,64,128]{2,1,0:T(8,128)(2,1)}, u32[]{:S(2)}, u32[]{:S(2)}) collective-permute-start(bf16[32,64,128]{2,1,0:T(8,128)(2,1)} %select_bitcast_fusion), channel_id=1, source_target_pairs={{0,8},{8,0},{16,24},{24,16},{32,40},{40,32},{48,56},{56,48},{64,72... | collective-permute-start | bytes 1572872 | tf_op jit(solution)/shard_map/ppermute | solution.py:297
  179.8 10.7 %copy-start.4 = (bf16[4,128,1024]{2,1,0:T(8,128)(2,1)S(1)}, bf16[4,128,1024]{2,1,0:T(8,128)(2,1)}, u32[]{:S(2)}) copy-start(bf16[4,128,1024]{2,1,0:T(8,128)(2,1)} %copy-done.3) | copy-start | bytes 3145732
  179.8 25.8 %all-to-all-start.2 = ((bf16[8,128,512]{2,1,0:T(8,128)(2,1)}), bf16[8,128,512]{2,1,0:T(8,128)(2,1)}, u32[]{:S(2)}, u32[]{:S(2)}) async-start(bf16[8,128,512]{2,1,0:T(8,128)(2,1)} %fusion.1), calls=%async_computation.2 | async-start | bytes 2097152 | tf_op jit(solution)/shard_map/all_to_all | solution.py:289
  188.5 16.3 %collective-permute-start.5 = (bf16[16,64,128]{2,1,0:T(8,128)(2,1)S(1)}, bf16[16,64,128]{2,1,0:T(8,128)(2,1)S(1)}, u32[]{:S(2)}, u32[]{:S(2)}) collective-permute-start(bf16[16,64,128]{2,1,0:T(8,128)(2,1)S(1)} %broadcast_select_fusion), channel_id=1, source_target_pairs={{0,256},{8,264},{16,272},{24,280},{32,288},{40,296},{48,304},{56,3... | collective-permute-start | bytes 786440 | tf_op jit(solution)/shard_map/ppermute | solution.py:300
  190.5 26.7 %collective-permute-start.2 = (bf16[2,128,1024]{2,1,0:T(8,128)(2,1)S(1)}, bf16[2,128,1024]{2,1,0:T(8,128)(2,1)S(1)}, u32[]{:S(2)}, u32[]{:S(2)}) collective-permute-start(bf16[2,128,1024]{2,1,0:T(8,128)(2,1)S(1)} %slice.44), channel_id=1, source_target_pairs={{0,8},{8,0},{16,24},{24,16},{32,40},{40,32},{48,56},{56,48},{64,72... | collective-permute-start | bytes 1572872 | tf_op jit(solution)/shard_map/ppermute | solution.py:269
  205.6 30.0 %all-to-all-start.3 = ((bf16[16,64,128]{2,1,0:T(8,128)(2,1)}), bf16[16,64,128]{2,1,0:T(8,128)(2,1)S(1)}, u32[]{:S(2)}, u32[]{:S(2)}) async-start(bf16[16,64,128]{2,1,0:T(8,128)(2,1)} %add_convert_fusion), calls=%async_computation.3 | async-start | bytes 524288 | tf_op jit(solution)/shard_map/all_to_all | solution.py:302
  217.3 9.6 %collective-permute-start.3 = (bf16[128,1024]{1,0:T(8,128)(2,1)S(1)}, bf16[128,1024]{1,0:T(8,128)(2,1)S(1)}, u32[]{:S(2)}, u32[]{:S(2)}) collective-permute-start(bf16[128,1024]{1,0:T(8,128)(2,1)S(1)} %fusion.8), channel_id=1, source_target_pairs={{0,256},{8,264},{16,272},{24,280},{32,288},{40,296},{48,304},{56,3... | collective-permute-start | bytes 786440 | tf_op jit(solution)/shard_map/ppermute | solution.py:271

commit v2 on v1

--- a/solution.py
+++ b/solution.py
@@ -21,6 +21,7 @@
 TILES = Z * ROWS // TILE
 NT = (((1,), (1,)), ((), ()))
 NN = (((1,), (0,)), ((), ()))
+TN = (((0,), (0,)), ((), ()))
 
 
 def at(y, z, c):
@@ -31,9 +32,25 @@
 C_SWAP = [(i, i ^ 1) for i in range(Y * Z * C)]
 QUADS = [[at(y, z, c) for y in range(Y) for c in range(C)] for z in range(Z)]
 LINES = [[at(y, z, c) for z in range(Z)] for y in range(Y) for c in range(C)]
-CLASSES = [
-    sorted(at((z + s) % 2, z, c) for z in range(Z)) for s in range(2) for c in range(C)
+COLUMNS = [
+    [at(y, z + 4 * k, c) for k in range(Z // 4)]
+    for y in range(Y)
+    for z in range(4)
+    for c in range(C)
 ]
+BASES = [0, 8, 12, 4]
+GROUPS = (4, 4, 4, 2, 2)
+PARTS = Y * C + len(GROUPS)
+
+
+def along_z(value, distance):
+    pairs = [
+        (at(y, z, c), at((y + distance) % 2, (z + distance) % Z, c))
+        for y in range(Y)
+        for z in range(Z)
+        for c in range(C)
+    ]
+    return lax.ppermute(value, "ctx", pairs)
 
 
 def dot(a, b, dims):
@@ -45,6 +62,28 @@
     low = place[4] + 8 * tile
     high = place[5] + 8 * (tile - half)
     return jnp.where(tile < half, low, high) * ROWS
+
+
+def tile_slots(place, tile):
+    half = TILES // 2
+    residue = jnp.where(tile < half, place[11], 1 - place[11]) - place[12] + Z
+    within = lax.rem(tile, half)
+    return place[13 + lax.rem(residue, 4)] + within, place[13 + lax.rem(residue + 2, 4)] + within
+
+
+def slot_rows(slot):
+    return pl.ds(pl.multiple_of(slot * ROWS, ROWS), ROWS)
+
+
+def gather_parts(refs, qd, kv):
+    for j in range(Y * C):
+        qd[j] = refs[j][...]
+    first = 0
+    for part in refs[Y * C :]:
+        count = part.shape[0]
+        for i in range(count):
+            kv[(first + i) * ROWS : (first + i + 1) * ROWS, :] = part[i]
+        first += count
 
 
 def doc_start(place, position):
@@ -72,7 +111,10 @@
     return (key_position <= query_position) & (key_position >= begin)
 
 
-def stats_kernel(place, qd, kv, out, top, total, inner):
+def stats_kernel(place, *refs):
+    out, qd, kv, top, total, inner = refs[PARTS:]
+    gather_parts(refs[:PARTS], qd, kv)
+
     def query_block(j, _):
         top[...] = jnp.full(top.shape, FLOOR, jnp.float32)
         total[...] = jnp.zeros(total.shape, jnp.float32)
@@ -84,9 +126,9 @@
             @pl.when(active)
             def _():
                 mask = tile_mask(place, query_first, key_first)
-                rows = pl.ds(pl.multiple_of(tile * TILE, TILE), TILE)
-                keys = kv[rows, :HD]
-                values = kv[rows, HD:]
+                one, two = (slot_rows(slot) for slot in tile_slots(place, tile))
+                keys = jnp.concatenate([kv[one, :HD], kv[two, :HD]], axis=0)
+                values = jnp.concatenate([kv[one, HD:], kv[two, HD:]], axis=0)
                 for pair in range(GROUP // 2):
                     span = pl.ds(pair * 2 * ROWS, 2 * ROWS)
                     grad_span = pl.ds((GROUP + pair * 2) * ROWS, 2 * ROWS)
@@ -120,9 +162,14 @@
     lax.fori_loop(0, Y * C, query_block, 0)
 
 
-def grads_kernel(
-    place, stats, qd, kv, kt, dq, dkv, log_total, delta, probs, grad_scores, dqt, dkv_sum
-):
+def grads_kernel(place, stats, *refs):
+    dq, dq_core = refs[PARTS : PARTS + 2]
+    sums, scratch = refs[PARTS + 2 : PARTS + 2 + len(GROUPS)], refs[PARTS + 2 + len(GROUPS) :]
+    qd, kv, kt, log_total, delta, probs, grad_scores, dqt, dkv_sum = scratch
+    gather_parts(refs[:PARTS], qd, kv)
+    for slot in range(Z):
+        rows = slice(slot * ROWS, (slot + 1) * ROWS)
+        kt[slot] = kv[rows, :HD].T
     mine_y, mine_c = place[9], place[10]
     for j in range(Y * C):
         parts = []
@@ -151,9 +198,9 @@
             @pl.when(active)
             def _():
                 mask = tile_mask(place, query_first, key_first)
-                rows = pl.ds(pl.multiple_of(tile * TILE, TILE), TILE)
-                keys = kv[rows, :HD]
-                values = kv[rows, HD:]
+                one, two = (slot_rows(slot) for slot in tile_slots(place, tile))
+                keys = jnp.concatenate([kv[one, :HD], kv[two, :HD]], axis=0)
+                values = jnp.concatenate([kv[one, HD:], kv[two, HD:]], axis=0)
                 for pair in range(GROUP // 2):
                     span = pl.ds(pair * 2 * ROWS, 2 * ROWS)
                     grad_span = pl.ds((GROUP + pair * 2) * ROWS, 2 * ROWS)
@@ -169,23 +216,82 @@
                         d = p * (grads[:, lanes] - delta[j, pl.ds(head, 1), :])
                         grad_scores[:, whole] = d.astype(jnp.bfloat16)
                 weights = grad_scores[...]
-                dqt[...] += dot(kt[:, rows], weights, NN)
-                dkv_sum[rows, :HD] += dot(weights, qd[j, pl.ds(0, GROUP * ROWS), :], NN)
-                dkv_sum[rows, HD:] += dot(
-                    probs[...], qd[j, pl.ds(GROUP * ROWS, GROUP * ROWS), :], NN
-                )
+                slots = tile_slots(place, tile)
+                keys_t = jnp.concatenate([kt[slots[0]], kt[slots[1]]], axis=1)
+                dqt[...] += dot(keys_t, weights, NN)
+                key_term = dot(weights, qd[j, pl.ds(0, GROUP * ROWS), :], NN)
+                value_term = dot(probs[...], qd[j, pl.ds(GROUP * ROWS, GROUP * ROWS), :], NN)
+                for i, rows in enumerate((one, two)):
+                    dkv_sum[rows, :HD] += key_term[i * ROWS : (i + 1) * ROWS]
+                    dkv_sum[rows, HD:] += value_term[i * ROWS : (i + 1) * ROWS]
 
             return 0
 
         lax.fori_loop(0, TILES, key_tile, 0)
-        for head in range(GROUP):
-            lanes = slice(head * ROWS, (head + 1) * ROWS)
-            dq[j, :, lanes] = (dqt[:, lanes].T * SCALE).astype(jnp.bfloat16)
+        for half, place_of in enumerate((dq, dq_core)):
+
+            @pl.when(j // 2 == half)
+            def _():
+                for head in range(GROUP):
+                    lanes = slice(head * ROWS, (head + 1) * ROWS)
+                    turned = dqt[:, lanes].T * SCALE
+                    place_of[lax.rem(j, 2), :, lanes] = turned.astype(jnp.bfloat16)
+
         return 0
 
     lax.fori_loop(0, Y * C, query_block, 0)
-    dkv[:, :HD] = (dkv_sum[:, :HD] * SCALE).astype(jnp.bfloat16)
-    dkv[:, HD:] = dkv_sum[:, HD:].astype(jnp.bfloat16)
+    slot = 0
+    for part in sums:
+        for i in range(part.shape[0]):
+            rows = slice(slot * ROWS, (slot + 1) * ROWS)
+            part[i, :, :HD] = (dkv_sum[rows, :HD] * SCALE).astype(jnp.bfloat16)
+            part[i, :, HD:] = dkv_sum[rows, HD:].astype(jnp.bfloat16)
+            slot += 1
+
+
+def own_kv_kernel(inputs, weight, keys, out):
+    values = dot(inputs[...], weight[...], NN).astype(jnp.bfloat16)
+    for k in range(out.shape[0]):
+        out[k, :, :HD] = keys[...]
+        out[k, :, HD:] = values
+
+
+def own_queries_kernel(index, labels, segments, queries, grads, out, place):
+    context = index[0]
+    y, z, c = context // (Z * C), lax.rem(context // C, Z), lax.rem(context, C)
+    side = lax.rem(y + z, 2)
+    for j in range(Y * C):
+        place[j] = at(y ^ (j & 1), z, c ^ (j >> 1))
+    place[4] = 2 * side + c
+    place[5] = 2 * Z + 2 * (1 - side) + c
+    for k in range(1, 4):
+        before = jnp.where(segments[...] < k, 1.0, 0.0).astype(jnp.float32)
+        place[5 + k] = jnp.sum(before).astype(jnp.int32)
+    for i, value in enumerate((y, c, side, z)):
+        place[9 + i] = value
+    for i, base in enumerate(BASES):
+        place[13 + i] = base
+    position = context * ROWS + lax.broadcasted_iota(
+        jnp.int32, (ROWS, labels.shape[1]), 0
+    )
+    labelled = jnp.where(position == labels[...], 3.0, 0.0).astype(jnp.float32)
+    weight = 1.0 + jnp.max(labelled, axis=1, keepdims=True)
+    for head in range(GROUP):
+        lanes = slice(head * HD, (head + 1) * HD)
+        out[head * ROWS : (head + 1) * ROWS] = queries[:, lanes]
+        weighted = grads[:, lanes].astype(jnp.float32) * weight
+        out[(GROUP + head) * ROWS : (GROUP + head + 1) * ROWS] = weighted.astype(jnp.bfloat16)
+
+
+def weight_kernel(place, inputs, grads, kept, sent):
+    total = dot(grads[...], inputs[...], TN)
+    width = kept.shape[1]
+    first = place[10] == 0
+    for i in range(kept.shape[0]):
+        turned = total[:, i * C * width : (i + 1) * C * width].T
+        low, high = turned[:width], turned[width:]
+        kept[i] = jnp.where(first, low, high).astype(jnp.bfloat16)
+        sent[i] = jnp.where(first, high, low).astype(jnp.bfloat16)
 
 
 def on_device(
@@ -199,82 +305,96 @@
 ):
     bf16, f32 = jnp.bfloat16, jnp.float32
     context = lax.axis_index("ctx")
-    mine_y, mine_z, mine_c = context // (Z * C), context // C % Z, context % C
-    side = (mine_y + mine_z) % 2
-    own_positions = context * ROWS + jnp.arange(ROWS, dtype=jnp.int32)
-    labelled = jnp.any(own_positions[:, None] == label_positions[None, :], axis=1)
-    loss_weight = jnp.where(labelled, 4.0, 1.0).astype(f32)
-    weighted = (output_grad.astype(f32) * loss_weight[:, None]).astype(bf16)
-    starts = [jnp.sum((segment_ids < k).astype(jnp.int32)) for k in range(1, 4)]
-    place = jnp.stack(
-        [
-            at(mine_y ^ (j & 1), mine_z, mine_c ^ (j >> 1)).astype(jnp.int32)
-            for j in range(Y * C)
-        ]
-        + [2 * side + mine_c, 2 * Z + 2 * (1 - side) + mine_c]
-        + starts
-        + [mine_y, mine_c]
-    ).astype(jnp.int32)
-
-    def by_head(x):
-        return x.reshape(ROWS, GROUP, HD).transpose(1, 0, 2).reshape(GROUP * ROWS, HD)
-
-    own = jnp.concatenate([by_head(rotated_queries), by_head(weighted)], axis=0)
-    across = lax.ppermute(own, "ctx", Y_SWAP)
-    values = jnp.dot(sublayer_input, value_weight, preferred_element_type=f32).astype(bf16)
-    own_kv = jnp.concatenate([rotated_keys, values], axis=1)
-    kv = lax.all_to_all(
-        jnp.broadcast_to(own_kv[None], (Z,) + own_kv.shape),
-        "ctx",
-        0,
-        0,
-        axis_index_groups=CLASSES,
-    ).reshape(Z * ROWS, 2 * HD)
-    beside = lax.ppermute(jnp.stack([own, across]), "ctx", C_SWAP)
-    qd = jnp.concatenate([own[None], across[None], beside], axis=0)
-
+    mine_y, mine_c = context // (Z * C), context % C
     smem = pl.BlockSpec(memory_space=pltpu.SMEM)
     vmem = pl.BlockSpec(memory_space=pltpu.VMEM)
-    params = pltpu.CompilerParams(vmem_limit_bytes=48 * 1024 * 1024)
+    params = pltpu.CompilerParams(vmem_limit_bytes=24 * 1024 * 1024)
+    column = pl.pallas_call(
+        own_kv_kernel,
+        out_shape=jax.ShapeDtypeStruct((Z // 4, ROWS, 2 * HD), bf16),
+        in_specs=[vmem] * 3,
+        out_specs=vmem,
+        compiler_params=params,
+    )(sublayer_input, value_weight, rotated_keys)
+    column, output_grad, rotated_queries = lax.optimization_barrier(
+        (column, output_grad, rotated_queries)
+    )
+    column = lax.all_to_all(column, "ctx", 0, 0, axis_index_groups=COLUMNS)
+
+    own, place = pl.pallas_call(
+        own_queries_kernel,
+        out_shape=(
+            jax.ShapeDtypeStruct((2 * GROUP * ROWS, HD), bf16),
+            jax.ShapeDtypeStruct((13 + len(BASES),), jnp.int32),
+        ),
+        in_specs=[smem] + [vmem] * 4,
+        out_specs=(vmem, smem),
+        compiler_params=params,
+    )(
+        context.astype(jnp.int32).reshape(1),
+        label_positions[None],
+        segment_ids.reshape(-1, HD),
+        rotated_queries,
+        output_grad,
+    )
+    across = lax.ppermute(own, "ctx", Y_SWAP)
+    beside = lax.ppermute(own, "ctx", C_SWAP)
+    plane = Y * C
+    column, beside = lax.optimization_barrier((column, beside))
+    kv = [
+        column,
+        along_z(column, 1),
+        along_z(column, -1),
+        along_z(column[:2], 2),
+        along_z(column[2:], -2),
+    ]
+    corner = lax.ppermute(across, "ctx", C_SWAP)
+    operands = [own, across, beside, corner]
+    operands += kv
     stat = pltpu.VMEM((GROUP, 8, ROWS), f32)
+    all_qd = pltpu.VMEM((plane, 2 * GROUP * ROWS, HD), bf16)
+    all_kv = pltpu.VMEM((Z * ROWS, 2 * HD), bf16)
     stats = pl.pallas_call(
         stats_kernel,
-        out_shape=jax.ShapeDtypeStruct((3, Y * C, GROUP, ROWS), f32),
-        in_specs=[smem, vmem, vmem],
+        out_shape=jax.ShapeDtypeStruct((3, plane, GROUP, ROWS), f32),
+        in_specs=[smem] + [vmem] * PARTS,
         out_specs=vmem,
-        scratch_shapes=[stat, stat, stat],
+        scratch_shapes=[all_qd, all_kv, stat, stat, stat],
         compiler_params=params,
-    )(place, qd, kv)
+    )(place, *operands)
     all_stats = lax.all_gather(stats, "ctx", axis_index_groups=QUADS)
-    kt = kv[:, :HD].T
-    dq, dkv = pl.pallas_call(
+    dq, dq_core, *sums = pl.pallas_call(
         grads_kernel,
-        out_shape=(
-            jax.ShapeDtypeStruct((Y * C, ROWS, GROUP * HD), bf16),
-            jax.ShapeDtypeStruct((Z * ROWS, 2 * HD), bf16),
-        ),
-        in_specs=[smem, vmem, vmem, vmem, vmem],
-        out_specs=(vmem, vmem),
+        out_shape=[jax.ShapeDtypeStruct((2, ROWS, GROUP * HD), bf16)] * 2
+        + [jax.ShapeDtypeStruct((n, ROWS, 2 * HD), bf16) for n in GROUPS],
+        in_specs=[smem, vmem] + [vmem] * PARTS,
+        out_specs=[vmem] * (2 + len(GROUPS)),
         scratch_shapes=[
-            pltpu.VMEM((Y * C, GROUP, ROWS), f32),
-            pltpu.VMEM((Y * C, GROUP, ROWS), f32),
+            all_qd,
+            all_kv,
+            pltpu.VMEM((Z, HD, ROWS), bf16),
+            pltpu.VMEM((plane, GROUP, ROWS), f32),
+            pltpu.VMEM((plane, GROUP, ROWS), f32),
             pltpu.VMEM((TILE, GROUP * ROWS), bf16),
             pltpu.VMEM((TILE, GROUP * ROWS), bf16),
             pltpu.VMEM((HD, GROUP * ROWS), f32),
             pltpu.VMEM((Z * ROWS, 2 * HD), f32),
         ],
         compiler_params=params,
-    )(place, all_stats, qd, kv, kt)
-
-    from_core = lax.ppermute(dq[2:], "ctx", C_SWAP).astype(f32)
+    )(place, all_stats, *operands)
+
+    back = [along_z(part, d) for part, d in zip(sums[1:], (-1, 1, -2, 2))]
+    back[2], dq_core = lax.optimization_barrier((back[2], dq_core))
+    from_core = lax.ppermute(dq_core, "ctx", C_SWAP)
+    last = jnp.concatenate(back[2:], axis=0)
+    column = sums[0].astype(f32) + back[0].astype(f32) + back[1].astype(f32) + last.astype(f32)
+    column, from_core = lax.optimization_barrier((column.astype(bf16), from_core))
+    from_core = from_core.astype(f32)
     for_across = (dq[1].astype(f32) + from_core[1]).astype(bf16)
     from_across = lax.ppermute(for_across, "ctx", Y_SWAP).astype(f32)
     query_grad = (dq[0].astype(f32) + from_core[0] + from_across).astype(bf16)
-
-    parts = lax.all_to_all(
-        dkv.reshape(Z, ROWS, 2 * HD), "ctx", 0, 0, axis_index_groups=CLASSES
-    )
-    summed = jnp.sum(parts.astype(f32), axis=0).astype(bf16)
+    column = lax.all_to_all(column, "ctx", 0, 0, axis_index_groups=COLUMNS)
+    summed = jnp.sum(column.astype(f32), axis=0).astype(bf16)
     key_grad = summed[:, :HD]
     value_grad = summed[:, HD:]
 
@@ -289,17 +409,20 @@
     input_parts = lax.all_to_all(input_terms, "mp", 0, 0)
     input_grad = jnp.sum(input_parts.astype(f32), axis=0).astype(bf16)
 
-    term = lax.dot_general(
-        sublayer_input, value_grad, (((0,), (0,)), ((), ())), preferred_element_type=f32
-    ).astype(bf16)
-    piece = term.shape[0] // (Y * Z * C)
-    term = term.reshape(Y * Z, C, piece, HD)
-    near = lax.ppermute(jnp.where(mine_c == 0, term[:, 1], term[:, 0]), "ctx", C_SWAP)
-    term = jnp.where(mine_c == 0, term[:, 0], term[:, 1]).astype(f32) + near.astype(f32)
-    term = term.astype(bf16).reshape(Y, Z, piece, HD)
+    piece = sublayer_input.shape[1] // (Y * Z * C)
+    kept, sent = pl.pallas_call(
+        weight_kernel,
+        out_shape=[jax.ShapeDtypeStruct((Y * Z, piece, HD), bf16)] * C,
+        in_specs=[smem, vmem, vmem],
+        out_specs=[vmem] * C,
+        compiler_params=params,
+    )(place, sublayer_input, value_grad)
+    near = lax.ppermute(sent, "ctx", C_SWAP)
+    term = (kept.astype(f32) + near.astype(f32)).astype(bf16).reshape(Y, Z, piece, HD)
     far = lax.ppermute(jnp.where(mine_y == 0, term[1], term[0]), "ctx", Y_SWAP)
     term = jnp.where(mine_y == 0, term[0], term[1]).astype(f32) + far.astype(f32)
-    pieces = lax.all_to_all(term.astype(bf16), "ctx", 0, 0, axis_index_groups=LINES)
+    term = term.astype(bf16)
+    pieces = lax.all_to_all(term, "ctx", 0, 0, axis_index_groups=LINES)
     value_weight_grad = jnp.sum(pieces.astype(f32), axis=0).astype(bf16)
     return (query_grad, key_grad, input_grad, value_weight_grad)
 

time: 238 us -> 214 us (0.90)
  waiting for transfers between devices: 107 us -> 65 us
  blocking collectives: 5.61 us -> 29.8 us
  starting transfers between devices: 73.2 us -> 89.4 us
  local copies, waits for them, and re-layouts: 16.1 us -> 3.87 us
  other arithmetic: 9.79 us -> 4.72 us
  matrix products: 4.65 us -> 1.45 us
    all_to_all x3 -> x2, waiting for transfers between devices: 71.1 us -> 6.6 us  [the longest x1 6 us: on_device(): pieces = lax.all_to_all(term, 'ctx', 0, 0, axis_index_groups=LINES)]
    ppermute x3 -> x12, starting transfers between devices: 5.74 us -> 54.6 us  [the longest x8 41.3 us: along_z(): return lax.ppermute(value, 'ctx', pairs)]
    all_to_all x3 -> x2, starting transfers between devices: 52.8 us -> 19.7 us  [the longest x1 15.1 us: on_device(): column = lax.all_to_all(column, 'ctx', 0, 0, axis_index_groups=COLUMNS)]
    ppermute x3 -> x12, waiting for transfers between devices: 0.03 us -> 26.5 us  [the longest x8 26.5 us: along_z(): return lax.ppermute(value, 'ctx', pairs)]
    all_to_all x0 -> x1, blocking collectives: none -> 21.9 us  [on_device(): column = lax.all_to_all(column, 'ctx', 0, 0, axis_index_groups=COLUMNS)]
    ppermute x1, waiting for transfers between devices: 17.3 us -> 10.7 us  [on_device(): across = lax.ppermute(own, 'ctx', Y_SWAP)]
    reshape x3 -> x0, local copies, waits for them, and re-layouts: 3.69 us -> none  [the longest x2 3.64 us: on_device(): kv = lax.all_to_all(jnp.broadcast_to(own_kv[None], (Z,) + own_kv.shape),...]
    dot_general x2 -> x0, matrix products: 3.22 us -> none  [the longest x1 1.74 us: on_device(): jnp.dot(sublayer_input, value_weight, preferred_element_type=f32)]
  transfers between devices with their start and end apart: 10 -> 18, of which waited for: 6 -> 9; matrix products, arithmetic and copies ran while one was open for 5% -> 3% of each run, Pallas kernels for 0% -> 0%
where the time goes in v2:
time: 214 us; the launch traced here: 212 us
  starting transfers between devices  89.4 us (42%)
  waiting for transfers between devices  65 us (30%)
  blocking collectives  29.8 us (14%)
  Pallas kernels  17.1 us (8%)
  other arithmetic  4.72 us (2%)
  local copies, waits for them, and re-layouts  3.87 us (2%)
    ppermute x8, starting transfers between devices, along_z(): return lax.ppermute(value, 'ctx', pairs)  41.3 us
    ppermute x8, waiting for transfers between devices, along_z(): return lax.ppermute(value, 'ctx', pairs)  26.5 us
    all_to_all x1, blocking collectives, on_device(): column = lax.all_to_all(column, 'ctx', 0, 0, axis_index_groups=COLUMNS)  21.9 us
    ppermute x1, waiting for transfers between devices, on_device(): far = lax.ppermute(jnp.where(mine_y == 0, term[1], term[0]), 'ctx', Y_SWAP)  15.2 us
    all_to_all x1, starting transfers between devices, on_device(): column = lax.all_to_all(column, 'ctx', 0, 0, axis_index_groups=COLUMNS)  15.1 us
    ppermute x1, waiting for transfers between devices, on_device(): across = lax.ppermute(own, 'ctx', Y_SWAP)  10.7 us
    pallas_call x1, Pallas kernels, on_device(): pl.pallas_call(grads_kernel, out_shape=[jax.ShapeDtypeStruct((2, ROWS, GR...  8.65 us
    all_gather x1, blocking collectives, on_device(): all_stats = lax.all_gather(stats, 'ctx', axis_index_groups=QUADS)  7.88 us
  transfers between devices with their start and end apart: 18, of which 9 were waited for; matrix products, arithmetic and copies ran while one was open for 3% of the time, Pallas kernels for 0%

profile of v2, /device:TPU:24, one launch (start us, length us, event | category | flops | bytes accessed | tf_op | source)
XLA Modules:
  0.0 212.3 jit_solution(1568086582315979897)
XLA Ops:
  5.0 15.1 %all-to-all-start = ((bf16[4,128,256]{2,1,0:T(8,128)(2,1)}), bf16[4,128,256]{2,1,0:T(8,128)(2,1)S(1)}, u32[]{:S(2)}, u32[]{:S(2)}) async-start(bf16[4,128,256]{2,1,0:T(8,128)(2,1)} %shard_map.102), calls=%async_computation | async-start | bytes 524288 | tf_op jit(solution)/shard_map/all_to_all | solution.py:322
  20.8 2.7 %collective-permute-start = (bf16[2048,128]{1,0:T(8,128)(2,1)S(1)}, bf16[2048,128]{1,0:T(8,128)(2,1)S(1)}, u32[]{:S(2)}, u32[]{:S(2)}) collective-permute-start(bf16[2048,128]{1,0:T(8,128)(2,1)S(1)} %get-tuple-element.27.refs_0_), channel_id=1, source_target_pairs={{0,256},{8,264},{16,272},{24,280},{32,288},{40,296},{48,304},{56,3... | collective-permute-start | bytes 1572872 | tf_op jit(solution)/shard_map/ppermute | solution.py:340
  25.4 10.7 %collective-permute-done.refs_1_ = bf16[2048,128]{1,0:T(8,128)(2,1)S(1)} collective-permute-done((bf16[2048,128]{1,0:T(8,128)(2,1)S(1)}, bf16[2048,128]{1,0:T(8,128)(2,1)S(1)}, u32[]{:S(2)}, u32[]{:S(2)}) %collective-permute-start) | collective-permute-done | bytes 524320 | tf_op jit(solution)/shard_map/ppermute | solution.py:340
  38.6 5.8 %collective-permute-start.4 = (bf16[4,128,256]{2,1,0:T(8,128)(2,1)S(1)}, bf16[4,128,256]{2,1,0:T(8,128)(2,1)S(1)}, u32[]{:S(2)}, u32[]{:S(2)}) collective-permute-start(bf16[4,128,256]{2,1,0:T(8,128)(2,1)S(1)} %all-to-all-done.refs_4_), channel_id=1, source_target_pairs={{0,496},{8,504},{16,256},{24,264},{32,272},{40,280},{48,288},{56,2... | collective-permute-start | bytes 786440 | tf_op jit(solution)/shard_map/ppermute | solution.py:53
  46.4 5.1 %collective-permute-start.6 = (bf16[2,128,256]{2,1,0:T(8,128)(2,1)S(1)}, bf16[2,128,256]{2,1,0:T(8,128)(2,1)S(1)}, u32[]{:S(2)}, u32[]{:S(2)}) collective-permute-start(bf16[2,128,256]{2,1,0:T(8,128)(2,1)S(1)} %get-tuple-element.44), channel_id=1, source_target_pairs={{0,224},{8,232},{16,240},{24,248},{32,0},{40,8},{48,16},{56,24},{6... | collective-permute-start | bytes 393224 | tf_op jit(solution)/shard_map/ppermute | solution.py:53
  53.4 3.7 %collective-permute-done.6.refs_8_ = bf16[2,128,256]{2,1,0:T(8,128)(2,1)S(1)} collective-permute-done((bf16[2,128,256]{2,1,0:T(8,128)(2,1)S(1)}, bf16[2,128,256]{2,1,0:T(8,128)(2,1)S(1)}, u32[]{:S(2)}, u32[]{:S(2)}) %collective-permute-start.6) | collective-permute-done | bytes 131104 | tf_op jit(solution)/shard_map/ppermute | solution.py:53
  57.1 5.2 %collective-permute-done.5.refs_7_ = bf16[2,128,256]{2,1,0:T(8,128)(2,1)S(1)} collective-permute-done((bf16[2,128,256]{2,1,0:T(8,128)(2,1)S(1)}, bf16[2,128,256]{2,1,0:T(8,128)(2,1)S(1)}, u32[]{:S(2)}, u32[]{:S(2)}) %collective-permute-start.5) | collective-permute-done | bytes 131104 | tf_op jit(solution)/shard_map/ppermute | solution.py:53
  62.3 4.7 %shard_map.104 = f32[3,4,8,128]{3,2,1,0:T(8,128)S(1)} custom-call(s32[17]{0:T(128)S(1)} %get-tuple-element.26.place, bf16[2048,128]{1,0:T(8,128)(2,1)S(1)} %get-tuple-element.27.refs_0_, bf16[2048,128]{1,0:T(8,128)(2,1)S(1)} %collective-permute-done.refs_1_, bf16[2048,128]{1,0:T(8,128)(2,1)S(1)} %collective-permute-done.1.refs_2_, ...), custom_call_target="tpu_custom_call" | custom-call | tf_op jit(solution)/shard_map/pallas_call | solution.py:357
  67.0 7.9 %all-gather = f32[12,4,8,128]{3,2,1,0:T(8,128)S(1)} all-gather(f32[3,4,8,128]{3,2,1,0:T(8,128)S(1)} %shard_map.104), channel_id=2, replica_groups={{0,8,256,264},{16,24,272,280},{32,40,288,296},{48,56,304,312},{64,72,32..., dimensions={0}, use_global_device_ids=true | all-gather | bytes 245760 | tf_op jit(solution)/shard_map/all_gather | solution.py:365
  74.9 8.7 %shard_map.105 = (bf16[2,128,1024]{2,1,0:T(8,128)(2,1)S(1)}, bf16[2,128,1024]{2,1,0:T(8,128)(2,1)S(1)}, bf16[4,128,256]{2,1,0:T(8,128)(2,1)S(1)}, bf16[4,128,256...) custom-call(s32[17]{0:T(128)S(1)} %get-tuple-element.26.place, ...), custom_call_target="tpu_custom_call" | custom-call | tf_op jit(solution)/shard_map/pallas_call | solution.py:366
  83.5 16.4 %collective-permute-start.9 = (bf16[2,128,256]{2,1,0:T(8,128)(2,1)S(1)}, bf16[2,128,256]{2,1,0:T(8,128)(2,1)S(1)}, u32[]{:S(2)}, u32[]{:S(2)}) collective-permute-start(bf16[2,128,256]{2,1,0:T(8,128)(2,1)S(1)} %get-tuple-element.35), channel_id=1, source_target_pairs={{0,224},{8,232},{16,240},{24,248},{32,0},{40,8},{48,16},{56,24},{6... | collective-permute-start | bytes 393224 | tf_op jit(solution)/shard_map/ppermute | solution.py:53
  99.9 2.5 %collective-permute-done.9 = bf16[2,128,256]{2,1,0:T(8,128)(2,1)S(1)} collective-permute-done((bf16[2,128,256]{2,1,0:T(8,128)(2,1)S(1)}, bf16[2,128,256]{2,1,0:T(8,128)(2,1)S(1)}, u32[]{:S(2)}, u32[]{:S(2)}) %collective-permute-start.9) | collective-permute-done | bytes 131104 | tf_op jit(solution)/shard_map/ppermute | solution.py:53
  102.4 7.5 %collective-permute-start.11 = (bf16[2,128,1024]{2,1,0:T(8,128)(2,1)S(1)}, bf16[2,128,1024]{2,1,0:T(8,128)(2,1)}, u32[]{:S(2)}, u32[]{:S(2)}) collective-permute-start(bf16[2,128,1024]{2,1,0:T(8,128)(2,1)S(1)} %get-tuple-element.39), channel_id=1, source_target_pairs={{0,8},{8,0},{16,24},{24,16},{32,40},{40,32},{48,56},{56,48},{64,72... | collective-permute-start | bytes 1572872 | tf_op jit(solution)/shard_map/ppermute | solution.py:388
  109.9 6.4 %collective-permute-start.7 = (bf16[4,128,256]{2,1,0:T(8,128)(2,1)S(1)}, bf16[4,128,256]{2,1,0:T(8,128)(2,1)S(1)}, u32[]{:S(2)}, u32[]{:S(2)}) collective-permute-start(bf16[4,128,256]{2,1,0:T(8,128)(2,1)S(1)} %get-tuple-element.33), channel_id=1, source_target_pairs={{0,496},{8,504},{16,256},{24,264},{32,272},{40,280},{48,288},{56,2... | collective-permute-start | bytes 786440 | tf_op jit(solution)/shard_map/ppermute | solution.py:53
  116.3 1.9 collective-permute-start.8
  118.2 1.9 collective-permute-start.10
  120.2 15.1 %collective-permute-done.10 = bf16[2,128,256]{2,1,0:T(8,128)(2,1)S(1)} collective-permute-done((bf16[2,128,256]{2,1,0:T(8,128)(2,1)S(1)}, bf16[2,128,256]{2,1,0:T(8,128)(2,1)S(1)}, u32[]{:S(2)}, u32[]{:S(2)}) %collective-permute-start.10) | collective-permute-done | bytes 131104 | tf_op jit(solution)/shard_map/ppermute | solution.py:53
  135.5 21.9 %all_to_all.20 = bf16[4,128,256]{2,1,0:T(8,128)(2,1)S(1)} all-to-all(bf16[4,128,256]{2,1,0:T(8,128)(2,1)S(1)} %add_convert_fusion.2), channel_id=1, replica_groups={{0,64,128,192},{8,72,136,200},{16,80,144,208},{24,88,152,216},{32,96,16..., dimensions={0} | all-to-all | bytes 524288 | tf_op jit(solution)/shard_map/all_to_all | solution.py:396
  163.4 7.3 %all-to-all-start.2 = ((bf16[8,128,512]{2,1,0:T(8,128)(2,1)}), bf16[8,128,512]{2,1,0:T(8,128)(2,1)S(1)}, u32[]{:S(2)}, u32[]{:S(2)}) async-start(bf16[8,128,512]{2,1,0:T(8,128)(2,1)} %fusion), calls=%async_computation.2 | async-start | bytes 2097152 | tf_op jit(solution)/shard_map/all_to_all | solution.py:409
  172.8 15.2 %collective-permute-done.14 = bf16[16,64,128]{2,1,0:T(8,128)(2,1)S(1)} collective-permute-done((bf16[16,64,128]{2,1,0:T(8,128)(2,1)S(1)}, bf16[16,64,128]{2,1,0:T(8,128)(2,1)S(1)}, u32[]{:S(2)}, u32[]{:S(2)}) %collective-permute-start.14) | collective-permute-done | bytes 262176 | tf_op jit(solution)/shard_map/ppermute | solution.py:422
  188.9 4.6 %all-to-all-start.3 = ((bf16[16,64,128]{2,1,0:T(8,128)(2,1)}), bf16[16,64,128]{2,1,0:T(8,128)(2,1)S(1)}, u32[]{:S(2)}, u32[]{:S(2)}) async-start(bf16[16,64,128]{2,1,0:T(8,128)(2,1)} %add_convert_fusion.1), calls=%async_computation.3 | async-start | bytes 524288 | tf_op jit(solution)/shard_map/all_to_all | solution.py:425
  194.7 3.3 %collective-permute-start.12 = (bf16[128,1024]{1,0:T(8,128)(2,1)S(1)}, bf16[128,1024]{1,0:T(8,128)(2,1)S(1)}, u32[]{:S(2)}, u32[]{:S(2)}) collective-permute-start(bf16[128,1024]{1,0:T(8,128)(2,1)S(1)} %fusion.5), channel_id=1, source_target_pairs={{0,256},{8,264},{16,272},{24,280},{32,288},{40,296},{48,304},{56,3... | collective-permute-start | bytes 786440 | tf_op jit(solution)/shard_map/ppermute | solution.py:394
  198.0 6.0 %collective-permute-done.12 = bf16[128,1024]{1,0:T(8,128)(2,1)S(1)} collective-permute-done((bf16[128,1024]{1,0:T(8,128)(2,1)S(1)}, bf16[128,1024]{1,0:T(8,128)(2,1)S(1)}, u32[]{:S(2)}, u32[]{:S(2)}) %collective-permute-start.12) | collective-permute-done | bytes 262176 | tf_op jit(solution)/shard_map/ppermute | solution.py:394
  205.6 6.0 %all-to-all-done.3 = bf16[16,64,128]{2,1,0:T(8,128)(2,1)S(1)} async-done(((bf16[16,64,128]{2,1,0:T(8,128)(2,1)}), bf16[16,64,128]{2,1,0:T(8,128)(2,1)S(1)}, u32[]{:S(2)}, u32[]{:S(2)}) %all-to-all-start.3) | async-done | bytes 262176 | tf_op jit(solution)/shard_map/all_to_all | solution.py:425
  (50 shorter events, 25.9 us)
Async XLA Ops:
  3.8 16.2 %copy-start.4 = (bf16[128,1024]{1,0:T(8,128)(2,1)S(1)}, bf16[128,1024]{1,0:T(8,128)(2,1)}, u32[]{:S(2)}) copy-start(bf16[128,1024]{1,0:T(8,128)(2,1)} %queries) | copy-start | bytes 786436
  3.8 16.2 %copy-start.5 = (bf16[128,1024]{1,0:T(8,128)(2,1)S(1)}, bf16[128,1024]{1,0:T(8,128)(2,1)}, u32[]{:S(2)}) copy-start(bf16[128,1024]{1,0:T(8,128)(2,1)} %grads) | copy-start | bytes 786436
  3.8 16.2 %copy-start.7 = (s32[8192]{0:T(1024)S(1)}, s32[8192]{0:T(1024)}, u32[]{:S(2)}) copy-start(s32[8192]{0:T(1024)} %param.12) | copy-start | bytes 98308
  3.9 16.2 %copy-start.8 = (s32[128]{0:T(128)S(1)}, s32[128]{0:T(128)}, u32[]{:S(2)}) copy-start(s32[128]{0:T(128)} %param.13) | copy-start | bytes 1540
  5.0 33.7 %all-to-all-start = ((bf16[4,128,256]{2,1,0:T(8,128)(2,1)}), bf16[4,128,256]{2,1,0:T(8,128)(2,1)S(1)}, u32[]{:S(2)}, u32[]{:S(2)}) async-start(bf16[4,128,256]{2,1,0:T(8,128)(2,1)} %shard_map.102), calls=%async_computation | async-start | bytes 524288 | tf_op jit(solution)/shard_map/all_to_all | solution.py:322
  20.8 15.3 %collective-permute-start = (bf16[2048,128]{1,0:T(8,128)(2,1)S(1)}, bf16[2048,128]{1,0:T(8,128)(2,1)S(1)}, u32[]{:S(2)}, u32[]{:S(2)}) collective-permute-start(bf16[2048,128]{1,0:T(8,128)(2,1)S(1)} %get-tuple-element.27.refs_0_), channel_id=1, source_target_pairs={{0,256},{8,264},{16,272},{24,280},{32,288},{40,296},{48,304},{56,3... | collective-permute-start | bytes 1572872 | tf_op jit(solution)/shard_map/ppermute | solution.py:340
  23.5 14.5 %collective-permute-start.1 = (bf16[2048,128]{1,0:T(8,128)(2,1)S(1)}, bf16[2048,128]{1,0:T(8,128)(2,1)S(1)}, u32[]{:S(2)}, u32[]{:S(2)}) collective-permute-start(bf16[2048,128]{1,0:T(8,128)(2,1)S(1)} %get-tuple-element.27.refs_0_), channel_id=1, source_target_pairs={{0,8},{8,0},{16,24},{24,16},{32,40},{40,32},{48,56},{56,48},{64,72... | collective-permute-start | bytes 1572872 | tf_op jit(solution)/shard_map/ppermute | solution.py:341
  36.1 26.2 %collective-permute-start.2 = (bf16[2048,128]{1,0:T(8,128)(2,1)S(1)}, bf16[2048,128]{1,0:T(8,128)(2,1)S(1)}, u32[]{:S(2)}, u32[]{:S(2)}) collective-permute-start(bf16[2048,128]{1,0:T(8,128)(2,1)S(1)} %collective-permute-done.refs_1_), channel_id=1, source_target_pairs={{0,8},{8,0},{16,24},{24,16},{32,40},{40,32},{48,56},{56,48},{64,72... | collective-permute-start | bytes 1572872 | tf_op jit(solution)/shard_map/ppermute | solution.py:351
  38.6 23.7 %collective-permute-start.4 = (bf16[4,128,256]{2,1,0:T(8,128)(2,1)S(1)}, bf16[4,128,256]{2,1,0:T(8,128)(2,1)S(1)}, u32[]{:S(2)}, u32[]{:S(2)}) collective-permute-start(bf16[4,128,256]{2,1,0:T(8,128)(2,1)S(1)} %all-to-all-done.refs_4_), channel_id=1, source_target_pairs={{0,496},{8,504},{16,256},{24,264},{32,272},{40,280},{48,288},{56,2... | collective-permute-start | bytes 786440 | tf_op jit(solution)/shard_map/ppermute | solution.py:53
  44.5 17.8 %collective-permute-start.3 = (bf16[4,128,256]{2,1,0:T(8,128)(2,1)S(1)}, bf16[4,128,256]{2,1,0:T(8,128)(2,1)S(1)}, u32[]{:S(2)}, u32[]{:S(2)}) collective-permute-start(bf16[4,128,256]{2,1,0:T(8,128)(2,1)S(1)} %all-to-all-done.refs_4_), channel_id=1, source_target_pairs={{0,272},{8,280},{16,288},{24,296},{32,304},{40,312},{48,320},{56,3... | collective-permute-start | bytes 786440 | tf_op jit(solution)/shard_map/ppermute | solution.py:53
  46.4 10.7 %collective-permute-start.6 = (bf16[2,128,256]{2,1,0:T(8,128)(2,1)S(1)}, bf16[2,128,256]{2,1,0:T(8,128)(2,1)S(1)}, u32[]{:S(2)}, u32[]{:S(2)}) collective-permute-start(bf16[2,128,256]{2,1,0:T(8,128)(2,1)S(1)} %get-tuple-element.44), channel_id=1, source_target_pairs={{0,224},{8,232},{16,240},{24,248},{32,0},{40,8},{48,16},{56,24},{6... | collective-permute-start | bytes 393224 | tf_op jit(solution)/shard_map/ppermute | solution.py:53
  51.5 10.8 %collective-permute-start.5 = (bf16[2,128,256]{2,1,0:T(8,128)(2,1)S(1)}, bf16[2,128,256]{2,1,0:T(8,128)(2,1)S(1)}, u32[]{:S(2)}, u32[]{:S(2)}) collective-permute-start(bf16[2,128,256]{2,1,0:T(8,128)(2,1)S(1)} %get-tuple-element.45), channel_id=1, source_target_pairs={{0,32},{8,40},{16,48},{24,56},{32,64},{40,72},{48,80},{56,88},{64,... | collective-permute-start | bytes 393224 | tf_op jit(solution)/shard_map/ppermute | solution.py:53
  83.5 18.9 %collective-permute-start.9 = (bf16[2,128,256]{2,1,0:T(8,128)(2,1)S(1)}, bf16[2,128,256]{2,1,0:T(8,128)(2,1)S(1)}, u32[]{:S(2)}, u32[]{:S(2)}) collective-permute-start(bf16[2,128,256]{2,1,0:T(8,128)(2,1)S(1)} %get-tuple-element.35), channel_id=1, source_target_pairs={{0,224},{8,232},{16,240},{24,248},{32,0},{40,8},{48,16},{56,24},{6... | collective-permute-start | bytes 393224 | tf_op jit(solution)/shard_map/ppermute | solution.py:53
  102.4 33.1 %collective-permute-start.11 = (bf16[2,128,1024]{2,1,0:T(8,128)(2,1)S(1)}, bf16[2,128,1024]{2,1,0:T(8,128)(2,1)}, u32[]{:S(2)}, u32[]{:S(2)}) collective-permute-start(bf16[2,128,1024]{2,1,0:T(8,128)(2,1)S(1)} %get-tuple-element.39), channel_id=1, source_target_pairs={{0,8},{8,0},{16,24},{24,16},{32,40},{40,32},{48,56},{56,48},{64,72... | collective-permute-start | bytes 1572872 | tf_op jit(solution)/shard_map/ppermute | solution.py:388
  109.9 25.3 %collective-permute-start.7 = (bf16[4,128,256]{2,1,0:T(8,128)(2,1)S(1)}, bf16[4,128,256]{2,1,0:T(8,128)(2,1)S(1)}, u32[]{:S(2)}, u32[]{:S(2)}) collective-permute-start(bf16[4,128,256]{2,1,0:T(8,128)(2,1)S(1)} %get-tuple-element.33), channel_id=1, source_target_pairs={{0,496},{8,504},{16,256},{24,264},{32,272},{40,280},{48,288},{56,2... | collective-permute-start | bytes 786440 | tf_op jit(solution)/shard_map/ppermute | solution.py:53
  116.3 19.0 %collective-permute-start.8 = (bf16[4,128,256]{2,1,0:T(8,128)(2,1)S(1)}, bf16[4,128,256]{2,1,0:T(8,128)(2,1)S(1)}, u32[]{:S(2)}, u32[]{:S(2)}) collective-permute-start(bf16[4,128,256]{2,1,0:T(8,128)(2,1)S(1)} %get-tuple-element.34), channel_id=1, source_target_pairs={{0,272},{8,280},{16,288},{24,296},{32,304},{40,312},{48,320},{56,3... | collective-permute-start | bytes 786440 | tf_op jit(solution)/shard_map/ppermute | solution.py:53
  118.2 17.0 %collective-permute-start.10 = (bf16[2,128,256]{2,1,0:T(8,128)(2,1)S(1)}, bf16[2,128,256]{2,1,0:T(8,128)(2,1)S(1)}, u32[]{:S(2)}, u32[]{:S(2)}) collective-permute-start(bf16[2,128,256]{2,1,0:T(8,128)(2,1)S(1)} %get-tuple-element.38), channel_id=1, source_target_pairs={{0,32},{8,40},{16,48},{24,56},{32,64},{40,72},{48,80},{56,88},{64,... | collective-permute-start | bytes 393224 | tf_op jit(solution)/shard_map/ppermute | solution.py:53
  135.3 22.8 %copy-start.1 = (bf16[128,4096]{1,0:T(8,128)(2,1)S(1)}, bf16[128,4096]{1,0:T(8,128)(2,1)}, u32[]{:S(2)}) copy-start(bf16[128,4096]{1,0:T(8,128)(2,1)} %inputs.3) | copy-start | bytes 3145732
  135.4 26.5 %copy-start.3 = (bf16[4096,128]{1,0:T(8,128)(2,1)S(1)}, bf16[4096,128]{1,0:T(8,128)(2,1)}, u32[]{:S(2)}) copy-start(bf16[4096,128]{1,0:T(8,128)(2,1)} %weight.1) | copy-start | bytes 3145732
  160.0 10.7 %collective-permute-start.13 = (bf16[32,64,128]{2,1,0:T(8,128)(2,1)}, bf16[32,64,128]{2,1,0:T(8,128)(2,1)S(1)}, u32[]{:S(2)}, u32[]{:S(2)}) collective-permute-start(bf16[32,64,128]{2,1,0:T(8,128)(2,1)} %get-tuple-element.43), channel_id=1, source_target_pairs={{0,8},{8,0},{16,24},{24,16},{32,40},{40,32},{48,56},{56,48},{64,72... | collective-permute-start | bytes 1572872 | tf_op jit(solution)/shard_map/ppermute | solution.py:420
  163.4 25.5 %all-to-all-start.2 = ((bf16[8,128,512]{2,1,0:T(8,128)(2,1)}), bf16[8,128,512]{2,1,0:T(8,128)(2,1)S(1)}, u32[]{:S(2)}, u32[]{:S(2)}) async-start(bf16[8,128,512]{2,1,0:T(8,128)(2,1)} %fusion), calls=%async_computation.2 | async-start | bytes 2097152 | tf_op jit(solution)/shard_map/all_to_all | solution.py:409
  170.9 17.2 %collective-permute-start.14 = (bf16[16,64,128]{2,1,0:T(8,128)(2,1)S(1)}, bf16[16,64,128]{2,1,0:T(8,128)(2,1)S(1)}, u32[]{:S(2)}, u32[]{:S(2)}) collective-permute-start(bf16[16,64,128]{2,1,0:T(8,128)(2,1)S(1)} %broadcast_select_fusion), channel_id=1, source_target_pairs={{0,256},{8,264},{16,272},{24,280},{32,288},{40,296},{48,304},{56,3... | collective-permute-start | bytes 786440 | tf_op jit(solution)/shard_map/ppermute | solution.py:422
  188.9 22.8 %all-to-all-start.3 = ((bf16[16,64,128]{2,1,0:T(8,128)(2,1)}), bf16[16,64,128]{2,1,0:T(8,128)(2,1)S(1)}, u32[]{:S(2)}, u32[]{:S(2)}) async-start(bf16[16,64,128]{2,1,0:T(8,128)(2,1)} %add_convert_fusion.1), calls=%async_computation.3 | async-start | bytes 524288 | tf_op jit(solution)/shard_map/all_to_all | solution.py:425
  194.7 9.3 %collective-permute-start.12 = (bf16[128,1024]{1,0:T(8,128)(2,1)S(1)}, bf16[128,1024]{1,0:T(8,128)(2,1)S(1)}, u32[]{:S(2)}, u32[]{:S(2)}) collective-permute-start(bf16[128,1024]{1,0:T(8,128)(2,1)S(1)} %fusion.5), channel_id=1, source_target_pairs={{0,256},{8,264},{16,272},{24,280},{32,288},{40,296},{48,304},{56,3... | collective-permute-start | bytes 786440 | tf_op jit(solution)/shard_map/ppermute | solution.py:394
  (3 other events, 3.2 us)

commit v3 on v2

--- a/solution.py
+++ b/solution.py
@@ -17,7 +17,8 @@
 FLOOR = -1e30
 HIDDEN = -1e32
 Y, Z, C = 2, 16, 2
-TILE = 256
+TILE = 512
+BLOCKS = TILE // ROWS
 TILES = Z * ROWS // TILE
 NT = (((1,), (1,)), ((), ()))
 NN = (((1,), (0,)), ((), ()))
@@ -31,6 +32,9 @@
 Y_SWAP = [(i, i ^ (Z * C)) for i in range(Y * Z * C)]
 C_SWAP = [(i, i ^ 1) for i in range(Y * Z * C)]
 QUADS = [[at(y, z, c) for y in range(Y) for c in range(C)] for z in range(Z)]
+X = 4
+X_GROUPS = [[h * X + x for x in range(X)] for h in range(2)]
+H_SWAP = [(i, (i + X) % (2 * X)) for i in range(2 * X)]
 LINES = [[at(y, z, c) for z in range(Z)] for y in range(Y) for c in range(C)]
 COLUMNS = [
     [at(y, z + 4 * k, c) for k in range(Z // 4)]
@@ -59,16 +63,17 @@
 
 def tile_first(place, tile):
     half = TILES // 2
-    low = place[4] + 8 * tile
-    high = place[5] + 8 * (tile - half)
+    low = place[4] + 4 * BLOCKS * tile
+    high = place[5] + 4 * BLOCKS * (tile - half)
     return jnp.where(tile < half, low, high) * ROWS
 
 
 def tile_slots(place, tile):
     half = TILES // 2
     residue = jnp.where(tile < half, place[11], 1 - place[11]) - place[12] + Z
-    within = lax.rem(tile, half)
-    return place[13 + lax.rem(residue, 4)] + within, place[13 + lax.rem(residue + 2, 4)] + within
+    within = lax.rem(tile, half) * (BLOCKS // 2)
+    bases = [place[13 + lax.rem(residue + 2 * i, 4)] for i in range(2)]
+    return [bases[i % 2] + within + i // 2 for i in range(BLOCKS)]
 
 
 def slot_rows(slot):
@@ -96,7 +101,7 @@
 def tile_state(place, j, tile):
     query_first = place[j] * ROWS
     key_first = tile_first(place, tile)
-    key_last = key_first + 5 * ROWS - 1
+    key_last = key_first + (4 * BLOCKS - 3) * ROWS - 1
     active = (key_first < query_first + ROWS) & (
         key_last >= doc_start(place, query_first)
     )
@@ -105,7 +110,7 @@
 
 def tile_mask(place, query_first, key_first):
     row = lax.broadcasted_iota(jnp.int32, (TILE, ROWS), 0)
-    key_position = key_first + row + jnp.where(row >= ROWS, 3 * ROWS, 0)
+    key_position = key_first + row + row // ROWS * (3 * ROWS)
     query_position = query_first + lax.broadcasted_iota(jnp.int32, (TILE, ROWS), 1)
     begin = doc_start(place, query_position)
     return (key_position <= query_position) & (key_position >= begin)
@@ -126,9 +131,10 @@
             @pl.when(active)
             def _():
                 mask = tile_mask(place, query_first, key_first)
-                one, two = (slot_rows(slot) for slot in tile_slots(place, tile))
-                keys = jnp.concatenate([kv[one, :HD], kv[two, :HD]], axis=0)
-                values = jnp.concatenate([kv[one, HD:], kv[two, HD:]], axis=0)
+                slots = tile_slots(place, tile)
+                spans = [slot_rows(slot) for slot in slots]
+                keys = jnp.concatenate([kv[rows, :HD] for rows in spans], axis=0)
+                values = jnp.concatenate([kv[rows, HD:] for rows in spans], axis=0)
                 for pair in range(GROUP // 2):
                     span = pl.ds(pair * 2 * ROWS, 2 * ROWS)
                     grad_span = pl.ds((GROUP + pair * 2) * ROWS, 2 * ROWS)
@@ -198,9 +204,10 @@
             @pl.when(active)
             def _():
                 mask = tile_mask(place, query_first, key_first)
-                one, two = (slot_rows(slot) for slot in tile_slots(place, tile))
-                keys = jnp.concatenate([kv[one, :HD], kv[two, :HD]], axis=0)
-                values = jnp.concatenate([kv[one, HD:], kv[two, HD:]], axis=0)
+                slots = tile_slots(place, tile)
+                spans = [slot_rows(slot) for slot in slots]
+                keys = jnp.concatenate([kv[rows, :HD] for rows in spans], axis=0)
+                values = jnp.concatenate([kv[rows, HD:] for rows in spans], axis=0)
                 for pair in range(GROUP // 2):
                     span = pl.ds(pair * 2 * ROWS, 2 * ROWS)
                     grad_span = pl.ds((GROUP + pair * 2) * ROWS, 2 * ROWS)
@@ -216,12 +223,11 @@
                         d = p * (grads[:, lanes] - delta[j, pl.ds(head, 1), :])
                         grad_scores[:, whole] = d.astype(jnp.bfloat16)
                 weights = grad_scores[...]
-                slots = tile_slots(place, tile)
-                keys_t = jnp.concatenate([kt[slots[0]], kt[slots[1]]], axis=1)
+                keys_t = jnp.concatenate([kt[slot] for slot in slots], axis=1)
                 dqt[...] += dot(keys_t, weights, NN)
                 key_term = dot(weights, qd[j, pl.ds(0, GROUP * ROWS), :], NN)
                 value_term = dot(probs[...], qd[j, pl.ds(GROUP * ROWS, GROUP * ROWS), :], NN)
-                for i, rows in enumerate((one, two)):
+                for i, rows in enumerate(spans):
                     dkv_sum[rows, :HD] += key_term[i * ROWS : (i + 1) * ROWS]
                     dkv_sum[rows, HD:] += value_term[i * ROWS : (i + 1) * ROWS]
 
@@ -283,8 +289,14 @@
         out[(GROUP + head) * ROWS : (GROUP + head + 1) * ROWS] = weighted.astype(jnp.bfloat16)
 
 
-def weight_kernel(place, inputs, grads, kept, sent):
-    total = dot(grads[...], inputs[...], TN)
+def finish_kernel(place, parts, inputs, weight, key_grad, kept, sent, terms):
+    summed = parts[0].astype(jnp.float32)
+    for i in range(1, parts.shape[0]):
+        summed += parts[i].astype(jnp.float32)
+    summed = summed.astype(jnp.bfloat16)
+    key_grad[...] = summed[:, :HD]
+    value_grad = summed[:, HD:]
+    total = dot(value_grad, inputs[...], TN)
     width = kept.shape[1]
     first = place[10] == 0
     for i in range(kept.shape[0]):
@@ -292,6 +304,11 @@
         low, high = turned[:width], turned[width:]
         kept[i] = jnp.where(first, low, high).astype(jnp.bfloat16)
         sent[i] = jnp.where(first, high, low).astype(jnp.bfloat16)
+    across, lines, _, span = terms.shape
+    for x in range(across):
+        for h in range(lines):
+            rows = slice((h * across + x) * span, (h * across + x + 1) * span)
+            terms[x, h] = dot(value_grad, weight[rows, :], NT).astype(jnp.bfloat16)
 
 
 def on_device(
@@ -384,44 +401,38 @@
     )(place, all_stats, *operands)
 
     back = [along_z(part, d) for part, d in zip(sums[1:], (-1, 1, -2, 2))]
-    back[2], dq_core = lax.optimization_barrier((back[2], dq_core))
-    from_core = lax.ppermute(dq_core, "ctx", C_SWAP)
     last = jnp.concatenate(back[2:], axis=0)
     column = sums[0].astype(f32) + back[0].astype(f32) + back[1].astype(f32) + last.astype(f32)
-    column, from_core = lax.optimization_barrier((column.astype(bf16), from_core))
-    from_core = from_core.astype(f32)
-    for_across = (dq[1].astype(f32) + from_core[1]).astype(bf16)
-    from_across = lax.ppermute(for_across, "ctx", Y_SWAP).astype(f32)
-    query_grad = (dq[0].astype(f32) + from_core[0] + from_across).astype(bf16)
-    column = lax.all_to_all(column, "ctx", 0, 0, axis_index_groups=COLUMNS)
-    summed = jnp.sum(column.astype(f32), axis=0).astype(bf16)
-    key_grad = summed[:, :HD]
-    value_grad = summed[:, HD:]
-
-    mp_count = lax.axis_size("mp")
-    width = value_weight.shape[0] // mp_count
-    input_terms = jnp.einsum(
-        "td,med->mte",
-        value_grad,
-        value_weight.reshape(mp_count, width, HD),
-        preferred_element_type=f32,
-    ).astype(bf16)
-    input_parts = lax.all_to_all(input_terms, "mp", 0, 0)
-    input_grad = jnp.sum(input_parts.astype(f32), axis=0).astype(bf16)
-
+    column = lax.all_to_all(column.astype(bf16), "ctx", 0, 0, axis_index_groups=COLUMNS)
     piece = sublayer_input.shape[1] // (Y * Z * C)
-    kept, sent = pl.pallas_call(
-        weight_kernel,
-        out_shape=[jax.ShapeDtypeStruct((Y * Z, piece, HD), bf16)] * C,
-        in_specs=[smem, vmem, vmem],
-        out_specs=[vmem] * C,
+    width = value_weight.shape[0] // (2 * X)
+    key_grad, kept, sent, terms = pl.pallas_call(
+        finish_kernel,
+        out_shape=[
+            jax.ShapeDtypeStruct((ROWS, HD), bf16),
+            jax.ShapeDtypeStruct((Y * Z, piece, HD), bf16),
+            jax.ShapeDtypeStruct((Y * Z, piece, HD), bf16),
+            jax.ShapeDtypeStruct((X, 2, ROWS, width), bf16),
+        ],
+        in_specs=[smem] + [vmem] * 3,
+        out_specs=[vmem] * 4,
         compiler_params=params,
-    )(place, sublayer_input, value_grad)
+    )(place, column, sublayer_input, value_weight)
+    terms = lax.all_to_all(terms, "mp", 0, 0, axis_index_groups=X_GROUPS)
+    terms = jnp.sum(terms.astype(f32), axis=0)
+    upper = lax.axis_index("mp") // X == 1
+    other = jnp.where(upper, terms[0], terms[1]).astype(bf16)
+    other = lax.ppermute(other, "mp", H_SWAP).astype(f32)
+    input_grad = (jnp.where(upper, terms[1], terms[0]) + other).astype(bf16)
     near = lax.ppermute(sent, "ctx", C_SWAP)
     term = (kept.astype(f32) + near.astype(f32)).astype(bf16).reshape(Y, Z, piece, HD)
     far = lax.ppermute(jnp.where(mine_y == 0, term[1], term[0]), "ctx", Y_SWAP)
     term = jnp.where(mine_y == 0, term[0], term[1]).astype(f32) + far.astype(f32)
     term = term.astype(bf16)
+    from_core = lax.ppermute(dq_core, "ctx", C_SWAP).astype(f32)
+    for_across = (dq[1].astype(f32) + from_core[1]).astype(bf16)
+    from_across = lax.ppermute(for_across, "ctx", Y_SWAP).astype(f32)
+    query_grad = (dq[0].astype(f32) + from_core[0] + from_across).astype(bf16)
     pieces = lax.all_to_all(term, "ctx", 0, 0, axis_index_groups=LINES)
     value_weight_grad = jnp.sum(pieces.astype(f32), axis=0).astype(bf16)
     return (query_grad, key_grad, input_grad, value_weight_grad)

time: 214 us -> 205 us (0.958)
  waiting for transfers between devices: 65 us -> 52.3 us
  starting transfers between devices: 89.4 us -> 82 us
  blocking collectives: 29.8 us -> 36.1 us
  Pallas kernels: 17.1 us -> 23.3 us
    ppermute x1, waiting for transfers between devices: 15.2 us -> 6.96 us  [on_device(): far = lax.ppermute(jnp.where(mine_y == 0, term[1], term[0]), 'ctx', Y_SWAP)]
    ppermute x8, waiting for transfers between devices: 26.5 us -> 19.4 us  [along_z(): return lax.ppermute(value, 'ctx', pairs)]
    all_to_all x1, blocking collectives: 21.9 us -> 28.3 us  [on_device(): lax.all_to_all(column.astype(bf16), 'ctx', 0, 0, axis_index_groups=COLUMNS)]
    all_to_all x1, waiting for transfers between devices: 0.01 us -> 4.44 us  [on_device(): terms = lax.all_to_all(terms, 'mp', 0, 0, axis_index_groups=X_GROUPS)]
    pallas_call x1, Pallas kernels: 8.65 us -> 12.1 us  [on_device(): pl.pallas_call(grads_kernel, out_shape=[jax.ShapeDtypeStruct((2, ROWS, GR...]
    all_to_all x1, starting transfers between devices: 7.26 us -> 4.31 us  [on_device(): terms = lax.all_to_all(terms, 'mp', 0, 0, axis_index_groups=X_GROUPS)]
    pallas_call x1, Pallas kernels: 4.7 us -> 6.99 us  [on_device(): pl.pallas_call(stats_kernel, out_shape=jax.ShapeDtypeStruct((3, plane, GR...]
    ppermute x1 -> x2, starting transfers between devices: 7.53 us -> 5.59 us  [the longest x1 3.18 us: on_device(): other = lax.ppermute(other, 'mp', H_SWAP).astype(f32)]
  transfers between devices with their start and end apart: 18 -> 19, of which waited for: 9 -> 11; matrix products, arithmetic and copies ran while one was open for 3% -> 3% of each run, Pallas kernels for 0% -> 0%
where the time goes in v3:
time: 205 us; the launch traced here: 204 us
  starting transfers between devices  82 us (40%)
  waiting for transfers between devices  52.3 us (26%)
  blocking collectives  36.1 us (18%)
  Pallas kernels  23.3 us (11%)
  other arithmetic  5.98 us (3%)
  local copies, waits for them, and re-layouts  3.25 us (2%)
    ppermute x8, starting transfers between devices, along_z(): return lax.ppermute(value, 'ctx', pairs)  41.3 us
    all_to_all x1, blocking collectives, on_device(): lax.all_to_all(column.astype(bf16), 'ctx', 0, 0, axis_index_groups=COLUMNS)  28.3 us
    ppermute x8, waiting for transfers between devices, along_z(): return lax.ppermute(value, 'ctx', pairs)  19.4 us
    all_to_all x1, starting transfers between devices, on_device(): column = lax.all_to_all(column, 'ctx', 0, 0, axis_index_groups=COLUMNS)  15.1 us
    pallas_call x1, Pallas kernels, on_device(): pl.pallas_call(grads_kernel, out_shape=[jax.ShapeDtypeStruct((2, ROWS, GR...  12.1 us
    ppermute x1, waiting for transfers between devices, on_device(): across = lax.ppermute(own, 'ctx', Y_SWAP)  10.7 us
    all_gather x1, blocking collectives, on_device(): all_stats = lax.all_gather(stats, 'ctx', axis_index_groups=QUADS)  7.89 us
    pallas_call x1, Pallas kernels, on_device(): pl.pallas_call(stats_kernel, out_shape=jax.ShapeDtypeStruct((3, plane, GR...  6.99 us
  transfers between devices with their start and end apart: 19, of which 11 were waited for; matrix products, arithmetic and copies ran while one was open for 3% of the time, Pallas kernels for 0%

profile of v3, /device:TPU:24, one launch (start us, length us, event | category | flops | bytes accessed | tf_op | source)
XLA Modules:
  0.0 203.9 jit_solution(12850346851841950727)
XLA Ops:
  5.0 15.1 %all-to-all-start = ((bf16[4,128,256]{2,1,0:T(8,128)(2,1)}), bf16[4,128,256]{2,1,0:T(8,128)(2,1)S(1)}, u32[]{:S(2)}, u32[]{:S(2)}) async-start(bf16[4,128,256]{2,1,0:T(8,128)(2,1)} %shard_map.102), calls=%async_computation | async-start | bytes 524288 | tf_op jit(solution)/shard_map/all_to_all | solution.py:339
  20.8 2.7 %collective-permute-start = (bf16[2048,128]{1,0:T(8,128)(2,1)S(1)}, bf16[2048,128]{1,0:T(8,128)(2,1)S(1)}, u32[]{:S(2)}, u32[]{:S(2)}) collective-permute-start(bf16[2048,128]{1,0:T(8,128)(2,1)S(1)} %get-tuple-element.25.refs_0_), channel_id=1, source_target_pairs={{0,256},{8,264},{16,272},{24,280},{32,288},{40,296},{48,304},{56,3... | collective-permute-start | bytes 1572872 | tf_op jit(solution)/shard_map/ppermute | solution.py:357
  25.4 10.7 %collective-permute-done.refs_1_ = bf16[2048,128]{1,0:T(8,128)(2,1)S(1)} collective-permute-done((bf16[2048,128]{1,0:T(8,128)(2,1)S(1)}, bf16[2048,128]{1,0:T(8,128)(2,1)S(1)}, u32[]{:S(2)}, u32[]{:S(2)}) %collective-permute-start) | collective-permute-done | bytes 524320 | tf_op jit(solution)/shard_map/ppermute | solution.py:357
  38.6 5.8 %collective-permute-start.4 = (bf16[4,128,256]{2,1,0:T(8,128)(2,1)S(1)}, bf16[4,128,256]{2,1,0:T(8,128)(2,1)S(1)}, u32[]{:S(2)}, u32[]{:S(2)}) collective-permute-start(bf16[4,128,256]{2,1,0:T(8,128)(2,1)S(1)} %all-to-all-done.refs_4_), channel_id=1, source_target_pairs={{0,496},{8,504},{16,256},{24,264},{32,272},{40,280},{48,288},{56,2... | collective-permute-start | bytes 786440 | tf_op jit(solution)/shard_map/ppermute | solution.py:57
  46.4 5.1 %collective-permute-start.6 = (bf16[2,128,256]{2,1,0:T(8,128)(2,1)S(1)}, bf16[2,128,256]{2,1,0:T(8,128)(2,1)S(1)}, u32[]{:S(2)}, u32[]{:S(2)}) collective-permute-start(bf16[2,128,256]{2,1,0:T(8,128)(2,1)S(1)} %get-tuple-element.40), channel_id=1, source_target_pairs={{0,224},{8,232},{16,240},{24,248},{32,0},{40,8},{48,16},{56,24},{6... | collective-permute-start | bytes 393224 | tf_op jit(solution)/shard_map/ppermute | solution.py:57
  53.4 3.7 %collective-permute-done.6.refs_8_ = bf16[2,128,256]{2,1,0:T(8,128)(2,1)S(1)} collective-permute-done((bf16[2,128,256]{2,1,0:T(8,128)(2,1)S(1)}, bf16[2,128,256]{2,1,0:T(8,128)(2,1)S(1)}, u32[]{:S(2)}, u32[]{:S(2)}) %collective-permute-start.6) | collective-permute-done | bytes 131104 | tf_op jit(solution)/shard_map/ppermute | solution.py:57
  57.1 5.2 %collective-permute-done.5.refs_7_ = bf16[2,128,256]{2,1,0:T(8,128)(2,1)S(1)} collective-permute-done((bf16[2,128,256]{2,1,0:T(8,128)(2,1)S(1)}, bf16[2,128,256]{2,1,0:T(8,128)(2,1)S(1)}, u32[]{:S(2)}, u32[]{:S(2)}) %collective-permute-start.5) | collective-permute-done | bytes 131104 | tf_op jit(solution)/shard_map/ppermute | solution.py:57
  62.3 7.0 %shard_map.104 = f32[3,4,8,128]{3,2,1,0:T(8,128)S(1)} custom-call(s32[17]{0:T(128)S(1)} %get-tuple-element.24.place, bf16[2048,128]{1,0:T(8,128)(2,1)S(1)} %get-tuple-element.25.refs_0_, bf16[2048,128]{1,0:T(8,128)(2,1)S(1)} %collective-permute-done.refs_1_, bf16[2048,128]{1,0:T(8,128)(2,1)S(1)} %collective-permute-done.1.refs_2_, ...), custom_call_target="tpu_custom_call" | custom-call | tf_op jit(solution)/shard_map/pallas_call | solution.py:374
  69.3 7.9 %all-gather = f32[12,4,8,128]{3,2,1,0:T(8,128)S(1)} all-gather(f32[3,4,8,128]{3,2,1,0:T(8,128)S(1)} %shard_map.104), channel_id=2, replica_groups={{0,8,256,264},{16,24,272,280},{32,40,288,296},{48,56,304,312},{64,72,32..., dimensions={0}, use_global_device_ids=true | all-gather | bytes 245760 | tf_op jit(solution)/shard_map/all_gather | solution.py:382
  77.2 12.1 %shard_map.105 = (bf16[2,128,1024]{2,1,0:T(8,128)(2,1)S(1)}, bf16[2,128,1024]{2,1,0:T(8,128)(2,1)S(1)}, bf16[4,128,256]{2,1,0:T(8,128)(2,1)S(1)}, bf16[4,128,256...) custom-call(s32[17]{0:T(128)S(1)} %get-tuple-element.24.place, ...), custom_call_target="tpu_custom_call" | custom-call | tf_op jit(solution)/shard_map/pallas_call | solution.py:383
  89.3 3.5 %collective-permute-start.9 = (bf16[4,128,256]{2,1,0:T(8,128)(2,1)S(1)}, bf16[4,128,256]{2,1,0:T(8,128)(2,1)S(1)}, u32[]{:S(2)}, u32[]{:S(2)}) collective-permute-start(bf16[4,128,256]{2,1,0:T(8,128)(2,1)S(1)} %get-tuple-element.32), channel_id=1, source_target_pairs={{0,496},{8,504},{16,256},{24,264},{32,272},{40,280},{48,288},{56,2... | collective-permute-start | bytes 786440 | tf_op jit(solution)/shard_map/ppermute | solution.py:57
  92.9 6.6 %collective-permute-start.10 = (bf16[4,128,256]{2,1,0:T(8,128)(2,1)S(1)}, bf16[4,128,256]{2,1,0:T(8,128)(2,1)S(1)}, u32[]{:S(2)}, u32[]{:S(2)}) collective-permute-start(bf16[4,128,256]{2,1,0:T(8,128)(2,1)S(1)} %get-tuple-element.33), channel_id=1, source_target_pairs={{0,272},{8,280},{16,288},{24,296},{32,304},{40,312},{48,320},{56,3... | collective-permute-start | bytes 786440 | tf_op jit(solution)/shard_map/ppermute | solution.py:57
  99.5 14.5 %collective-permute-start.11 = (bf16[2,128,256]{2,1,0:T(8,128)(2,1)S(1)}, bf16[2,128,256]{2,1,0:T(8,128)(2,1)S(1)}, u32[]{:S(2)}, u32[]{:S(2)}) collective-permute-start(bf16[2,128,256]{2,1,0:T(8,128)(2,1)S(1)} %get-tuple-element.34), channel_id=1, source_target_pairs={{0,224},{8,232},{16,240},{24,248},{32,0},{40,8},{48,16},{56,24},{6... | collective-permute-start | bytes 393224 | tf_op jit(solution)/shard_map/ppermute | solution.py:57
  116.9 9.5 %collective-permute-done.12 = bf16[2,128,256]{2,1,0:T(8,128)(2,1)S(1)} collective-permute-done((bf16[2,128,256]{2,1,0:T(8,128)(2,1)S(1)}, bf16[2,128,256]{2,1,0:T(8,128)(2,1)S(1)}, u32[]{:S(2)}, u32[]{:S(2)}) %collective-permute-start.12) | collective-permute-done | bytes 131104 | tf_op jit(solution)/shard_map/ppermute | solution.py:57
  126.5 28.3 %all_to_all.20.parts = bf16[4,128,256]{2,1,0:T(8,128)(2,1)S(1)} all-to-all(bf16[4,128,256]{2,1,0:T(8,128)(2,1)S(1)} %add_convert_fusion.2), channel_id=1, replica_groups={{0,64,128,192},{8,72,136,200},{16,80,144,208},{24,88,152,216},{32,96,16..., dimensions={0} | all-to-all | bytes 524288 | tf_op jit(solution)/shard_map/all_to_all | solution.py:406
  154.8 2.3 %shard_map.106 = (bf16[128,128]{1,0:T(8,128)(2,1)}, bf16[32,64,128]{2,1,0:T(8,128)(2,1)S(1)}, bf16[32,64,128]{2,1,0:T(8,128)(2,1)S(1)}, bf16[4,2,128,512]{3,2,1,0:T(8,128)(2,1)}) custom-call(s32[17]{0:T(128)S(1)} %get-tuple-element.24.place, bf16[4,128,256]{2,1,0:T(8,128)(2,1)S(1)} %all_to_all.20.parts, bf16[128,4096]{1,0:T(8,128)(2,1)S(1)} %copy-done.1, ...), custom_call_target="tpu_custom_call" | custom-call | tf_op jit(solution)/shard_map/pallas_call | solution.py:409
  159.0 2.4 %collective-permute-start.7 = (bf16[2,128,1024]{2,1,0:T(8,128)(2,1)S(1)}, bf16[2,128,1024]{2,1,0:T(8,128)(2,1)}, u32[]{:S(2)}, u32[]{:S(2)}) collective-permute-start(bf16[2,128,1024]{2,1,0:T(8,128)(2,1)S(1)} %get-tuple-element.30), channel_id=1, source_target_pairs={{0,8},{8,0},{16,24},{24,16},{32,40},{40,32},{48,56},{56,48},{64,72... | collective-permute-start | bytes 1572872 | tf_op jit(solution)/shard_map/ppermute | solution.py:432
  161.4 4.3 %all-to-all-start.2 = ((bf16[4,2,128,512]{3,2,1,0:T(8,128)(2,1)}), bf16[4,2,128,512]{3,2,1,0:T(8,128)(2,1)}, u32[]{:S(2)}, u32[]{:S(2)}) async-start(bf16[4,2,128,512]{3,2,1,0:T(8,128)(2,1)} %get-tuple-element.37), calls=%async_computation.2 | async-start | bytes 2097152 | tf_op jit(solution)/shard_map/all_to_all | solution.py:421
  169.1 7.0 %collective-permute-done.15 = bf16[16,64,128]{2,1,0:T(8,128)(2,1)S(1)} collective-permute-done((bf16[16,64,128]{2,1,0:T(8,128)(2,1)S(1)}, bf16[16,64,128]{2,1,0:T(8,128)(2,1)S(1)}, u32[]{:S(2)}, u32[]{:S(2)}) %collective-permute-start.15) | collective-permute-done | bytes 262176 | tf_op jit(solution)/shard_map/ppermute | solution.py:429
  176.9 4.4 %all-to-all-done.2 = bf16[4,2,128,512]{3,2,1,0:T(8,128)(2,1)} async-done(((bf16[4,2,128,512]{3,2,1,0:T(8,128)(2,1)}), bf16[4,2,128,512]{3,2,1,0:T(8,128)(2,1)}, u32[]{:S(2)}, u32[]{:S(2)}) %all-to-all-start.2) | async-done | bytes 1048608 | tf_op jit(solution)/shard_map/all_to_all | solution.py:421
  181.3 3.5 %all-to-all-start.3 = ((bf16[16,64,128]{2,1,0:T(8,128)(2,1)}), bf16[16,64,128]{2,1,0:T(8,128)(2,1)S(1)}, u32[]{:S(2)}, u32[]{:S(2)}) async-start(bf16[16,64,128]{2,1,0:T(8,128)(2,1)} %add_convert_fusion.1), calls=%async_computation.3 | async-start | bytes 524288 | tf_op jit(solution)/shard_map/all_to_all | solution.py:436
  188.3 3.2 %collective-permute-start.13 = (bf16[128,512]{1,0:T(8,128)(2,1)S(1)}, bf16[128,512]{1,0:T(8,128)(2,1)S(1)}, u32[]{:S(2)}, u32[]{:S(2)}) collective-permute-start(bf16[128,512]{1,0:T(8,128)(2,1)S(1)} %fusion.6), channel_id=1, source_target_pairs={{0,4},{1,5},{2,6},{3,7},{4,0},{5,1},{6,2},{7,3},{8,12},{9,13},{10,... | collective-permute-start | bytes 393224 | tf_op jit(solution)/shard_map/ppermute | solution.py:425
  191.5 4.0 %collective-permute-done.8 = bf16[128,1024]{1,0:T(8,128)(2,1)S(1)} collective-permute-done((bf16[128,1024]{1,0:T(8,128)(2,1)S(1)}, bf16[128,1024]{1,0:T(8,128)(2,1)S(1)}, u32[]{:S(2)}, u32[]{:S(2)}) %collective-permute-start.8) | collective-permute-done | bytes 262176 | tf_op jit(solution)/shard_map/ppermute | solution.py:434
  197.4 5.8 %all-to-all-done.3 = bf16[16,64,128]{2,1,0:T(8,128)(2,1)S(1)} async-done(((bf16[16,64,128]{2,1,0:T(8,128)(2,1)}), bf16[16,64,128]{2,1,0:T(8,128)(2,1)S(1)}, u32[]{:S(2)}, u32[]{:S(2)}) %all-to-all-start.3) | async-done | bytes 262176 | tf_op jit(solution)/shard_map/all_to_all | solution.py:436
  (51 shorter events, 28.5 us)
Async XLA Ops:
  3.8 16.2 %copy-start.5 = (bf16[128,1024]{1,0:T(8,128)(2,1)S(1)}, bf16[128,1024]{1,0:T(8,128)(2,1)}, u32[]{:S(2)}) copy-start(bf16[128,1024]{1,0:T(8,128)(2,1)} %grads) | copy-start | bytes 786436
  3.8 16.2 %copy-start.7 = (s32[8192]{0:T(1024)S(1)}, s32[8192]{0:T(1024)}, u32[]{:S(2)}) copy-start(s32[8192]{0:T(1024)} %param.12) | copy-start | bytes 98308
  3.9 16.2 %copy-start.8 = (s32[128]{0:T(128)S(1)}, s32[128]{0:T(128)}, u32[]{:S(2)}) copy-start(s32[128]{0:T(128)} %param.13) | copy-start | bytes 1540
  5.0 33.7 %all-to-all-start = ((bf16[4,128,256]{2,1,0:T(8,128)(2,1)}), bf16[4,128,256]{2,1,0:T(8,128)(2,1)S(1)}, u32[]{:S(2)}, u32[]{:S(2)}) async-start(bf16[4,128,256]{2,1,0:T(8,128)(2,1)} %shard_map.102), calls=%async_computation | async-start | bytes 524288 | tf_op jit(solution)/shard_map/all_to_all | solution.py:339
  20.8 15.3 %collective-permute-start = (bf16[2048,128]{1,0:T(8,128)(2,1)S(1)}, bf16[2048,128]{1,0:T(8,128)(2,1)S(1)}, u32[]{:S(2)}, u32[]{:S(2)}) collective-permute-start(bf16[2048,128]{1,0:T(8,128)(2,1)S(1)} %get-tuple-element.25.refs_0_), channel_id=1, source_target_pairs={{0,256},{8,264},{16,272},{24,280},{32,288},{40,296},{48,304},{56,3... | collective-permute-start | bytes 1572872 | tf_op jit(solution)/shard_map/ppermute | solution.py:357
  23.5 14.5 %collective-permute-start.1 = (bf16[2048,128]{1,0:T(8,128)(2,1)S(1)}, bf16[2048,128]{1,0:T(8,128)(2,1)S(1)}, u32[]{:S(2)}, u32[]{:S(2)}) collective-permute-start(bf16[2048,128]{1,0:T(8,128)(2,1)S(1)} %get-tuple-element.25.refs_0_), channel_id=1, source_target_pairs={{0,8},{8,0},{16,24},{24,16},{32,40},{40,32},{48,56},{56,48},{64,72... | collective-permute-start | bytes 1572872 | tf_op jit(solution)/shard_map/ppermute | solution.py:358
  36.1 26.2 %collective-permute-start.2 = (bf16[2048,128]{1,0:T(8,128)(2,1)S(1)}, bf16[2048,128]{1,0:T(8,128)(2,1)S(1)}, u32[]{:S(2)}, u32[]{:S(2)}) collective-permute-start(bf16[2048,128]{1,0:T(8,128)(2,1)S(1)} %collective-permute-done.refs_1_), channel_id=1, source_target_pairs={{0,8},{8,0},{16,24},{24,16},{32,40},{40,32},{48,56},{56,48},{64,72... | collective-permute-start | bytes 1572872 | tf_op jit(solution)/shard_map/ppermute | solution.py:368
  38.6 23.7 %collective-permute-start.4 = (bf16[4,128,256]{2,1,0:T(8,128)(2,1)S(1)}, bf16[4,128,256]{2,1,0:T(8,128)(2,1)S(1)}, u32[]{:S(2)}, u32[]{:S(2)}) collective-permute-start(bf16[4,128,256]{2,1,0:T(8,128)(2,1)S(1)} %all-to-all-done.refs_4_), channel_id=1, source_target_pairs={{0,496},{8,504},{16,256},{24,264},{32,272},{40,280},{48,288},{56,2... | collective-permute-start | bytes 786440 | tf_op jit(solution)/shard_map/ppermute | solution.py:57
  44.5 17.8 %collective-permute-start.3 = (bf16[4,128,256]{2,1,0:T(8,128)(2,1)S(1)}, bf16[4,128,256]{2,1,0:T(8,128)(2,1)S(1)}, u32[]{:S(2)}, u32[]{:S(2)}) collective-permute-start(bf16[4,128,256]{2,1,0:T(8,128)(2,1)S(1)} %all-to-all-done.refs_4_), channel_id=1, source_target_pairs={{0,272},{8,280},{16,288},{24,296},{32,304},{40,312},{48,320},{56,3... | collective-permute-start | bytes 786440 | tf_op jit(solution)/shard_map/ppermute | solution.py:57
  46.4 10.7 %collective-permute-start.6 = (bf16[2,128,256]{2,1,0:T(8,128)(2,1)S(1)}, bf16[2,128,256]{2,1,0:T(8,128)(2,1)S(1)}, u32[]{:S(2)}, u32[]{:S(2)}) collective-permute-start(bf16[2,128,256]{2,1,0:T(8,128)(2,1)S(1)} %get-tuple-element.40), channel_id=1, source_target_pairs={{0,224},{8,232},{16,240},{24,248},{32,0},{40,8},{48,16},{56,24},{6... | collective-permute-start | bytes 393224 | tf_op jit(solution)/shard_map/ppermute | solution.py:57
  51.5 10.8 %collective-permute-start.5 = (bf16[2,128,256]{2,1,0:T(8,128)(2,1)S(1)}, bf16[2,128,256]{2,1,0:T(8,128)(2,1)S(1)}, u32[]{:S(2)}, u32[]{:S(2)}) collective-permute-start(bf16[2,128,256]{2,1,0:T(8,128)(2,1)S(1)} %get-tuple-element.41), channel_id=1, source_target_pairs={{0,32},{8,40},{16,48},{24,56},{32,64},{40,72},{48,80},{56,88},{64,... | collective-permute-start | bytes 393224 | tf_op jit(solution)/shard_map/ppermute | solution.py:57
  77.2 77.6 %copy-start.3 = (bf16[4096,128]{1,0:T(8,128)(2,1)S(1)}, bf16[4096,128]{1,0:T(8,128)(2,1)}, u32[]{:S(2)}) copy-start(bf16[4096,128]{1,0:T(8,128)(2,1)} %weight.3) | copy-start | bytes 3145732
  89.3 65.5 %copy-start.1 = (bf16[128,4096]{1,0:T(8,128)(2,1)S(1)}, bf16[128,4096]{1,0:T(8,128)(2,1)}, u32[]{:S(2)}) copy-start(bf16[128,4096]{1,0:T(8,128)(2,1)} %inputs.3) | copy-start | bytes 3145732
  89.3 37.1 %collective-permute-start.9 = (bf16[4,128,256]{2,1,0:T(8,128)(2,1)S(1)}, bf16[4,128,256]{2,1,0:T(8,128)(2,1)S(1)}, u32[]{:S(2)}, u32[]{:S(2)}) collective-permute-start(bf16[4,128,256]{2,1,0:T(8,128)(2,1)S(1)} %get-tuple-element.32), channel_id=1, source_target_pairs={{0,496},{8,504},{16,256},{24,264},{32,272},{40,280},{48,288},{56,2... | collective-permute-start | bytes 786440 | tf_op jit(solution)/shard_map/ppermute | solution.py:57
  92.9 33.5 %collective-permute-start.10 = (bf16[4,128,256]{2,1,0:T(8,128)(2,1)S(1)}, bf16[4,128,256]{2,1,0:T(8,128)(2,1)S(1)}, u32[]{:S(2)}, u32[]{:S(2)}) collective-permute-start(bf16[4,128,256]{2,1,0:T(8,128)(2,1)S(1)} %get-tuple-element.33), channel_id=1, source_target_pairs={{0,272},{8,280},{16,288},{24,296},{32,304},{40,312},{48,320},{56,3... | collective-permute-start | bytes 786440 | tf_op jit(solution)/shard_map/ppermute | solution.py:57
  99.5 17.4 %collective-permute-start.11 = (bf16[2,128,256]{2,1,0:T(8,128)(2,1)S(1)}, bf16[2,128,256]{2,1,0:T(8,128)(2,1)S(1)}, u32[]{:S(2)}, u32[]{:S(2)}) collective-permute-start(bf16[2,128,256]{2,1,0:T(8,128)(2,1)S(1)} %get-tuple-element.34), channel_id=1, source_target_pairs={{0,224},{8,232},{16,240},{24,248},{32,0},{40,8},{48,16},{56,24},{6... | collective-permute-start | bytes 393224 | tf_op jit(solution)/shard_map/ppermute | solution.py:57
  113.9 12.4 %collective-permute-start.12 = (bf16[2,128,256]{2,1,0:T(8,128)(2,1)S(1)}, bf16[2,128,256]{2,1,0:T(8,128)(2,1)S(1)}, u32[]{:S(2)}, u32[]{:S(2)}) collective-permute-start(bf16[2,128,256]{2,1,0:T(8,128)(2,1)S(1)} %get-tuple-element.35), channel_id=1, source_target_pairs={{0,32},{8,40},{16,48},{24,56},{32,64},{40,72},{48,80},{56,88},{64,... | collective-permute-start | bytes 393224 | tf_op jit(solution)/shard_map/ppermute | solution.py:57
  157.1 8.7 %collective-permute-start.14 = (bf16[32,64,128]{2,1,0:T(8,128)(2,1)S(1)}, bf16[32,64,128]{2,1,0:T(8,128)(2,1)S(1)}, u32[]{:S(2)}, u32[]{:S(2)}) collective-permute-start(bf16[32,64,128]{2,1,0:T(8,128)(2,1)S(1)} %get-tuple-element.39), channel_id=1, source_target_pairs={{0,8},{8,0},{16,24},{24,16},{32,40},{40,32},{48,56},{56,48},{64,72... | collective-permute-start | bytes 1572872 | tf_op jit(solution)/shard_map/ppermute | solution.py:427
  159.0 8.9 %collective-permute-start.7 = (bf16[2,128,1024]{2,1,0:T(8,128)(2,1)S(1)}, bf16[2,128,1024]{2,1,0:T(8,128)(2,1)}, u32[]{:S(2)}, u32[]{:S(2)}) collective-permute-start(bf16[2,128,1024]{2,1,0:T(8,128)(2,1)S(1)} %get-tuple-element.30), channel_id=1, source_target_pairs={{0,8},{8,0},{16,24},{24,16},{32,40},{40,32},{48,56},{56,48},{64,72... | collective-permute-start | bytes 1572872 | tf_op jit(solution)/shard_map/ppermute | solution.py:432
  161.4 19.9 %all-to-all-start.2 = ((bf16[4,2,128,512]{3,2,1,0:T(8,128)(2,1)}), bf16[4,2,128,512]{3,2,1,0:T(8,128)(2,1)}, u32[]{:S(2)}, u32[]{:S(2)}) async-start(bf16[4,2,128,512]{3,2,1,0:T(8,128)(2,1)} %get-tuple-element.37), calls=%async_computation.2 | async-start | bytes 2097152 | tf_op jit(solution)/shard_map/all_to_all | solution.py:421
  166.0 10.1 %collective-permute-start.15 = (bf16[16,64,128]{2,1,0:T(8,128)(2,1)S(1)}, bf16[16,64,128]{2,1,0:T(8,128)(2,1)S(1)}, u32[]{:S(2)}, u32[]{:S(2)}) collective-permute-start(bf16[16,64,128]{2,1,0:T(8,128)(2,1)S(1)} %broadcast_select_fusion), channel_id=1, source_target_pairs={{0,256},{8,264},{16,272},{24,280},{32,288},{40,296},{48,304},{56,3... | collective-permute-start | bytes 786440 | tf_op jit(solution)/shard_map/ppermute | solution.py:429
  181.3 21.9 %all-to-all-start.3 = ((bf16[16,64,128]{2,1,0:T(8,128)(2,1)}), bf16[16,64,128]{2,1,0:T(8,128)(2,1)S(1)}, u32[]{:S(2)}, u32[]{:S(2)}) async-start(bf16[16,64,128]{2,1,0:T(8,128)(2,1)} %add_convert_fusion.1), calls=%async_computation.3 | async-start | bytes 524288 | tf_op jit(solution)/shard_map/all_to_all | solution.py:436
  184.9 10.6 %collective-permute-start.8 = (bf16[128,1024]{1,0:T(8,128)(2,1)S(1)}, bf16[128,1024]{1,0:T(8,128)(2,1)S(1)}, u32[]{:S(2)}, u32[]{:S(2)}) collective-permute-start(bf16[128,1024]{1,0:T(8,128)(2,1)S(1)} %fusion.4), channel_id=1, source_target_pairs={{0,256},{8,264},{16,272},{24,280},{32,288},{40,296},{48,304},{56,3... | collective-permute-start | bytes 786440 | tf_op jit(solution)/shard_map/ppermute | solution.py:434
  188.3 8.4 %collective-permute-start.13 = (bf16[128,512]{1,0:T(8,128)(2,1)S(1)}, bf16[128,512]{1,0:T(8,128)(2,1)S(1)}, u32[]{:S(2)}, u32[]{:S(2)}) collective-permute-start(bf16[128,512]{1,0:T(8,128)(2,1)S(1)} %fusion.6), channel_id=1, source_target_pairs={{0,4},{1,5},{2,6},{3,7},{4,0},{5,1},{6,2},{7,3},{8,12},{9,13},{10,... | collective-permute-start | bytes 393224 | tf_op jit(solution)/shard_map/ppermute | solution.py:425
  (4 other events, 19.4 us)

commit v4 on v3

--- a/solution.py
+++ b/solution.py
@@ -43,13 +43,14 @@
     for c in range(C)
 ]
 BASES = [0, 8, 12, 4]
-GROUPS = (4, 4, 4, 2, 2)
+GROUPS = (4, 4, 4, 4)
 PARTS = Y * C + len(GROUPS)
 
 
-def along_z(value, distance):
+def along_z(value, distance, other_distance=None):
+    distances = (distance, distance if other_distance is None else other_distance)
     pairs = [
-        (at(y, z, c), at((y + distance) % 2, (z + distance) % Z, c))
+        (at(y, z, c), at((y + distances[c]) % 2, (z + distances[c]) % Z, c))
         for y in range(Y)
         for z in range(Z)
         for c in range(C)
@@ -362,8 +363,7 @@
         column,
         along_z(column, 1),
         along_z(column, -1),
-        along_z(column[:2], 2),
-        along_z(column[2:], -2),
+        along_z(column, 2, -2),
     ]
     corner = lax.ppermute(across, "ctx", C_SWAP)
     operands = [own, across, beside, corner]
@@ -400,9 +400,10 @@
         compiler_params=params,
     )(place, all_stats, *operands)
 
-    back = [along_z(part, d) for part, d in zip(sums[1:], (-1, 1, -2, 2))]
-    last = jnp.concatenate(back[2:], axis=0)
-    column = sums[0].astype(f32) + back[0].astype(f32) + back[1].astype(f32) + last.astype(f32)
+    back = [along_z(sums[1], -1), along_z(sums[2], 1), along_z(sums[3], -2, 2)]
+    column = sums[0].astype(f32)
+    for part in back:
+        column += part.astype(f32)
     column = lax.all_to_all(column.astype(bf16), "ctx", 0, 0, axis_index_groups=COLUMNS)
     piece = sublayer_input.shape[1] // (Y * Z * C)
     width = value_weight.shape[0] // (2 * X)

time: 205 us -> 204 us (level)
  waiting for transfers between devices: 52.3 us -> 46.2 us
  starting transfers between devices: 82 us -> 87.3 us
    ppermute x1, starting transfers between devices: 1.91 us -> 9.02 us  [on_device(): near = lax.ppermute(sent, 'ctx', C_SWAP)]
    ppermute x8 -> x6, waiting for transfers between devices: 19.4 us -> 15.3 us  [along_z(): return lax.ppermute(value, 'ctx', pairs)]
    ppermute x8 -> x6, starting transfers between devices: 41.3 us -> 37.5 us  [along_z(): return lax.ppermute(value, 'ctx', pairs)]
    all_gather x1, blocking collectives: 7.89 us -> 5.61 us  [on_device(): all_stats = lax.all_gather(stats, 'ctx', axis_index_groups=QUADS)]
  transfers between devices with their start and end apart: 19 -> 17, of which waited for: 11 -> 10; matrix products, arithmetic and copies ran while one was open for 3% -> 3% of each run, Pallas kernels for 0% -> 0%
where the time goes in v4:
time: 204 us; the launch traced here: 202 us
  starting transfers between devices  87.3 us (43%)
  waiting for transfers between devices  46.2 us (23%)
  blocking collectives  34.8 us (17%)
  Pallas kernels  23.3 us (11%)
  other arithmetic  5.99 us (3%)
  local copies, waits for them, and re-layouts  3.23 us (2%)
    ppermute x6, starting transfers between devices, along_z(): return lax.ppermute(value, 'ctx', pairs)  37.5 us
    all_to_all x1, blocking collectives, on_device(): lax.all_to_all(column.astype(bf16), 'ctx', 0, 0, axis_index_groups=COLUMNS)  29.2 us
    ppermute x6, waiting for transfers between devices, along_z(): return lax.ppermute(value, 'ctx', pairs)  15.3 us
    all_to_all x1, starting transfers between devices, on_device(): column = lax.all_to_all(column, 'ctx', 0, 0, axis_index_groups=COLUMNS)  15.1 us
    pallas_call x1, Pallas kernels, on_device(): pl.pallas_call(grads_kernel, out_shape=[jax.ShapeDtypeStruct((2, ROWS, GR...  12.1 us
    ppermute x1, waiting for transfers between devices, on_device(): across = lax.ppermute(own, 'ctx', Y_SWAP)  10.7 us
    ppermute x1, starting transfers between devices, on_device(): near = lax.ppermute(sent, 'ctx', C_SWAP)  9.02 us
    pallas_call x1, Pallas kernels, on_device(): pl.pallas_call(stats_kernel, out_shape=jax.ShapeDtypeStruct((3, plane, GR...  6.98 us
  transfers between devices with their start and end apart: 17, of which 10 were waited for; matrix products, arithmetic and copies ran while one was open for 3% of the time, Pallas kernels for 0%

profile of v4, /device:TPU:24, one launch (start us, length us, event | category | flops | bytes accessed | tf_op | source)
XLA Modules:
  0.0 201.8 jit_solution(5945619634809865063)
XLA Ops:
  5.0 15.1 %all-to-all-start = ((bf16[4,128,256]{2,1,0:T(8,128)(2,1)}), bf16[4,128,256]{2,1,0:T(8,128)(2,1)S(1)}, u32[]{:S(2)}, u32[]{:S(2)}) async-start(bf16[4,128,256]{2,1,0:T(8,128)(2,1)} %shard_map.102), calls=%async_computation | async-start | bytes 524288 | tf_op jit(solution)/shard_map/all_to_all | solution.py:340
  25.4 10.7 %collective-permute-done.refs_1_ = bf16[2048,128]{1,0:T(8,128)(2,1)S(1)} collective-permute-done((bf16[2048,128]{1,0:T(8,128)(2,1)S(1)}, bf16[2048,128]{1,0:T(8,128)(2,1)S(1)}, u32[]{:S(2)}, u32[]{:S(2)}) %collective-permute-start) | collective-permute-done | bytes 524320 | tf_op jit(solution)/shard_map/ppermute | solution.py:358
  38.6 5.8 %collective-permute-start.5 = (bf16[4,128,256]{2,1,0:T(8,128)(2,1)S(1)}, bf16[4,128,256]{2,1,0:T(8,128)(2,1)S(1)}, u32[]{:S(2)}, u32[]{:S(2)}) collective-permute-start(bf16[4,128,256]{2,1,0:T(8,128)(2,1)S(1)} %all-to-all-done.refs_4_), channel_id=1, source_target_pairs={{0,32},{8,232},{16,48},{24,248},{32,64},{40,8},{48,80},{56,24},{64... | collective-permute-start | bytes 786440 | tf_op jit(solution)/shard_map/ppermute | solution.py:58
  44.4 4.3 %collective-permute-start.4 = (bf16[4,128,256]{2,1,0:T(8,128)(2,1)S(1)}, bf16[4,128,256]{2,1,0:T(8,128)(2,1)S(1)}, u32[]{:S(2)}, u32[]{:S(2)}) collective-permute-start(bf16[4,128,256]{2,1,0:T(8,128)(2,1)S(1)} %all-to-all-done.refs_4_), channel_id=1, source_target_pairs={{0,496},{8,504},{16,256},{24,264},{32,272},{40,280},{48,288},{56,2... | collective-permute-start | bytes 786440 | tf_op jit(solution)/shard_map/ppermute | solution.py:58
  51.2 8.0 %collective-permute-done.4.refs_6_ = bf16[4,128,256]{2,1,0:T(8,128)(2,1)S(1)} collective-permute-done((bf16[4,128,256]{2,1,0:T(8,128)(2,1)S(1)}, bf16[4,128,256]{2,1,0:T(8,128)(2,1)S(1)}, u32[]{:S(2)}, u32[]{:S(2)}) %collective-permute-start.4) | collective-permute-done | bytes 262176 | tf_op jit(solution)/shard_map/ppermute | solution.py:58
  59.2 3.5 %collective-permute-done.3.refs_5_ = bf16[4,128,256]{2,1,0:T(8,128)(2,1)S(1)} collective-permute-done((bf16[4,128,256]{2,1,0:T(8,128)(2,1)S(1)}, bf16[4,128,256]{2,1,0:T(8,128)(2,1)S(1)}, u32[]{:S(2)}, u32[]{:S(2)}) %collective-permute-start.3) | collective-permute-done | bytes 262176 | tf_op jit(solution)/shard_map/ppermute | solution.py:58
  62.7 7.0 %shard_map.104 = f32[3,4,8,128]{3,2,1,0:T(8,128)S(1)} custom-call(s32[17]{0:T(128)S(1)} %get-tuple-element.23.place, bf16[2048,128]{1,0:T(8,128)(2,1)S(1)} %get-tuple-element.24.refs_0_, bf16[2048,128]{1,0:T(8,128)(2,1)S(1)} %collective-permute-done.refs_1_, bf16[2048,128]{1,0:T(8,128)(2,1)S(1)} %collective-permute-done.1.refs_2_, ...), custom_call_target="tpu_custom_call" | custom-call | tf_op jit(solution)/shard_map/pallas_call | solution.py:374
  69.6 5.6 %all-gather = f32[12,4,8,128]{3,2,1,0:T(8,128)S(1)} all-gather(f32[3,4,8,128]{3,2,1,0:T(8,128)S(1)} %shard_map.104), channel_id=2, replica_groups={{0,8,256,264},{16,24,272,280},{32,40,288,296},{48,56,304,312},{64,72,32..., dimensions={0}, use_global_device_ids=true | all-gather | bytes 245760 | tf_op jit(solution)/shard_map/all_gather | solution.py:382
  75.3 12.1 %shard_map.105 = (bf16[2,128,1024]{2,1,0:T(8,128)(2,1)S(1)}, bf16[2,128,1024]{2,1,0:T(8,128)(2,1)S(1)}, bf16[4,128,256]{2,1,0:T(8,128)(2,1)S(1)}, bf16[4,128,256...) custom-call(s32[17]{0:T(128)S(1)} %get-tuple-element.23.place, ...), custom_call_target="tpu_custom_call" | custom-call | tf_op jit(solution)/shard_map/pallas_call | solution.py:383
  87.4 5.1 %collective-permute-start.8 = (bf16[4,128,256]{2,1,0:T(8,128)(2,1)S(1)}, bf16[4,128,256]{2,1,0:T(8,128)(2,1)S(1)}, u32[]{:S(2)}, u32[]{:S(2)}) collective-permute-start(bf16[4,128,256]{2,1,0:T(8,128)(2,1)S(1)} %get-tuple-element.31), channel_id=1, source_target_pairs={{0,496},{8,504},{16,256},{24,264},{32,272},{40,280},{48,288},{56,2... | collective-permute-start | bytes 786440 | tf_op jit(solution)/shard_map/ppermute | solution.py:58
  92.5 3.7 %collective-permute-start.9 = (bf16[4,128,256]{2,1,0:T(8,128)(2,1)S(1)}, bf16[4,128,256]{2,1,0:T(8,128)(2,1)S(1)}, u32[]{:S(2)}, u32[]{:S(2)}) collective-permute-start(bf16[4,128,256]{2,1,0:T(8,128)(2,1)S(1)} %get-tuple-element.32), channel_id=1, source_target_pairs={{0,272},{8,280},{16,288},{24,296},{32,304},{40,312},{48,320},{56,3... | collective-permute-start | bytes 786440 | tf_op jit(solution)/shard_map/ppermute | solution.py:58
  96.2 16.2 %collective-permute-start.10 = (bf16[4,128,256]{2,1,0:T(8,128)(2,1)S(1)}, bf16[4,128,256]{2,1,0:T(8,128)(2,1)S(1)}, u32[]{:S(2)}, u32[]{:S(2)}) collective-permute-start(bf16[4,128,256]{2,1,0:T(8,128)(2,1)S(1)} %get-tuple-element.33), channel_id=1, source_target_pairs={{0,224},{8,40},{16,240},{24,56},{32,0},{40,72},{48,16},{56,88},{64... | collective-permute-start | bytes 786440 | tf_op jit(solution)/shard_map/ppermute | solution.py:58
  112.5 3.8 %collective-permute-done.10 = bf16[4,128,256]{2,1,0:T(8,128)(2,1)S(1)} collective-permute-done((bf16[4,128,256]{2,1,0:T(8,128)(2,1)S(1)}, bf16[4,128,256]{2,1,0:T(8,128)(2,1)S(1)}, u32[]{:S(2)}, u32[]{:S(2)}) %collective-permute-start.10) | collective-permute-done | bytes 262176 | tf_op jit(solution)/shard_map/ppermute | solution.py:58
  116.4 29.2 %all_to_all.20.parts = bf16[4,128,256]{2,1,0:T(8,128)(2,1)S(1)} all-to-all(bf16[4,128,256]{2,1,0:T(8,128)(2,1)S(1)} %add_convert_fusion.2), channel_id=1, replica_groups={{0,64,128,192},{8,72,136,200},{16,80,144,208},{24,88,152,216},{32,96,16..., dimensions={0} | all-to-all | bytes 524288 | tf_op jit(solution)/shard_map/all_to_all | solution.py:407
  147.9 9.0 %collective-permute-start.12 = (bf16[32,64,128]{2,1,0:T(8,128)(2,1)S(1)}, bf16[32,64,128]{2,1,0:T(8,128)(2,1)S(1)}, u32[]{:S(2)}, u32[]{:S(2)}) collective-permute-start(bf16[32,64,128]{2,1,0:T(8,128)(2,1)S(1)} %get-tuple-element.37), channel_id=1, source_target_pairs={{0,8},{8,0},{16,24},{24,16},{32,40},{40,32},{48,56},{56,48},{64,72... | collective-permute-start | bytes 1572872 | tf_op jit(solution)/shard_map/ppermute | solution.py:428
  158.9 4.3 %all-to-all-start.2 = ((bf16[4,2,128,512]{3,2,1,0:T(8,128)(2,1)}), bf16[4,2,128,512]{3,2,1,0:T(8,128)(2,1)}, u32[]{:S(2)}, u32[]{:S(2)}) async-start(bf16[4,2,128,512]{3,2,1,0:T(8,128)(2,1)} %get-tuple-element.35), calls=%async_computation.2 | async-start | bytes 2097152 | tf_op jit(solution)/shard_map/all_to_all | solution.py:422
  163.4 3.2 %collective-permute-start.13 = (bf16[16,64,128]{2,1,0:T(8,128)(2,1)S(1)}, bf16[16,64,128]{2,1,0:T(8,128)(2,1)S(1)}, u32[]{:S(2)}, u32[]{:S(2)}) collective-permute-start(bf16[16,64,128]{2,1,0:T(8,128)(2,1)S(1)} %broadcast_select_fusion), channel_id=1, source_target_pairs={{0,256},{8,264},{16,272},{24,280},{32,288},{40,296},{48,304},{56,3... | collective-permute-start | bytes 786440 | tf_op jit(solution)/shard_map/ppermute | solution.py:430
  167.8 6.2 %collective-permute-done.13 = bf16[16,64,128]{2,1,0:T(8,128)(2,1)S(1)} collective-permute-done((bf16[16,64,128]{2,1,0:T(8,128)(2,1)S(1)}, bf16[16,64,128]{2,1,0:T(8,128)(2,1)S(1)}, u32[]{:S(2)}, u32[]{:S(2)}) %collective-permute-start.13) | collective-permute-done | bytes 262176 | tf_op jit(solution)/shard_map/ppermute | solution.py:430
  174.8 4.4 %all-to-all-done.2 = bf16[4,2,128,512]{3,2,1,0:T(8,128)(2,1)} async-done(((bf16[4,2,128,512]{3,2,1,0:T(8,128)(2,1)}), bf16[4,2,128,512]{3,2,1,0:T(8,128)(2,1)}, u32[]{:S(2)}, u32[]{:S(2)}) %all-to-all-start.2) | async-done | bytes 1048608 | tf_op jit(solution)/shard_map/all_to_all | solution.py:422
  179.3 3.5 %all-to-all-start.3 = ((bf16[16,64,128]{2,1,0:T(8,128)(2,1)}), bf16[16,64,128]{2,1,0:T(8,128)(2,1)S(1)}, u32[]{:S(2)}, u32[]{:S(2)}) async-start(bf16[16,64,128]{2,1,0:T(8,128)(2,1)} %add_convert_fusion.1), calls=%async_computation.3 | async-start | bytes 524288 | tf_op jit(solution)/shard_map/all_to_all | solution.py:437
  182.9 3.2 %collective-permute-start.7 = (bf16[128,1024]{1,0:T(8,128)(2,1)S(1)}, bf16[128,1024]{1,0:T(8,128)(2,1)S(1)}, u32[]{:S(2)}, u32[]{:S(2)}) collective-permute-start(bf16[128,1024]{1,0:T(8,128)(2,1)S(1)} %fusion.4), channel_id=1, source_target_pairs={{0,256},{8,264},{16,272},{24,280},{32,288},{40,296},{48,304},{56,3... | collective-permute-start | bytes 786440 | tf_op jit(solution)/shard_map/ppermute | solution.py:435
  187.5 3.1 %collective-permute-start.11 = (bf16[128,512]{1,0:T(8,128)(2,1)S(1)}, bf16[128,512]{1,0:T(8,128)(2,1)S(1)}, u32[]{:S(2)}, u32[]{:S(2)}) collective-permute-start(bf16[128,512]{1,0:T(8,128)(2,1)S(1)} %fusion.6), channel_id=1, source_target_pairs={{0,4},{1,5},{2,6},{3,7},{4,0},{5,1},{6,2},{7,3},{8,12},{9,13},{10,... | collective-permute-start | bytes 393224 | tf_op jit(solution)/shard_map/ppermute | solution.py:426
  190.6 3.4 %collective-permute-done.7 = bf16[128,1024]{1,0:T(8,128)(2,1)S(1)} collective-permute-done((bf16[128,1024]{1,0:T(8,128)(2,1)S(1)}, bf16[128,1024]{1,0:T(8,128)(2,1)S(1)}, u32[]{:S(2)}, u32[]{:S(2)}) %collective-permute-start.7) | collective-permute-done | bytes 262176 | tf_op jit(solution)/shard_map/ppermute | solution.py:435
  196.6 4.5 %all-to-all-done.3 = bf16[16,64,128]{2,1,0:T(8,128)(2,1)S(1)} async-done(((bf16[16,64,128]{2,1,0:T(8,128)(2,1)}), bf16[16,64,128]{2,1,0:T(8,128)(2,1)S(1)}, u32[]{:S(2)}, u32[]{:S(2)}) %all-to-all-start.3) | async-done | bytes 262176 | tf_op jit(solution)/shard_map/all_to_all | solution.py:437
  (46 shorter events, 26.0 us)
Async XLA Ops:
  0.6 1.2 copy-start
  3.8 16.2 %copy-start.4 = (bf16[128,1024]{1,0:T(8,128)(2,1)S(1)}, bf16[128,1024]{1,0:T(8,128)(2,1)}, u32[]{:S(2)}) copy-start(bf16[128,1024]{1,0:T(8,128)(2,1)} %queries) | copy-start | bytes 786436
  3.8 16.2 %copy-start.5 = (bf16[128,1024]{1,0:T(8,128)(2,1)S(1)}, bf16[128,1024]{1,0:T(8,128)(2,1)}, u32[]{:S(2)}) copy-start(bf16[128,1024]{1,0:T(8,128)(2,1)} %grads) | copy-start | bytes 786436
  3.8 16.2 %copy-start.7 = (s32[8192]{0:T(1024)S(1)}, s32[8192]{0:T(1024)}, u32[]{:S(2)}) copy-start(s32[8192]{0:T(1024)} %param.12) | copy-start | bytes 98308
  3.9 16.2 %copy-start.8 = (s32[128]{0:T(128)S(1)}, s32[128]{0:T(128)}, u32[]{:S(2)}) copy-start(s32[128]{0:T(128)} %param.13) | copy-start | bytes 1540
  5.0 33.7 %all-to-all-start = ((bf16[4,128,256]{2,1,0:T(8,128)(2,1)}), bf16[4,128,256]{2,1,0:T(8,128)(2,1)S(1)}, u32[]{:S(2)}, u32[]{:S(2)}) async-start(bf16[4,128,256]{2,1,0:T(8,128)(2,1)} %shard_map.102), calls=%async_computation | async-start | bytes 524288 | tf_op jit(solution)/shard_map/all_to_all | solution.py:340
  20.8 15.3 %collective-permute-start = (bf16[2048,128]{1,0:T(8,128)(2,1)S(1)}, bf16[2048,128]{1,0:T(8,128)(2,1)S(1)}, u32[]{:S(2)}, u32[]{:S(2)}) collective-permute-start(bf16[2048,128]{1,0:T(8,128)(2,1)S(1)} %get-tuple-element.24.refs_0_), channel_id=1, source_target_pairs={{0,256},{8,264},{16,272},{24,280},{32,288},{40,296},{48,304},{56,3... | collective-permute-start | bytes 1572872 | tf_op jit(solution)/shard_map/ppermute | solution.py:358
  23.5 14.5 %collective-permute-start.1 = (bf16[2048,128]{1,0:T(8,128)(2,1)S(1)}, bf16[2048,128]{1,0:T(8,128)(2,1)S(1)}, u32[]{:S(2)}, u32[]{:S(2)}) collective-permute-start(bf16[2048,128]{1,0:T(8,128)(2,1)S(1)} %get-tuple-element.24.refs_0_), channel_id=1, source_target_pairs={{0,8},{8,0},{16,24},{24,16},{32,40},{40,32},{48,56},{56,48},{64,72... | collective-permute-start | bytes 1572872 | tf_op jit(solution)/shard_map/ppermute | solution.py:359
  36.1 26.5 %collective-permute-start.2 = (bf16[2048,128]{1,0:T(8,128)(2,1)S(1)}, bf16[2048,128]{1,0:T(8,128)(2,1)S(1)}, u32[]{:S(2)}, u32[]{:S(2)}) collective-permute-start(bf16[2048,128]{1,0:T(8,128)(2,1)S(1)} %collective-permute-done.refs_1_), channel_id=1, source_target_pairs={{0,8},{8,0},{16,24},{24,16},{32,40},{40,32},{48,56},{56,48},{64,72... | collective-permute-start | bytes 1572872 | tf_op jit(solution)/shard_map/ppermute | solution.py:368
  38.6 12.5 %collective-permute-start.5 = (bf16[4,128,256]{2,1,0:T(8,128)(2,1)S(1)}, bf16[4,128,256]{2,1,0:T(8,128)(2,1)S(1)}, u32[]{:S(2)}, u32[]{:S(2)}) collective-permute-start(bf16[4,128,256]{2,1,0:T(8,128)(2,1)S(1)} %all-to-all-done.refs_4_), channel_id=1, source_target_pairs={{0,32},{8,232},{16,48},{24,248},{32,64},{40,8},{48,80},{56,24},{64... | collective-permute-start | bytes 786440 | tf_op jit(solution)/shard_map/ppermute | solution.py:58
  44.4 14.8 %collective-permute-start.4 = (bf16[4,128,256]{2,1,0:T(8,128)(2,1)S(1)}, bf16[4,128,256]{2,1,0:T(8,128)(2,1)S(1)}, u32[]{:S(2)}, u32[]{:S(2)}) collective-permute-start(bf16[4,128,256]{2,1,0:T(8,128)(2,1)S(1)} %all-to-all-done.refs_4_), channel_id=1, source_target_pairs={{0,496},{8,504},{16,256},{24,264},{32,272},{40,280},{48,288},{56,2... | collective-permute-start | bytes 786440 | tf_op jit(solution)/shard_map/ppermute | solution.py:58
  48.7 14.0 %collective-permute-start.3 = (bf16[4,128,256]{2,1,0:T(8,128)(2,1)S(1)}, bf16[4,128,256]{2,1,0:T(8,128)(2,1)S(1)}, u32[]{:S(2)}, u32[]{:S(2)}) collective-permute-start(bf16[4,128,256]{2,1,0:T(8,128)(2,1)S(1)} %all-to-all-done.refs_4_), channel_id=1, source_target_pairs={{0,272},{8,280},{16,288},{24,296},{32,304},{40,312},{48,320},{56,3... | collective-permute-start | bytes 786440 | tf_op jit(solution)/shard_map/ppermute | solution.py:58
  75.3 70.3 %copy-start.3 = (bf16[4096,128]{1,0:T(8,128)(2,1)S(1)}, bf16[4096,128]{1,0:T(8,128)(2,1)}, u32[]{:S(2)}) copy-start(bf16[4096,128]{1,0:T(8,128)(2,1)} %weight.3) | copy-start | bytes 3145732
  87.4 58.2 %copy-start.1 = (bf16[128,4096]{1,0:T(8,128)(2,1)S(1)}, bf16[128,4096]{1,0:T(8,128)(2,1)}, u32[]{:S(2)}) copy-start(bf16[128,4096]{1,0:T(8,128)(2,1)} %inputs.3) | copy-start | bytes 3145732
  87.4 25.1 %collective-permute-start.8 = (bf16[4,128,256]{2,1,0:T(8,128)(2,1)S(1)}, bf16[4,128,256]{2,1,0:T(8,128)(2,1)S(1)}, u32[]{:S(2)}, u32[]{:S(2)}) collective-permute-start(bf16[4,128,256]{2,1,0:T(8,128)(2,1)S(1)} %get-tuple-element.31), channel_id=1, source_target_pairs={{0,496},{8,504},{16,256},{24,264},{32,272},{40,280},{48,288},{56,2... | collective-permute-start | bytes 786440 | tf_op jit(solution)/shard_map/ppermute | solution.py:58
  92.5 20.0 %collective-permute-start.9 = (bf16[4,128,256]{2,1,0:T(8,128)(2,1)S(1)}, bf16[4,128,256]{2,1,0:T(8,128)(2,1)S(1)}, u32[]{:S(2)}, u32[]{:S(2)}) collective-permute-start(bf16[4,128,256]{2,1,0:T(8,128)(2,1)S(1)} %get-tuple-element.32), channel_id=1, source_target_pairs={{0,272},{8,280},{16,288},{24,296},{32,304},{40,312},{48,320},{56,3... | collective-permute-start | bytes 786440 | tf_op jit(solution)/shard_map/ppermute | solution.py:58
  96.2 20.1 %collective-permute-start.10 = (bf16[4,128,256]{2,1,0:T(8,128)(2,1)S(1)}, bf16[4,128,256]{2,1,0:T(8,128)(2,1)S(1)}, u32[]{:S(2)}, u32[]{:S(2)}) collective-permute-start(bf16[4,128,256]{2,1,0:T(8,128)(2,1)S(1)} %get-tuple-element.33), channel_id=1, source_target_pairs={{0,224},{8,40},{16,240},{24,56},{32,0},{40,72},{48,16},{56,88},{64... | collective-permute-start | bytes 786440 | tf_op jit(solution)/shard_map/ppermute | solution.py:58
  147.9 15.3 %collective-permute-start.12 = (bf16[32,64,128]{2,1,0:T(8,128)(2,1)S(1)}, bf16[32,64,128]{2,1,0:T(8,128)(2,1)S(1)}, u32[]{:S(2)}, u32[]{:S(2)}) collective-permute-start(bf16[32,64,128]{2,1,0:T(8,128)(2,1)S(1)} %get-tuple-element.37), channel_id=1, source_target_pairs={{0,8},{8,0},{16,24},{24,16},{32,40},{40,32},{48,56},{56,48},{64,72... | collective-permute-start | bytes 1572872 | tf_op jit(solution)/shard_map/ppermute | solution.py:428
  157.0 9.7 %collective-permute-start.6 = (bf16[2,128,1024]{2,1,0:T(8,128)(2,1)S(1)}, bf16[2,128,1024]{2,1,0:T(8,128)(2,1)}, u32[]{:S(2)}, u32[]{:S(2)}) collective-permute-start(bf16[2,128,1024]{2,1,0:T(8,128)(2,1)S(1)} %get-tuple-element.29), channel_id=1, source_target_pairs={{0,8},{8,0},{16,24},{24,16},{32,40},{40,32},{48,56},{56,48},{64,72... | collective-permute-start | bytes 1572872 | tf_op jit(solution)/shard_map/ppermute | solution.py:433
  158.9 20.4 %all-to-all-start.2 = ((bf16[4,2,128,512]{3,2,1,0:T(8,128)(2,1)}), bf16[4,2,128,512]{3,2,1,0:T(8,128)(2,1)}, u32[]{:S(2)}, u32[]{:S(2)}) async-start(bf16[4,2,128,512]{3,2,1,0:T(8,128)(2,1)} %get-tuple-element.35), calls=%async_computation.2 | async-start | bytes 2097152 | tf_op jit(solution)/shard_map/all_to_all | solution.py:422
  163.4 10.6 %collective-permute-start.13 = (bf16[16,64,128]{2,1,0:T(8,128)(2,1)S(1)}, bf16[16,64,128]{2,1,0:T(8,128)(2,1)S(1)}, u32[]{:S(2)}, u32[]{:S(2)}) collective-permute-start(bf16[16,64,128]{2,1,0:T(8,128)(2,1)S(1)} %broadcast_select_fusion), channel_id=1, source_target_pairs={{0,256},{8,264},{16,272},{24,280},{32,288},{40,296},{48,304},{56,3... | collective-permute-start | bytes 786440 | tf_op jit(solution)/shard_map/ppermute | solution.py:430
  179.3 21.8 %all-to-all-start.3 = ((bf16[16,64,128]{2,1,0:T(8,128)(2,1)}), bf16[16,64,128]{2,1,0:T(8,128)(2,1)S(1)}, u32[]{:S(2)}, u32[]{:S(2)}) async-start(bf16[16,64,128]{2,1,0:T(8,128)(2,1)} %add_convert_fusion.1), calls=%async_computation.3 | async-start | bytes 524288 | tf_op jit(solution)/shard_map/all_to_all | solution.py:437
  182.9 11.1 %collective-permute-start.7 = (bf16[128,1024]{1,0:T(8,128)(2,1)S(1)}, bf16[128,1024]{1,0:T(8,128)(2,1)S(1)}, u32[]{:S(2)}, u32[]{:S(2)}) collective-permute-start(bf16[128,1024]{1,0:T(8,128)(2,1)S(1)} %fusion.4), channel_id=1, source_target_pairs={{0,256},{8,264},{16,272},{24,280},{32,288},{40,296},{48,304},{56,3... | collective-permute-start | bytes 786440 | tf_op jit(solution)/shard_map/ppermute | solution.py:435
  187.5 8.4 %collective-permute-start.11 = (bf16[128,512]{1,0:T(8,128)(2,1)S(1)}, bf16[128,512]{1,0:T(8,128)(2,1)S(1)}, u32[]{:S(2)}, u32[]{:S(2)}) collective-permute-start(bf16[128,512]{1,0:T(8,128)(2,1)S(1)} %fusion.6), channel_id=1, source_target_pairs={{0,4},{1,5},{2,6},{3,7},{4,0},{5,1},{6,2},{7,3},{8,12},{9,13},{10,... | collective-permute-start | bytes 393224 | tf_op jit(solution)/shard_map/ppermute | solution.py:426
  (2 other events, 2.0 us)

commit v5 on v3

--- a/solution.py
+++ b/solution.py
@@ -365,6 +365,7 @@
         along_z(column[:2], 2),
         along_z(column[2:], -2),
     ]
+    across, kv = lax.optimization_barrier((across, kv))
     corner = lax.ppermute(across, "ctx", C_SWAP)
     operands = [own, across, beside, corner]
     operands += kv

time: 205 us -> 192 us (0.937)
  starting transfers between devices: 82 us -> 75.8 us
  blocking collectives: 36.1 us -> 31.8 us
    all_to_all x1, waiting for transfers between devices: 0.59 us -> 13.2 us  [on_device(): column = lax.all_to_all(column, 'ctx', 0, 0, axis_index_groups=COLUMNS)]
    ppermute x1, waiting for transfers between devices: 10.7 us -> 0.01 us  [on_device(): across = lax.ppermute(own, 'ctx', Y_SWAP)]
    ppermute x8, starting transfers between devices: 41.3 us -> 31.3 us  [along_z(): return lax.ppermute(value, 'ctx', pairs)]
    ppermute x8, waiting for transfers between devices: 19.4 us -> 15 us  [along_z(): return lax.ppermute(value, 'ctx', pairs)]
    all_to_all x1, starting transfers between devices: 3.53 us -> 6.38 us  [on_device(): pieces = lax.all_to_all(term, 'ctx', 0, 0, axis_index_groups=LINES)]
    all_gather x1, blocking collectives: 7.89 us -> 5.61 us  [on_device(): all_stats = lax.all_gather(stats, 'ctx', axis_index_groups=QUADS)]
  transfers between devices with their start and end apart: 19 -> 19, of which waited for: 11 -> 11; matrix products, arithmetic and copies ran while one was open for 3% -> 2% of each run, Pallas kernels for 0% -> 0%
where the time goes in v5:
time: 192 us; the launch traced here: 191 us
  starting transfers between devices  75.8 us (39%)
  waiting for transfers between devices  51.2 us (27%)
  blocking collectives  31.8 us (17%)
  Pallas kernels  23.2 us (12%)
  other arithmetic  4.93 us (3%)
  local copies, waits for them, and re-layouts  3.25 us (2%)
    ppermute x8, starting transfers between devices, along_z(): return lax.ppermute(value, 'ctx', pairs)  31.3 us
    all_to_all x1, blocking collectives, on_device(): lax.all_to_all(column.astype(bf16), 'ctx', 0, 0, axis_index_groups=COLUMNS)  26.2 us
    all_to_all x1, starting transfers between devices, on_device(): column = lax.all_to_all(column, 'ctx', 0, 0, axis_index_groups=COLUMNS)  15.1 us
    ppermute x8, waiting for transfers between devices, along_z(): return lax.ppermute(value, 'ctx', pairs)  15 us
    all_to_all x1, waiting for transfers between devices, on_device(): column = lax.all_to_all(column, 'ctx', 0, 0, axis_index_groups=COLUMNS)  13.2 us
    pallas_call x1, Pallas kernels, on_device(): pl.pallas_call(grads_kernel, out_shape=[jax.ShapeDtypeStruct((2, ROWS, GR...  12.1 us
    ppermute x1, waiting for transfers between devices, on_device(): far = lax.ppermute(jnp.where(mine_y == 0, term[1], term[0]), 'ctx', Y_SWAP)  7.08 us
    pallas_call x1, Pallas kernels, on_device(): pl.pallas_call(stats_kernel, out_shape=jax.ShapeDtypeStruct((3, plane, GR...  6.98 us
  transfers between devices with their start and end apart: 19, of which 11 were waited for; matrix products, arithmetic and copies ran while one was open for 2% of the time, Pallas kernels for 0%

profile of v5, /device:TPU:24, one launch (start us, length us, event | category | flops | bytes accessed | tf_op | source)
XLA Modules:
  0.0 191.3 jit_solution(638334607824833043)
XLA Ops:
  5.0 15.1 %all-to-all-start = ((bf16[4,128,256]{2,1,0:T(8,128)(2,1)}), bf16[4,128,256]{2,1,0:T(8,128)(2,1)S(1)}, u32[]{:S(2)}, u32[]{:S(2)}) async-start(bf16[4,128,256]{2,1,0:T(8,128)(2,1)} %shard_map.102), calls=%async_computation | async-start | bytes 524288 | tf_op jit(solution)/shard_map/all_to_all | solution.py:339
  22.8 2.7 %collective-permute-start = (bf16[2048,128]{1,0:T(8,128)(2,1)S(1)}, bf16[2048,128]{1,0:T(8,128)(2,1)S(1)}, u32[]{:S(2)}, u32[]{:S(2)}) collective-permute-start(bf16[2048,128]{1,0:T(8,128)(2,1)S(1)} %get-tuple-element.31.refs_0_), channel_id=1, source_target_pairs={{0,256},{8,264},{16,272},{24,280},{32,288},{40,296},{48,304},{56,3... | collective-permute-start | bytes 1572872 | tf_op jit(solution)/shard_map/ppermute | solution.py:357
  25.4 13.2 %all-to-all-done.refs_4_ = bf16[4,128,256]{2,1,0:T(8,128)(2,1)S(1)} async-done(((bf16[4,128,256]{2,1,0:T(8,128)(2,1)}), bf16[4,128,256]{2,1,0:T(8,128)(2,1)S(1)}, u32[]{:S(2)}, u32[]{:S(2)}) %all-to-all-start) | async-done | bytes 262176 | tf_op jit(solution)/shard_map/all_to_all | solution.py:339
  38.6 5.0 %collective-permute-start.3 = (bf16[4,128,256]{2,1,0:T(8,128)(2,1)S(1)}, bf16[4,128,256]{2,1,0:T(8,128)(2,1)S(1)}, u32[]{:S(2)}, u32[]{:S(2)}) collective-permute-start(bf16[4,128,256]{2,1,0:T(8,128)(2,1)S(1)} %all-to-all-done.refs_4_), channel_id=1, source_target_pairs={{0,496},{8,504},{16,256},{24,264},{32,272},{40,280},{48,288},{56,2... | collective-permute-start | bytes 786440 | tf_op jit(solution)/shard_map/ppermute | solution.py:57
  46.0 4.2 %collective-permute-start.5 = (bf16[2,128,256]{2,1,0:T(8,128)(2,1)S(1)}, bf16[2,128,256]{2,1,0:T(8,128)(2,1)S(1)}, u32[]{:S(2)}, u32[]{:S(2)}) collective-permute-start(bf16[2,128,256]{2,1,0:T(8,128)(2,1)S(1)} %get-tuple-element.52), channel_id=1, source_target_pairs={{0,224},{8,232},{16,240},{24,248},{32,0},{40,8},{48,16},{56,24},{6... | collective-permute-start | bytes 393224 | tf_op jit(solution)/shard_map/ppermute | solution.py:57
  50.3 2.8 %collective-permute-start.4 = (bf16[2,128,256]{2,1,0:T(8,128)(2,1)S(1)}, bf16[2,128,256]{2,1,0:T(8,128)(2,1)S(1)}, u32[]{:S(2)}, u32[]{:S(2)}) collective-permute-start(bf16[2,128,256]{2,1,0:T(8,128)(2,1)S(1)} %get-tuple-element.53), channel_id=1, source_target_pairs={{0,32},{8,40},{16,48},{24,56},{32,64},{40,72},{48,80},{56,88},{64,... | collective-permute-start | bytes 393224 | tf_op jit(solution)/shard_map/ppermute | solution.py:57
  53.1 3.5 %collective-permute-done.5.refs_8_ = bf16[2,128,256]{2,1,0:T(8,128)(2,1)S(1)} collective-permute-done((bf16[2,128,256]{2,1,0:T(8,128)(2,1)S(1)}, bf16[2,128,256]{2,1,0:T(8,128)(2,1)S(1)}, u32[]{:S(2)}, u32[]{:S(2)}) %collective-permute-start.5) | collective-permute-done | bytes 131104 | tf_op jit(solution)/shard_map/ppermute | solution.py:57
  56.6 5.3 %collective-permute-done.4.refs_7_ = bf16[2,128,256]{2,1,0:T(8,128)(2,1)S(1)} collective-permute-done((bf16[2,128,256]{2,1,0:T(8,128)(2,1)S(1)}, bf16[2,128,256]{2,1,0:T(8,128)(2,1)S(1)}, u32[]{:S(2)}, u32[]{:S(2)}) %collective-permute-start.4) | collective-permute-done | bytes 131104 | tf_op jit(solution)/shard_map/ppermute | solution.py:57
  65.7 7.0 %shard_map.104 = f32[3,4,8,128]{3,2,1,0:T(8,128)S(1)} custom-call(s32[17]{0:T(128)S(1)} %get-tuple-element.30.place, bf16[2048,128]{1,0:T(8,128)(2,1)S(1)} %get-tuple-element.31.refs_0_, bf16[2048,128]{1,0:T(8,128)(2,1)S(1)} %collective-permute-done.refs_1_, bf16[2048,128]{1,0:T(8,128)(2,1)S(1)} %collective-permute-done.1.refs_2_, ...), custom_call_target="tpu_custom_call" | custom-call | tf_op jit(solution)/shard_map/pallas_call | solution.py:375
  72.7 5.6 %all-gather = f32[12,4,8,128]{3,2,1,0:T(8,128)S(1)} all-gather(f32[3,4,8,128]{3,2,1,0:T(8,128)S(1)} %shard_map.104), channel_id=2, replica_groups={{0,8,256,264},{16,24,272,280},{32,40,288,296},{48,56,304,312},{64,72,32..., dimensions={0}, use_global_device_ids=true | all-gather | bytes 245760 | tf_op jit(solution)/shard_map/all_gather | solution.py:383
  78.3 12.1 %shard_map.105 = (bf16[2,128,1024]{2,1,0:T(8,128)(2,1)S(1)}, bf16[2,128,1024]{2,1,0:T(8,128)(2,1)S(1)}, bf16[4,128,256]{2,1,0:T(8,128)(2,1)S(1)}, bf16[4,128,256...) custom-call(s32[17]{0:T(128)S(1)} %get-tuple-element.30.place, ...), custom_call_target="tpu_custom_call" | custom-call | tf_op jit(solution)/shard_map/pallas_call | solution.py:384
  92.5 8.1 %collective-permute-start.10 = (bf16[4,128,256]{2,1,0:T(8,128)(2,1)S(1)}, bf16[4,128,256]{2,1,0:T(8,128)(2,1)S(1)}, u32[]{:S(2)}, u32[]{:S(2)}) collective-permute-start(bf16[4,128,256]{2,1,0:T(8,128)(2,1)S(1)} %get-tuple-element.45), channel_id=1, source_target_pairs={{0,272},{8,280},{16,288},{24,296},{32,304},{40,312},{48,320},{56,3... | collective-permute-start | bytes 786440 | tf_op jit(solution)/shard_map/ppermute | solution.py:57
  102.5 4.8 %collective-permute-start.12 = (bf16[2,128,256]{2,1,0:T(8,128)(2,1)S(1)}, bf16[2,128,256]{2,1,0:T(8,128)(2,1)S(1)}, u32[]{:S(2)}, u32[]{:S(2)}) collective-permute-start(bf16[2,128,256]{2,1,0:T(8,128)(2,1)S(1)} %get-tuple-element.47), channel_id=1, source_target_pairs={{0,32},{8,40},{16,48},{24,56},{32,64},{40,72},{48,80},{56,88},{64,... | collective-permute-start | bytes 393224 | tf_op jit(solution)/shard_map/ppermute | solution.py:57
  107.3 4.5 %collective-permute-done.11 = bf16[2,128,256]{2,1,0:T(8,128)(2,1)S(1)} collective-permute-done((bf16[2,128,256]{2,1,0:T(8,128)(2,1)S(1)}, bf16[2,128,256]{2,1,0:T(8,128)(2,1)S(1)}, u32[]{:S(2)}, u32[]{:S(2)}) %collective-permute-start.11) | collective-permute-done | bytes 131104 | tf_op jit(solution)/shard_map/ppermute | solution.py:57
  113.7 26.2 %all_to_all.20.parts = bf16[4,128,256]{2,1,0:T(8,128)(2,1)S(1)} all-to-all(bf16[4,128,256]{2,1,0:T(8,128)(2,1)S(1)} %add_convert_fusion.2), channel_id=1, replica_groups={{0,64,128,192},{8,72,136,200},{16,80,144,208},{24,88,152,216},{32,96,16..., dimensions={0} | all-to-all | bytes 524288 | tf_op jit(solution)/shard_map/all_to_all | solution.py:407
  146.5 4.4 %all-to-all-start.2 = ((bf16[4,2,128,512]{3,2,1,0:T(8,128)(2,1)}), bf16[4,2,128,512]{3,2,1,0:T(8,128)(2,1)}, u32[]{:S(2)}, u32[]{:S(2)}) async-start(bf16[4,2,128,512]{3,2,1,0:T(8,128)(2,1)} %get-tuple-element.49), calls=%async_computation.2 | async-start | bytes 2097152 | tf_op jit(solution)/shard_map/all_to_all | solution.py:422
  151.1 2.8 %collective-permute-start.15 = (bf16[16,64,128]{2,1,0:T(8,128)(2,1)S(1)}, bf16[16,64,128]{2,1,0:T(8,128)(2,1)S(1)}, u32[]{:S(2)}, u32[]{:S(2)}) collective-permute-start(bf16[16,64,128]{2,1,0:T(8,128)(2,1)S(1)} %broadcast_select_fusion), channel_id=1, source_target_pairs={{0,256},{8,264},{16,272},{24,280},{32,288},{40,296},{48,304},{56,3... | collective-permute-start | bytes 786440 | tf_op jit(solution)/shard_map/ppermute | solution.py:430
  154.1 7.1 %collective-permute-done.15 = bf16[16,64,128]{2,1,0:T(8,128)(2,1)S(1)} collective-permute-done((bf16[16,64,128]{2,1,0:T(8,128)(2,1)S(1)}, bf16[16,64,128]{2,1,0:T(8,128)(2,1)S(1)}, u32[]{:S(2)}, u32[]{:S(2)}) %collective-permute-start.15) | collective-permute-done | bytes 262176 | tf_op jit(solution)/shard_map/ppermute | solution.py:430
  162.0 4.4 %all-to-all-done.2 = bf16[4,2,128,512]{3,2,1,0:T(8,128)(2,1)} async-done(((bf16[4,2,128,512]{3,2,1,0:T(8,128)(2,1)}), bf16[4,2,128,512]{3,2,1,0:T(8,128)(2,1)}, u32[]{:S(2)}, u32[]{:S(2)}) %all-to-all-start.2) | async-done | bytes 1048608 | tf_op jit(solution)/shard_map/all_to_all | solution.py:422
  166.4 6.4 %all-to-all-start.3 = ((bf16[16,64,128]{2,1,0:T(8,128)(2,1)}), bf16[16,64,128]{2,1,0:T(8,128)(2,1)S(1)}, u32[]{:S(2)}, u32[]{:S(2)}) async-start(bf16[16,64,128]{2,1,0:T(8,128)(2,1)} %add_convert_fusion.1), calls=%async_computation.3 | async-start | bytes 524288 | tf_op jit(solution)/shard_map/all_to_all | solution.py:437
  172.9 2.6 %collective-permute-start.8 = (bf16[128,1024]{1,0:T(8,128)(2,1)S(1)}, bf16[128,1024]{1,0:T(8,128)(2,1)S(1)}, u32[]{:S(2)}, u32[]{:S(2)}) collective-permute-start(bf16[128,1024]{1,0:T(8,128)(2,1)S(1)} %fusion.4), channel_id=1, source_target_pairs={{0,256},{8,264},{16,272},{24,280},{32,288},{40,296},{48,304},{56,3... | collective-permute-start | bytes 786440 | tf_op jit(solution)/shard_map/ppermute | solution.py:435
  177.0 2.5 %collective-permute-start.13 = (bf16[128,512]{1,0:T(8,128)(2,1)S(1)}, bf16[128,512]{1,0:T(8,128)(2,1)S(1)}, u32[]{:S(2)}, u32[]{:S(2)}) collective-permute-start(bf16[128,512]{1,0:T(8,128)(2,1)S(1)} %fusion.6), channel_id=1, source_target_pairs={{0,4},{1,5},{2,6},{3,7},{4,0},{5,1},{6,2},{7,3},{8,12},{9,13},{10,... | collective-permute-start | bytes 393224 | tf_op jit(solution)/shard_map/ppermute | solution.py:426
  179.5 3.7 %collective-permute-done.8 = bf16[128,1024]{1,0:T(8,128)(2,1)S(1)} collective-permute-done((bf16[128,1024]{1,0:T(8,128)(2,1)S(1)}, bf16[128,1024]{1,0:T(8,128)(2,1)S(1)}, u32[]{:S(2)}, u32[]{:S(2)}) %collective-permute-start.8) | collective-permute-done | bytes 262176 | tf_op jit(solution)/shard_map/ppermute | solution.py:435
  186.0 4.6 %all-to-all-done.3 = bf16[16,64,128]{2,1,0:T(8,128)(2,1)S(1)} async-done(((bf16[16,64,128]{2,1,0:T(8,128)(2,1)}), bf16[16,64,128]{2,1,0:T(8,128)(2,1)S(1)}, u32[]{:S(2)}, u32[]{:S(2)}) %all-to-all-start.3) | async-done | bytes 262176 | tf_op jit(solution)/shard_map/all_to_all | solution.py:437
  (51 shorter events, 31.7 us)
Async XLA Ops:
  3.8 16.2 %copy-start.5 = (bf16[128,1024]{1,0:T(8,128)(2,1)S(1)}, bf16[128,1024]{1,0:T(8,128)(2,1)}, u32[]{:S(2)}) copy-start(bf16[128,1024]{1,0:T(8,128)(2,1)} %grads) | copy-start | bytes 786436
  3.8 16.2 %copy-start.7 = (s32[8192]{0:T(1024)S(1)}, s32[8192]{0:T(1024)}, u32[]{:S(2)}) copy-start(s32[8192]{0:T(1024)} %param.12) | copy-start | bytes 98308
  3.9 16.2 %copy-start.8 = (s32[128]{0:T(128)S(1)}, s32[128]{0:T(128)}, u32[]{:S(2)}) copy-start(s32[128]{0:T(128)} %param.13) | copy-start | bytes 1540
  5.0 33.7 %all-to-all-start = ((bf16[4,128,256]{2,1,0:T(8,128)(2,1)}), bf16[4,128,256]{2,1,0:T(8,128)(2,1)S(1)}, u32[]{:S(2)}, u32[]{:S(2)}) async-start(bf16[4,128,256]{2,1,0:T(8,128)(2,1)} %shard_map.102), calls=%async_computation | async-start | bytes 524288 | tf_op jit(solution)/shard_map/all_to_all | solution.py:339
  20.8 4.6 %collective-permute-start.1 = (bf16[2048,128]{1,0:T(8,128)(2,1)S(1)}, bf16[2048,128]{1,0:T(8,128)(2,1)S(1)}, u32[]{:S(2)}, u32[]{:S(2)}) collective-permute-start(bf16[2048,128]{1,0:T(8,128)(2,1)S(1)} %get-tuple-element.31.refs_0_), channel_id=1, source_target_pairs={{0,8},{8,0},{16,24},{24,16},{32,40},{40,32},{48,56},{56,48},{64,72... | collective-permute-start | bytes 1572872 | tf_op jit(solution)/shard_map/ppermute | solution.py:358
  22.8 30.4 %collective-permute-start = (bf16[2048,128]{1,0:T(8,128)(2,1)S(1)}, bf16[2048,128]{1,0:T(8,128)(2,1)S(1)}, u32[]{:S(2)}, u32[]{:S(2)}) collective-permute-start(bf16[2048,128]{1,0:T(8,128)(2,1)S(1)} %get-tuple-element.31.refs_0_), channel_id=1, source_target_pairs={{0,256},{8,264},{16,272},{24,280},{32,288},{40,296},{48,304},{56,3... | collective-permute-start | bytes 1572872 | tf_op jit(solution)/shard_map/ppermute | solution.py:357
  38.6 23.2 %collective-permute-start.3 = (bf16[4,128,256]{2,1,0:T(8,128)(2,1)S(1)}, bf16[4,128,256]{2,1,0:T(8,128)(2,1)S(1)}, u32[]{:S(2)}, u32[]{:S(2)}) collective-permute-start(bf16[4,128,256]{2,1,0:T(8,128)(2,1)S(1)} %all-to-all-done.refs_4_), channel_id=1, source_target_pairs={{0,496},{8,504},{16,256},{24,264},{32,272},{40,280},{48,288},{56,2... | collective-permute-start | bytes 786440 | tf_op jit(solution)/shard_map/ppermute | solution.py:57
  43.7 18.2 %collective-permute-start.2 = (bf16[4,128,256]{2,1,0:T(8,128)(2,1)S(1)}, bf16[4,128,256]{2,1,0:T(8,128)(2,1)S(1)}, u32[]{:S(2)}, u32[]{:S(2)}) collective-permute-start(bf16[4,128,256]{2,1,0:T(8,128)(2,1)S(1)} %all-to-all-done.refs_4_), channel_id=1, source_target_pairs={{0,272},{8,280},{16,288},{24,296},{32,304},{40,312},{48,320},{56,3... | collective-permute-start | bytes 786440 | tf_op jit(solution)/shard_map/ppermute | solution.py:57
  46.0 10.6 %collective-permute-start.5 = (bf16[2,128,256]{2,1,0:T(8,128)(2,1)S(1)}, bf16[2,128,256]{2,1,0:T(8,128)(2,1)S(1)}, u32[]{:S(2)}, u32[]{:S(2)}) collective-permute-start(bf16[2,128,256]{2,1,0:T(8,128)(2,1)S(1)} %get-tuple-element.52), channel_id=1, source_target_pairs={{0,224},{8,232},{16,240},{24,248},{32,0},{40,8},{48,16},{56,24},{6... | collective-permute-start | bytes 393224 | tf_op jit(solution)/shard_map/ppermute | solution.py:57
  50.3 11.6 %collective-permute-start.4 = (bf16[2,128,256]{2,1,0:T(8,128)(2,1)S(1)}, bf16[2,128,256]{2,1,0:T(8,128)(2,1)S(1)}, u32[]{:S(2)}, u32[]{:S(2)}) collective-permute-start(bf16[2,128,256]{2,1,0:T(8,128)(2,1)S(1)} %get-tuple-element.53), channel_id=1, source_target_pairs={{0,32},{8,40},{16,48},{24,56},{32,64},{40,72},{48,80},{56,88},{64,... | collective-permute-start | bytes 393224 | tf_op jit(solution)/shard_map/ppermute | solution.py:57
  61.9 3.8 %collective-permute-start.6 = (bf16[2048,128]{1,0:T(8,128)(2,1)S(1)}, bf16[2048,128]{1,0:T(8,128)(2,1)S(1)}, u32[]{:S(2)}, u32[]{:S(2)}) collective-permute-start(bf16[2048,128]{1,0:T(8,128)(2,1)S(1)} %collective-permute-done.refs_1_), channel_id=1, source_target_pairs={{0,8},{8,0},{16,24},{24,16},{32,40},{40,32},{48,56},{56,48},{64,72... | collective-permute-start | bytes 1572872 | tf_op jit(solution)/shard_map/ppermute | solution.py:369
  78.3 61.6 %copy-start.3 = (bf16[4096,128]{1,0:T(8,128)(2,1)S(1)}, bf16[4096,128]{1,0:T(8,128)(2,1)}, u32[]{:S(2)}) copy-start(bf16[4096,128]{1,0:T(8,128)(2,1)} %weight.3) | copy-start | bytes 3145732
  90.4 49.5 %copy-start.1 = (bf16[128,4096]{1,0:T(8,128)(2,1)S(1)}, bf16[128,4096]{1,0:T(8,128)(2,1)}, u32[]{:S(2)}) copy-start(bf16[128,4096]{1,0:T(8,128)(2,1)} %inputs.3) | copy-start | bytes 3145732
  90.4 23.1 %collective-permute-start.9 = (bf16[4,128,256]{2,1,0:T(8,128)(2,1)S(1)}, bf16[4,128,256]{2,1,0:T(8,128)(2,1)S(1)}, u32[]{:S(2)}, u32[]{:S(2)}) collective-permute-start(bf16[4,128,256]{2,1,0:T(8,128)(2,1)S(1)} %get-tuple-element.44), channel_id=1, source_target_pairs={{0,496},{8,504},{16,256},{24,264},{32,272},{40,280},{48,288},{56,2... | collective-permute-start | bytes 786440 | tf_op jit(solution)/shard_map/ppermute | solution.py:57
  92.5 21.1 %collective-permute-start.10 = (bf16[4,128,256]{2,1,0:T(8,128)(2,1)S(1)}, bf16[4,128,256]{2,1,0:T(8,128)(2,1)S(1)}, u32[]{:S(2)}, u32[]{:S(2)}) collective-permute-start(bf16[4,128,256]{2,1,0:T(8,128)(2,1)S(1)} %get-tuple-element.45), channel_id=1, source_target_pairs={{0,272},{8,280},{16,288},{24,296},{32,304},{40,312},{48,320},{56,3... | collective-permute-start | bytes 786440 | tf_op jit(solution)/shard_map/ppermute | solution.py:57
  100.5 11.3 %collective-permute-start.11 = (bf16[2,128,256]{2,1,0:T(8,128)(2,1)S(1)}, bf16[2,128,256]{2,1,0:T(8,128)(2,1)S(1)}, u32[]{:S(2)}, u32[]{:S(2)}) collective-permute-start(bf16[2,128,256]{2,1,0:T(8,128)(2,1)S(1)} %get-tuple-element.46), channel_id=1, source_target_pairs={{0,224},{8,232},{16,240},{24,248},{32,0},{40,8},{48,16},{56,24},{6... | collective-permute-start | bytes 393224 | tf_op jit(solution)/shard_map/ppermute | solution.py:57
  102.5 11.1 %collective-permute-start.12 = (bf16[2,128,256]{2,1,0:T(8,128)(2,1)S(1)}, bf16[2,128,256]{2,1,0:T(8,128)(2,1)S(1)}, u32[]{:S(2)}, u32[]{:S(2)}) collective-permute-start(bf16[2,128,256]{2,1,0:T(8,128)(2,1)S(1)} %get-tuple-element.47), channel_id=1, source_target_pairs={{0,32},{8,40},{16,48},{24,56},{32,64},{40,72},{48,80},{56,88},{64,... | collective-permute-start | bytes 393224 | tf_op jit(solution)/shard_map/ppermute | solution.py:57
  142.2 8.7 %collective-permute-start.14 = (bf16[32,64,128]{2,1,0:T(8,128)(2,1)S(1)}, bf16[32,64,128]{2,1,0:T(8,128)(2,1)S(1)}, u32[]{:S(2)}, u32[]{:S(2)}) collective-permute-start(bf16[32,64,128]{2,1,0:T(8,128)(2,1)S(1)} %get-tuple-element.51), channel_id=1, source_target_pairs={{0,8},{8,0},{16,24},{24,16},{32,40},{40,32},{48,56},{56,48},{64,72... | collective-permute-start | bytes 1572872 | tf_op jit(solution)/shard_map/ppermute | solution.py:428
  144.1 9.8 %collective-permute-start.7 = (bf16[2,128,1024]{2,1,0:T(8,128)(2,1)S(1)}, bf16[2,128,1024]{2,1,0:T(8,128)(2,1)S(1)}, u32[]{:S(2)}, u32[]{:S(2)}) collective-permute-start(bf16[2,128,1024]{2,1,0:T(8,128)(2,1)S(1)} %get-tuple-element.42), channel_id=1, source_target_pairs={{0,8},{8,0},{16,24},{24,16},{32,40},{40,32},{48,56},{56,48},{64,72... | collective-permute-start | bytes 1572872 | tf_op jit(solution)/shard_map/ppermute | solution.py:433
  146.5 19.9 %all-to-all-start.2 = ((bf16[4,2,128,512]{3,2,1,0:T(8,128)(2,1)}), bf16[4,2,128,512]{3,2,1,0:T(8,128)(2,1)}, u32[]{:S(2)}, u32[]{:S(2)}) async-start(bf16[4,2,128,512]{3,2,1,0:T(8,128)(2,1)} %get-tuple-element.49), calls=%async_computation.2 | async-start | bytes 2097152 | tf_op jit(solution)/shard_map/all_to_all | solution.py:422
  151.1 10.0 %collective-permute-start.15 = (bf16[16,64,128]{2,1,0:T(8,128)(2,1)S(1)}, bf16[16,64,128]{2,1,0:T(8,128)(2,1)S(1)}, u32[]{:S(2)}, u32[]{:S(2)}) collective-permute-start(bf16[16,64,128]{2,1,0:T(8,128)(2,1)S(1)} %broadcast_select_fusion), channel_id=1, source_target_pairs={{0,256},{8,264},{16,272},{24,280},{32,288},{40,296},{48,304},{56,3... | collective-permute-start | bytes 786440 | tf_op jit(solution)/shard_map/ppermute | solution.py:430
  166.4 24.2 %all-to-all-start.3 = ((bf16[16,64,128]{2,1,0:T(8,128)(2,1)}), bf16[16,64,128]{2,1,0:T(8,128)(2,1)S(1)}, u32[]{:S(2)}, u32[]{:S(2)}) async-start(bf16[16,64,128]{2,1,0:T(8,128)(2,1)} %add_convert_fusion.1), calls=%async_computation.3 | async-start | bytes 524288 | tf_op jit(solution)/shard_map/all_to_all | solution.py:437
  172.9 10.3 %collective-permute-start.8 = (bf16[128,1024]{1,0:T(8,128)(2,1)S(1)}, bf16[128,1024]{1,0:T(8,128)(2,1)S(1)}, u32[]{:S(2)}, u32[]{:S(2)}) collective-permute-start(bf16[128,1024]{1,0:T(8,128)(2,1)S(1)} %fusion.4), channel_id=1, source_target_pairs={{0,256},{8,264},{16,272},{24,280},{32,288},{40,296},{48,304},{56,3... | collective-permute-start | bytes 786440 | tf_op jit(solution)/shard_map/ppermute | solution.py:435
  177.0 8.4 %collective-permute-start.13 = (bf16[128,512]{1,0:T(8,128)(2,1)S(1)}, bf16[128,512]{1,0:T(8,128)(2,1)S(1)}, u32[]{:S(2)}, u32[]{:S(2)}) collective-permute-start(bf16[128,512]{1,0:T(8,128)(2,1)S(1)} %fusion.6), channel_id=1, source_target_pairs={{0,4},{1,5},{2,6},{3,7},{4,0},{5,1},{6,2},{7,3},{8,12},{9,13},{10,... | collective-permute-start | bytes 393224 | tf_op jit(solution)/shard_map/ppermute | solution.py:426
  (4 other events, 19.4 us)

commit v6 on v4

--- a/solution.py
+++ b/solution.py
@@ -365,6 +365,7 @@
         along_z(column, -1),
         along_z(column, 2, -2),
     ]
+    across, kv = lax.optimization_barrier((across, kv))
     corner = lax.ppermute(across, "ctx", C_SWAP)
     operands = [own, across, beside, corner]
     operands += kv

time: 204 us -> 192 us (0.941); the launches traced: 202 us -> 193 us
  starting transfers between devices: 87.3 us -> 69.6 us
  waiting for transfers between devices: 46.2 us -> 55.5 us
    all_to_all x1, waiting for transfers between devices: 0.59 us -> 13.2 us  [on_device(): column = lax.all_to_all(column, 'ctx', 0, 0, axis_index_groups=COLUMNS)]
    ppermute x6, starting transfers between devices: 37.5 us -> 25 us  [along_z(): return lax.ppermute(value, 'ctx', pairs)]
    ppermute x1, waiting for transfers between devices: 10.7 us -> 0.01 us  [on_device(): across = lax.ppermute(own, 'ctx', Y_SWAP)]
    ppermute x1, starting transfers between devices: 9.02 us -> 2.01 us  [on_device(): near = lax.ppermute(sent, 'ctx', C_SWAP)]
    ppermute x6, waiting for transfers between devices: 15.3 us -> 20.1 us  [along_z(): return lax.ppermute(value, 'ctx', pairs)]
  transfers between devices with their start and end apart: 17 -> 17, of which waited for: 10 -> 12; matrix products, arithmetic and copies ran while one was open for 3% -> 2% of each run, Pallas kernels for 0% -> 0%
where the time goes in v6:
time: 192 us; the launch traced here: 193 us
  starting transfers between devices  69.6 us (36%)
  waiting for transfers between devices  55.5 us (29%)
  blocking collectives  35.6 us (19%)
  Pallas kernels  23.2 us (12%)
  other arithmetic  4.94 us (3%)
  local copies, waits for them, and re-layouts  3.23 us (2%)
    all_to_all x1, blocking collectives, on_device(): lax.all_to_all(column.astype(bf16), 'ctx', 0, 0, axis_index_groups=COLUMNS)  30 us
    ppermute x6, starting transfers between devices, along_z(): return lax.ppermute(value, 'ctx', pairs)  25 us
    ppermute x6, waiting for transfers between devices, along_z(): return lax.ppermute(value, 'ctx', pairs)  20.1 us
    all_to_all x1, starting transfers between devices, on_device(): column = lax.all_to_all(column, 'ctx', 0, 0, axis_index_groups=COLUMNS)  15.1 us
    all_to_all x1, waiting for transfers between devices, on_device(): column = lax.all_to_all(column, 'ctx', 0, 0, axis_index_groups=COLUMNS)  13.2 us
    pallas_call x1, Pallas kernels, on_device(): pl.pallas_call(grads_kernel, out_shape=[jax.ShapeDtypeStruct((2, ROWS, GR...  12.1 us
    ppermute x1, waiting for transfers between devices, on_device(): far = lax.ppermute(jnp.where(mine_y == 0, term[1], term[0]), 'ctx', Y_SWAP)  7.11 us
    pallas_call x1, Pallas kernels, on_device(): pl.pallas_call(stats_kernel, out_shape=jax.ShapeDtypeStruct((3, plane, GR...  6.98 us
  transfers between devices with their start and end apart: 17, of which 12 were waited for; matrix products, arithmetic and copies ran while one was open for 2% of the time, Pallas kernels for 0%

profile of v6, /device:TPU:24, one launch (start us, length us, event | category | flops | bytes accessed | tf_op | source)
XLA Modules:
  0.0 193.1 jit_solution(6567424863541149834)
XLA Ops:
  5.0 15.1 %all-to-all-start = ((bf16[4,128,256]{2,1,0:T(8,128)(2,1)}), bf16[4,128,256]{2,1,0:T(8,128)(2,1)S(1)}, u32[]{:S(2)}, u32[]{:S(2)}) async-start(bf16[4,128,256]{2,1,0:T(8,128)(2,1)} %shard_map.102), calls=%async_computation | async-start | bytes 524288 | tf_op jit(solution)/shard_map/all_to_all | solution.py:340
  22.8 2.7 %collective-permute-start = (bf16[2048,128]{1,0:T(8,128)(2,1)S(1)}, bf16[2048,128]{1,0:T(8,128)(2,1)S(1)}, u32[]{:S(2)}, u32[]{:S(2)}) collective-permute-start(bf16[2048,128]{1,0:T(8,128)(2,1)S(1)} %get-tuple-element.29.refs_0_), channel_id=1, source_target_pairs={{0,256},{8,264},{16,272},{24,280},{32,288},{40,296},{48,304},{56,3... | collective-permute-start | bytes 1572872 | tf_op jit(solution)/shard_map/ppermute | solution.py:358
  25.4 13.2 %all-to-all-done.refs_4_ = bf16[4,128,256]{2,1,0:T(8,128)(2,1)S(1)} async-done(((bf16[4,128,256]{2,1,0:T(8,128)(2,1)}), bf16[4,128,256]{2,1,0:T(8,128)(2,1)S(1)}, u32[]{:S(2)}, u32[]{:S(2)}) %all-to-all-start) | async-done | bytes 262176 | tf_op jit(solution)/shard_map/all_to_all | solution.py:340
  38.6 5.8 %collective-permute-start.4 = (bf16[4,128,256]{2,1,0:T(8,128)(2,1)S(1)}, bf16[4,128,256]{2,1,0:T(8,128)(2,1)S(1)}, u32[]{:S(2)}, u32[]{:S(2)}) collective-permute-start(bf16[4,128,256]{2,1,0:T(8,128)(2,1)S(1)} %all-to-all-done.refs_4_), channel_id=1, source_target_pairs={{0,32},{8,232},{16,48},{24,248},{32,64},{40,8},{48,80},{56,24},{64... | collective-permute-start | bytes 786440 | tf_op jit(solution)/shard_map/ppermute | solution.py:58
  44.4 4.3 %collective-permute-start.3 = (bf16[4,128,256]{2,1,0:T(8,128)(2,1)S(1)}, bf16[4,128,256]{2,1,0:T(8,128)(2,1)S(1)}, u32[]{:S(2)}, u32[]{:S(2)}) collective-permute-start(bf16[4,128,256]{2,1,0:T(8,128)(2,1)S(1)} %all-to-all-done.refs_4_), channel_id=1, source_target_pairs={{0,496},{8,504},{16,256},{24,264},{32,272},{40,280},{48,288},{56,2... | collective-permute-start | bytes 786440 | tf_op jit(solution)/shard_map/ppermute | solution.py:58
  48.7 2.5 %collective-permute-start.2 = (bf16[4,128,256]{2,1,0:T(8,128)(2,1)S(1)}, bf16[4,128,256]{2,1,0:T(8,128)(2,1)S(1)}, u32[]{:S(2)}, u32[]{:S(2)}) collective-permute-start(bf16[4,128,256]{2,1,0:T(8,128)(2,1)S(1)} %all-to-all-done.refs_4_), channel_id=1, source_target_pairs={{0,272},{8,280},{16,288},{24,296},{32,304},{40,312},{48,320},{56,3... | collective-permute-start | bytes 786440 | tf_op jit(solution)/shard_map/ppermute | solution.py:58
  51.2 6.9 %collective-permute-done.3.refs_6_ = bf16[4,128,256]{2,1,0:T(8,128)(2,1)S(1)} collective-permute-done((bf16[4,128,256]{2,1,0:T(8,128)(2,1)S(1)}, bf16[4,128,256]{2,1,0:T(8,128)(2,1)S(1)}, u32[]{:S(2)}, u32[]{:S(2)}) %collective-permute-start.3) | collective-permute-done | bytes 262176 | tf_op jit(solution)/shard_map/ppermute | solution.py:58
  64.1 7.0 %shard_map.104 = f32[3,4,8,128]{3,2,1,0:T(8,128)S(1)} custom-call(s32[17]{0:T(128)S(1)} %get-tuple-element.28.place, bf16[2048,128]{1,0:T(8,128)(2,1)S(1)} %get-tuple-element.29.refs_0_, bf16[2048,128]{1,0:T(8,128)(2,1)S(1)} %collective-permute-done.refs_1_, bf16[2048,128]{1,0:T(8,128)(2,1)S(1)} %collective-permute-done.1.refs_2_, ...), custom_call_target="tpu_custom_call" | custom-call | tf_op jit(solution)/shard_map/pallas_call | solution.py:375
  71.1 5.6 %all-gather = f32[12,4,8,128]{3,2,1,0:T(8,128)S(1)} all-gather(f32[3,4,8,128]{3,2,1,0:T(8,128)S(1)} %shard_map.104), channel_id=2, replica_groups={{0,8,256,264},{16,24,272,280},{32,40,288,296},{48,56,304,312},{64,72,32..., dimensions={0}, use_global_device_ids=true | all-gather | bytes 245760 | tf_op jit(solution)/shard_map/all_gather | solution.py:383
  76.7 12.1 %shard_map.105 = (bf16[2,128,1024]{2,1,0:T(8,128)(2,1)S(1)}, bf16[2,128,1024]{2,1,0:T(8,128)(2,1)S(1)}, bf16[4,128,256]{2,1,0:T(8,128)(2,1)S(1)}, bf16[4,128,256...) custom-call(s32[17]{0:T(128)S(1)} %get-tuple-element.28.place, ...), custom_call_target="tpu_custom_call" | custom-call | tf_op jit(solution)/shard_map/pallas_call | solution.py:384
  88.9 5.2 %collective-permute-start.8 = (bf16[4,128,256]{2,1,0:T(8,128)(2,1)S(1)}, bf16[4,128,256]{2,1,0:T(8,128)(2,1)S(1)}, u32[]{:S(2)}, u32[]{:S(2)}) collective-permute-start(bf16[4,128,256]{2,1,0:T(8,128)(2,1)S(1)} %get-tuple-element.41), channel_id=1, source_target_pairs={{0,496},{8,504},{16,256},{24,264},{32,272},{40,280},{48,288},{56,2... | collective-permute-start | bytes 786440 | tf_op jit(solution)/shard_map/ppermute | solution.py:58
  94.1 5.3 %collective-permute-start.9 = (bf16[4,128,256]{2,1,0:T(8,128)(2,1)S(1)}, bf16[4,128,256]{2,1,0:T(8,128)(2,1)S(1)}, u32[]{:S(2)}, u32[]{:S(2)}) collective-permute-start(bf16[4,128,256]{2,1,0:T(8,128)(2,1)S(1)} %get-tuple-element.42), channel_id=1, source_target_pairs={{0,272},{8,280},{16,288},{24,296},{32,304},{40,312},{48,320},{56,3... | collective-permute-start | bytes 786440 | tf_op jit(solution)/shard_map/ppermute | solution.py:58
  101.4 3.8 %collective-permute-done.8 = bf16[4,128,256]{2,1,0:T(8,128)(2,1)S(1)} collective-permute-done((bf16[4,128,256]{2,1,0:T(8,128)(2,1)S(1)}, bf16[4,128,256]{2,1,0:T(8,128)(2,1)S(1)}, u32[]{:S(2)}, u32[]{:S(2)}) %collective-permute-start.8) | collective-permute-done | bytes 262176 | tf_op jit(solution)/shard_map/ppermute | solution.py:58
  105.2 6.1 %collective-permute-done.9 = bf16[4,128,256]{2,1,0:T(8,128)(2,1)S(1)} collective-permute-done((bf16[4,128,256]{2,1,0:T(8,128)(2,1)S(1)}, bf16[4,128,256]{2,1,0:T(8,128)(2,1)S(1)}, u32[]{:S(2)}, u32[]{:S(2)}) %collective-permute-start.9) | collective-permute-done | bytes 262176 | tf_op jit(solution)/shard_map/ppermute | solution.py:58
  112.4 30.0 %all_to_all.20.parts = bf16[4,128,256]{2,1,0:T(8,128)(2,1)S(1)} all-to-all(bf16[4,128,256]{2,1,0:T(8,128)(2,1)S(1)} %add_convert_fusion.2), channel_id=1, replica_groups={{0,64,128,192},{8,72,136,200},{16,80,144,208},{24,88,152,216},{32,96,16..., dimensions={0} | all-to-all | bytes 524288 | tf_op jit(solution)/shard_map/all_to_all | solution.py:408
  149.1 4.3 %all-to-all-start.2 = ((bf16[4,2,128,512]{3,2,1,0:T(8,128)(2,1)}), bf16[4,2,128,512]{3,2,1,0:T(8,128)(2,1)}, u32[]{:S(2)}, u32[]{:S(2)}) async-start(bf16[4,2,128,512]{3,2,1,0:T(8,128)(2,1)} %get-tuple-element.45), calls=%async_computation.2 | async-start | bytes 2097152 | tf_op jit(solution)/shard_map/all_to_all | solution.py:423
  153.6 3.0 %collective-permute-start.13 = (bf16[16,64,128]{2,1,0:T(8,128)(2,1)S(1)}, bf16[16,64,128]{2,1,0:T(8,128)(2,1)S(1)}, u32[]{:S(2)}, u32[]{:S(2)}) collective-permute-start(bf16[16,64,128]{2,1,0:T(8,128)(2,1)S(1)} %broadcast_select_fusion), channel_id=1, source_target_pairs={{0,256},{8,264},{16,272},{24,280},{32,288},{40,296},{48,304},{56,3... | collective-permute-start | bytes 786440 | tf_op jit(solution)/shard_map/ppermute | solution.py:431
  156.7 7.1 %collective-permute-done.13 = bf16[16,64,128]{2,1,0:T(8,128)(2,1)S(1)} collective-permute-done((bf16[16,64,128]{2,1,0:T(8,128)(2,1)S(1)}, bf16[16,64,128]{2,1,0:T(8,128)(2,1)S(1)}, u32[]{:S(2)}, u32[]{:S(2)}) %collective-permute-start.13) | collective-permute-done | bytes 262176 | tf_op jit(solution)/shard_map/ppermute | solution.py:431
  164.6 4.4 %all-to-all-done.2 = bf16[4,2,128,512]{3,2,1,0:T(8,128)(2,1)} async-done(((bf16[4,2,128,512]{3,2,1,0:T(8,128)(2,1)}), bf16[4,2,128,512]{3,2,1,0:T(8,128)(2,1)}, u32[]{:S(2)}, u32[]{:S(2)}) %all-to-all-start.2) | async-done | bytes 1048608 | tf_op jit(solution)/shard_map/all_to_all | solution.py:423
  169.1 5.3 %all-to-all-start.3 = ((bf16[16,64,128]{2,1,0:T(8,128)(2,1)}), bf16[16,64,128]{2,1,0:T(8,128)(2,1)S(1)}, u32[]{:S(2)}, u32[]{:S(2)}) async-start(bf16[16,64,128]{2,1,0:T(8,128)(2,1)} %add_convert_fusion.1), calls=%async_computation.3 | async-start | bytes 524288 | tf_op jit(solution)/shard_map/all_to_all | solution.py:438
  174.4 3.3 %collective-permute-start.7 = (bf16[128,1024]{1,0:T(8,128)(2,1)S(1)}, bf16[128,1024]{1,0:T(8,128)(2,1)S(1)}, u32[]{:S(2)}, u32[]{:S(2)}) collective-permute-start(bf16[128,1024]{1,0:T(8,128)(2,1)S(1)} %fusion.4), channel_id=1, source_target_pairs={{0,256},{8,264},{16,272},{24,280},{32,288},{40,296},{48,304},{56,3... | collective-permute-start | bytes 786440 | tf_op jit(solution)/shard_map/ppermute | solution.py:436
  179.2 2.9 %collective-permute-start.11 = (bf16[128,512]{1,0:T(8,128)(2,1)S(1)}, bf16[128,512]{1,0:T(8,128)(2,1)S(1)}, u32[]{:S(2)}, u32[]{:S(2)}) collective-permute-start(bf16[128,512]{1,0:T(8,128)(2,1)S(1)} %fusion.6), channel_id=1, source_target_pairs={{0,4},{1,5},{2,6},{3,7},{4,0},{5,1},{6,2},{7,3},{8,12},{9,13},{10,... | collective-permute-start | bytes 393224 | tf_op jit(solution)/shard_map/ppermute | solution.py:427
  182.2 2.7 %collective-permute-done.7 = bf16[128,1024]{1,0:T(8,128)(2,1)S(1)} collective-permute-done((bf16[128,1024]{1,0:T(8,128)(2,1)S(1)}, bf16[128,1024]{1,0:T(8,128)(2,1)S(1)}, u32[]{:S(2)}, u32[]{:S(2)}) %collective-permute-start.7) | collective-permute-done | bytes 262176 | tf_op jit(solution)/shard_map/ppermute | solution.py:436
  188.3 4.1 %all-to-all-done.3 = bf16[16,64,128]{2,1,0:T(8,128)(2,1)S(1)} async-done(((bf16[16,64,128]{2,1,0:T(8,128)(2,1)}), bf16[16,64,128]{2,1,0:T(8,128)(2,1)S(1)}, u32[]{:S(2)}, u32[]{:S(2)}) %all-to-all-start.3) | async-done | bytes 262176 | tf_op jit(solution)/shard_map/all_to_all | solution.py:438
  (46 shorter events, 29.5 us)
Async XLA Ops:
  0.6 1.2 copy-start
  3.8 16.2 %copy-start.4 = (bf16[128,1024]{1,0:T(8,128)(2,1)S(1)}, bf16[128,1024]{1,0:T(8,128)(2,1)}, u32[]{:S(2)}) copy-start(bf16[128,1024]{1,0:T(8,128)(2,1)} %queries) | copy-start | bytes 786436
  3.8 16.2 %copy-start.5 = (bf16[128,1024]{1,0:T(8,128)(2,1)S(1)}, bf16[128,1024]{1,0:T(8,128)(2,1)}, u32[]{:S(2)}) copy-start(bf16[128,1024]{1,0:T(8,128)(2,1)} %grads) | copy-start | bytes 786436
  3.8 16.2 %copy-start.7 = (s32[8192]{0:T(1024)S(1)}, s32[8192]{0:T(1024)}, u32[]{:S(2)}) copy-start(s32[8192]{0:T(1024)} %param.12) | copy-start | bytes 98308
  3.9 16.2 %copy-start.8 = (s32[128]{0:T(128)S(1)}, s32[128]{0:T(128)}, u32[]{:S(2)}) copy-start(s32[128]{0:T(128)} %param.13) | copy-start | bytes 1540
  5.0 33.7 %all-to-all-start = ((bf16[4,128,256]{2,1,0:T(8,128)(2,1)}), bf16[4,128,256]{2,1,0:T(8,128)(2,1)S(1)}, u32[]{:S(2)}, u32[]{:S(2)}) async-start(bf16[4,128,256]{2,1,0:T(8,128)(2,1)} %shard_map.102), calls=%async_computation | async-start | bytes 524288 | tf_op jit(solution)/shard_map/all_to_all | solution.py:340
  20.8 4.6 %collective-permute-start.1 = (bf16[2048,128]{1,0:T(8,128)(2,1)S(1)}, bf16[2048,128]{1,0:T(8,128)(2,1)S(1)}, u32[]{:S(2)}, u32[]{:S(2)}) collective-permute-start(bf16[2048,128]{1,0:T(8,128)(2,1)S(1)} %get-tuple-element.29.refs_0_), channel_id=1, source_target_pairs={{0,8},{8,0},{16,24},{24,16},{32,40},{40,32},{48,56},{56,48},{64,72... | collective-permute-start | bytes 1572872 | tf_op jit(solution)/shard_map/ppermute | solution.py:359
  22.8 28.4 %collective-permute-start = (bf16[2048,128]{1,0:T(8,128)(2,1)S(1)}, bf16[2048,128]{1,0:T(8,128)(2,1)S(1)}, u32[]{:S(2)}, u32[]{:S(2)}) collective-permute-start(bf16[2048,128]{1,0:T(8,128)(2,1)S(1)} %get-tuple-element.29.refs_0_), channel_id=1, source_target_pairs={{0,256},{8,264},{16,272},{24,280},{32,288},{40,296},{48,304},{56,3... | collective-permute-start | bytes 1572872 | tf_op jit(solution)/shard_map/ppermute | solution.py:358
  38.6 12.5 %collective-permute-start.4 = (bf16[4,128,256]{2,1,0:T(8,128)(2,1)S(1)}, bf16[4,128,256]{2,1,0:T(8,128)(2,1)S(1)}, u32[]{:S(2)}, u32[]{:S(2)}) collective-permute-start(bf16[4,128,256]{2,1,0:T(8,128)(2,1)S(1)} %all-to-all-done.refs_4_), channel_id=1, source_target_pairs={{0,32},{8,232},{16,48},{24,248},{32,64},{40,8},{48,80},{56,24},{64... | collective-permute-start | bytes 786440 | tf_op jit(solution)/shard_map/ppermute | solution.py:58
  44.4 13.7 %collective-permute-start.3 = (bf16[4,128,256]{2,1,0:T(8,128)(2,1)S(1)}, bf16[4,128,256]{2,1,0:T(8,128)(2,1)S(1)}, u32[]{:S(2)}, u32[]{:S(2)}) collective-permute-start(bf16[4,128,256]{2,1,0:T(8,128)(2,1)S(1)} %all-to-all-done.refs_4_), channel_id=1, source_target_pairs={{0,496},{8,504},{16,256},{24,264},{32,272},{40,280},{48,288},{56,2... | collective-permute-start | bytes 786440 | tf_op jit(solution)/shard_map/ppermute | solution.py:58
  48.7 11.7 %collective-permute-start.2 = (bf16[4,128,256]{2,1,0:T(8,128)(2,1)S(1)}, bf16[4,128,256]{2,1,0:T(8,128)(2,1)S(1)}, u32[]{:S(2)}, u32[]{:S(2)}) collective-permute-start(bf16[4,128,256]{2,1,0:T(8,128)(2,1)S(1)} %all-to-all-done.refs_4_), channel_id=1, source_target_pairs={{0,272},{8,280},{16,288},{24,296},{32,304},{40,312},{48,320},{56,3... | collective-permute-start | bytes 786440 | tf_op jit(solution)/shard_map/ppermute | solution.py:58
  60.4 3.8 %collective-permute-start.5 = (bf16[2048,128]{1,0:T(8,128)(2,1)S(1)}, bf16[2048,128]{1,0:T(8,128)(2,1)S(1)}, u32[]{:S(2)}, u32[]{:S(2)}) collective-permute-start(bf16[2048,128]{1,0:T(8,128)(2,1)S(1)} %collective-permute-done.refs_1_), channel_id=1, source_target_pairs={{0,8},{8,0},{16,24},{24,16},{32,40},{40,32},{48,56},{56,48},{64,72... | collective-permute-start | bytes 1572872 | tf_op jit(solution)/shard_map/ppermute | solution.py:369
  76.7 65.7 %copy-start.3 = (bf16[4096,128]{1,0:T(8,128)(2,1)S(1)}, bf16[4096,128]{1,0:T(8,128)(2,1)}, u32[]{:S(2)}) copy-start(bf16[4096,128]{1,0:T(8,128)(2,1)} %weight.3) | copy-start | bytes 3145732
  88.9 53.6 %copy-start.1 = (bf16[128,4096]{1,0:T(8,128)(2,1)S(1)}, bf16[128,4096]{1,0:T(8,128)(2,1)}, u32[]{:S(2)}) copy-start(bf16[128,4096]{1,0:T(8,128)(2,1)} %inputs.3) | copy-start | bytes 3145732
  88.9 16.3 %collective-permute-start.8 = (bf16[4,128,256]{2,1,0:T(8,128)(2,1)S(1)}, bf16[4,128,256]{2,1,0:T(8,128)(2,1)S(1)}, u32[]{:S(2)}, u32[]{:S(2)}) collective-permute-start(bf16[4,128,256]{2,1,0:T(8,128)(2,1)S(1)} %get-tuple-element.41), channel_id=1, source_target_pairs={{0,496},{8,504},{16,256},{24,264},{32,272},{40,280},{48,288},{56,2... | collective-permute-start | bytes 786440 | tf_op jit(solution)/shard_map/ppermute | solution.py:58
  94.1 17.2 %collective-permute-start.9 = (bf16[4,128,256]{2,1,0:T(8,128)(2,1)S(1)}, bf16[4,128,256]{2,1,0:T(8,128)(2,1)S(1)}, u32[]{:S(2)}, u32[]{:S(2)}) collective-permute-start(bf16[4,128,256]{2,1,0:T(8,128)(2,1)S(1)} %get-tuple-element.42), channel_id=1, source_target_pairs={{0,272},{8,280},{16,288},{24,296},{32,304},{40,312},{48,320},{56,3... | collective-permute-start | bytes 786440 | tf_op jit(solution)/shard_map/ppermute | solution.py:58
  99.4 12.9 %collective-permute-start.10 = (bf16[4,128,256]{2,1,0:T(8,128)(2,1)S(1)}, bf16[4,128,256]{2,1,0:T(8,128)(2,1)S(1)}, u32[]{:S(2)}, u32[]{:S(2)}) collective-permute-start(bf16[4,128,256]{2,1,0:T(8,128)(2,1)S(1)} %get-tuple-element.43), channel_id=1, source_target_pairs={{0,224},{8,40},{16,240},{24,56},{32,0},{40,72},{48,16},{56,88},{64... | collective-permute-start | bytes 786440 | tf_op jit(solution)/shard_map/ppermute | solution.py:58
  144.7 8.6 %collective-permute-start.12 = (bf16[32,64,128]{2,1,0:T(8,128)(2,1)S(1)}, bf16[32,64,128]{2,1,0:T(8,128)(2,1)S(1)}, u32[]{:S(2)}, u32[]{:S(2)}) collective-permute-start(bf16[32,64,128]{2,1,0:T(8,128)(2,1)S(1)} %get-tuple-element.47), channel_id=1, source_target_pairs={{0,8},{8,0},{16,24},{24,16},{32,40},{40,32},{48,56},{56,48},{64,72... | collective-permute-start | bytes 1572872 | tf_op jit(solution)/shard_map/ppermute | solution.py:429
  146.8 9.8 %collective-permute-start.6 = (bf16[2,128,1024]{2,1,0:T(8,128)(2,1)S(1)}, bf16[2,128,1024]{2,1,0:T(8,128)(2,1)S(1)}, u32[]{:S(2)}, u32[]{:S(2)}) collective-permute-start(bf16[2,128,1024]{2,1,0:T(8,128)(2,1)S(1)} %get-tuple-element.39), channel_id=1, source_target_pairs={{0,8},{8,0},{16,24},{24,16},{32,40},{40,32},{48,56},{56,48},{64,72... | collective-permute-start | bytes 1572872 | tf_op jit(solution)/shard_map/ppermute | solution.py:434
  149.1 20.0 %all-to-all-start.2 = ((bf16[4,2,128,512]{3,2,1,0:T(8,128)(2,1)}), bf16[4,2,128,512]{3,2,1,0:T(8,128)(2,1)}, u32[]{:S(2)}, u32[]{:S(2)}) async-start(bf16[4,2,128,512]{3,2,1,0:T(8,128)(2,1)} %get-tuple-element.45), calls=%async_computation.2 | async-start | bytes 2097152 | tf_op jit(solution)/shard_map/all_to_all | solution.py:423
  153.6 10.2 %collective-permute-start.13 = (bf16[16,64,128]{2,1,0:T(8,128)(2,1)S(1)}, bf16[16,64,128]{2,1,0:T(8,128)(2,1)S(1)}, u32[]{:S(2)}, u32[]{:S(2)}) collective-permute-start(bf16[16,64,128]{2,1,0:T(8,128)(2,1)S(1)} %broadcast_select_fusion), channel_id=1, source_target_pairs={{0,256},{8,264},{16,272},{24,280},{32,288},{40,296},{48,304},{56,3... | collective-permute-start | bytes 786440 | tf_op jit(solution)/shard_map/ppermute | solution.py:431
  169.1 23.4 %all-to-all-start.3 = ((bf16[16,64,128]{2,1,0:T(8,128)(2,1)}), bf16[16,64,128]{2,1,0:T(8,128)(2,1)S(1)}, u32[]{:S(2)}, u32[]{:S(2)}) async-start(bf16[16,64,128]{2,1,0:T(8,128)(2,1)} %add_convert_fusion.1), calls=%async_computation.3 | async-start | bytes 524288 | tf_op jit(solution)/shard_map/all_to_all | solution.py:438
  174.4 10.4 %collective-permute-start.7 = (bf16[128,1024]{1,0:T(8,128)(2,1)S(1)}, bf16[128,1024]{1,0:T(8,128)(2,1)S(1)}, u32[]{:S(2)}, u32[]{:S(2)}) collective-permute-start(bf16[128,1024]{1,0:T(8,128)(2,1)S(1)} %fusion.4), channel_id=1, source_target_pairs={{0,256},{8,264},{16,272},{24,280},{32,288},{40,296},{48,304},{56,3... | collective-permute-start | bytes 786440 | tf_op jit(solution)/shard_map/ppermute | solution.py:436
  179.2 8.4 %collective-permute-start.11 = (bf16[128,512]{1,0:T(8,128)(2,1)S(1)}, bf16[128,512]{1,0:T(8,128)(2,1)S(1)}, u32[]{:S(2)}, u32[]{:S(2)}) collective-permute-start(bf16[128,512]{1,0:T(8,128)(2,1)S(1)} %fusion.6), channel_id=1, source_target_pairs={{0,4},{1,5},{2,6},{3,7},{4,0},{5,1},{6,2},{7,3},{8,12},{9,13},{10,... | collective-permute-start | bytes 393224 | tf_op jit(solution)/shard_map/ppermute | solution.py:427
  (2 other events, 2.0 us)
